TPU v7x, 32 devices: a whole 2x2x4 slice. The times are simulated.
32 devices in a mesh: dp: 8 (over z, y), tensor: 4 (over x, core).
Axes of the slice: x: 2, y: 2, z: 4, core: 2. Of those that a mesh axis runs over, the one named last changes fastest.
Arguments:
- tokens: bfloat16 [16384, 1024], P(('dp', 'tensor')), may hold values from -6 to 6
- lengths: int32 [8, 2], P('dp'), may hold values from 64 to 1984, as said below
- attn_gain: bfloat16 [1024], replicated, may hold values from 0.5 to 1.5
- qkv_weight: bfloat16 [1024, 3, 1024], P(None, None, 'tensor'), may hold values from -0.1875 to 0.1875
- beta_weight: bfloat16 [1024, 8], P(None, 'tensor'), may hold values from -0.1875 to 0.1875
- conv_weight: bfloat16 [4, 3, 1024], P(None, None, 'tensor'), may hold values from -3 to 3
- head_gain: bfloat16 [128], replicated, may hold values from 0.5 to 1.5
- out_weight: bfloat16 [1024, 1024], P('tensor'), may hold values from -0.1875 to 0.1875
- mlp_gain: bfloat16 [1024], replicated, may hold values from 0.5 to 1.5
- gate_up_weight: bfloat16 [1024, 2, 2816], P(None, None, 'tensor'), may hold values from -0.1875 to 0.1875
- down_weight: bfloat16 [2816, 1024], P('tensor'), may hold values from -0.109375 to 0.109375
- cotangent: bfloat16 [16384, 1024], P(('dp', 'tensor')), may hold values from -6 to 6
Outputs:
- output: bfloat16 [16384, 1024], P(('dp', 'tensor'))
- input_grad: float32 [16384, 1024], P(('dp', 'tensor'))
- attn_gain_grad: float32 [1024], replicated
- qkv_grad: float32 [1024, 3, 1024], P(None, None, 'tensor')
- beta_grad: float32 [1024, 8], P(None, 'tensor')
- conv_grad: float32 [4, 3, 1024], P(None, None, 'tensor')
- head_gain_grad: float32 [128], replicated
- out_grad: float32 [1024, 1024], P('tensor')
- mlp_gain_grad: float32 [1024], replicated
- gate_up_grad: float32 [1024, 2, 2816], P(None, None, 'tensor')
- down_grad: float32 [2816, 1024], P('tensor')
Inputs may be any that keep to these rules, and one draw needn't show every extreme that they name: Each row holds the lengths of the two sequences of one group, in order; both are multiples of 64, they sum to 2048, and the shorter is at most 448.
All inputs are finite; a program needn't handle non-finite values.
Results may differ from a plain program's by a relative error of at most 0.017.
Values may be sent and summed in bfloat16 or wider, within the bound.
A program may use at most 256 MiB of HBM per device.

v0:
```python
import jax
import jax.numpy as jnp
from jax import lax
from jax.sharding import PartitionSpec as P

SPAN = 64


precise = lax.Precision.HIGHEST


def rms_norm(values, scales):
    inverse = lax.rsqrt(jnp.mean(values * values, axis=-1, keepdims=True) + 1e-05)
    return values * inverse * scales


def doc_layout(first_len, group_rows, block_len):
    row_index = jnp.arange(group_rows, dtype=jnp.int32)
    doc_start = jnp.where(row_index >= first_len, first_len, 0)
    position = row_index - doc_start
    block_start = jnp.arange(group_rows // block_len, dtype=jnp.int32) * block_len
    reset_flags = jnp.where((block_start == 0) | (block_start == first_len), 1.0, 0.0).astype(
        jnp.float32
    )
    return (position, reset_flags)


def short_conv(projected, kernel, position):
    total_rows = projected.shape[0]
    summed = jnp.zeros_like(projected)
    for offset in range(kernel.shape[0]):
        shifted = jnp.pad(projected, ((offset, 0), (0, 0)))[:total_rows]
        usable = (position >= offset)[:, None]
        summed = summed + jnp.where(usable, shifted * kernel[offset], 0.0)
    return jax.nn.silu(summed)


def delta_rule(query_rows, key_rows, value_rows, beta_rows, reset_flags, block_len):
    total_rows, head_count, head_size = query_rows.shape
    block_count = total_rows // block_len

    def blocked(values):
        return jnp.swapaxes(values.reshape((block_count, block_len) + values.shape[1:]), 1, 2)

    query_all = blocked(query_rows)
    key_all = blocked(key_rows)
    value_all = blocked(value_rows)
    beta_all = blocked(beta_rows)
    index = jnp.arange(block_len)
    strict = index[:, None] > index[None, :]
    causal = index[:, None] >= index[None, :]
    identity = jnp.eye(block_len, dtype=jnp.float32)
    key_gram = jnp.einsum("nhid,nhjd->nhij", key_all, key_all, precision=precise)
    system = identity + jnp.where(strict, beta_all[..., None] * key_gram, 0.0)
    right_hand = beta_all[..., None] * jnp.concatenate([key_all, value_all], axis=-1)
    solved = jax.scipy.linalg.solve_triangular(system, right_hand, lower=True, unit_diagonal=True)
    solved_keys = solved[..., :head_size]
    solved_values = solved[..., head_size:]
    scores_all = jnp.where(
        causal, jnp.einsum("nhid,nhjd->nhij", query_all, key_all, precision=precise), 0.0
    )

    def advance(memory, inputs):
        query_block, key_block, keys_solved, values_solved, scores, reset_flag = inputs
        memory = memory * (1.0 - reset_flag)
        residual = values_solved - jnp.einsum(
            "hcd,hde->hce", keys_solved, memory, precision=precise
        )
        outputs = jnp.einsum("hcd,hde->hce", query_block, memory, precision=precise)
        outputs = outputs + jnp.einsum("hij,hje->hie", scores, residual, precision=precise)
        memory = memory + jnp.einsum("hcd,hce->hde", key_block, residual, precision=precise)
        return (memory, outputs)

    initial = jnp.zeros((head_count, head_size, head_size), jnp.float32)
    inputs = (query_all, key_all, solved_keys, solved_values, scores_all, reset_flags)
    _, outputs = lax.scan(jax.checkpoint(advance), initial, inputs)
    return jnp.swapaxes(outputs, 1, 2).reshape(total_rows, head_count, head_size)


def mixer(projected, beta_pre, kernel, head_scale, position, reset_flags):
    conved = short_conv(projected, kernel, position)
    total_rows = projected.shape[0]
    channels = projected.shape[1] // 3
    head_size = head_scale.shape[0]
    head_count = channels // head_size
    shaped = conved.reshape(total_rows, 3, head_count, head_size)
    query_rows = shaped[:, 0]
    key_rows = shaped[:, 1]
    value_rows = shaped[:, 2]
    query_rows = query_rows * lax.rsqrt(
        jnp.sum(query_rows * query_rows, axis=-1, keepdims=True) + 1e-06
    )
    key_rows = key_rows * lax.rsqrt(jnp.sum(key_rows * key_rows, axis=-1, keepdims=True) + 1e-06)
    mixed = delta_rule(
        query_rows, key_rows, value_rows, jax.nn.sigmoid(beta_pre), reset_flags, SPAN
    )
    return rms_norm(mixed, head_scale).reshape(total_rows, channels)


def on_device(
    tokens,
    lengths,
    attn_gain,
    qkv_weight,
    beta_weight,
    conv_weight,
    head_gain,
    out_weight,
    mlp_gain,
    gate_up_weight,
    down_weight,
    cotangent,
):
    local_rows, model_width = tokens.shape
    group_rows = local_rows * lax.axis_size("tensor")
    position, reset_flags = doc_layout(lengths[0, 0], group_rows, SPAN)
    local_in = tokens.astype(jnp.float32)
    first_scale = attn_gain.astype(jnp.float32)
    second_scale = mlp_gain.astype(jnp.float32)
    head_scale = head_gain.astype(jnp.float32)
    attn_in = rms_norm(local_in, first_scale).astype(jnp.bfloat16)
    attn_all = lax.all_gather(attn_in, "tensor", axis=0, tiled=True)
    qkv_matrix = qkv_weight.reshape(model_width, -1)
    projected = jnp.dot(attn_all, qkv_matrix, preferred_element_type=jnp.float32)
    beta_pre = jnp.dot(attn_all, beta_weight, preferred_element_type=jnp.float32)
    kernel = conv_weight.reshape(conv_weight.shape[0], -1).astype(jnp.float32)

    def local_mixer(proj_in, beta_in, kernel_in, scale_in):
        return mixer(proj_in, beta_in, kernel_in, scale_in, position, reset_flags)

    headed, mixer_back = jax.vjp(local_mixer, projected, beta_pre, kernel, head_scale)
    headed_low = headed.astype(jnp.bfloat16)
    attn_out = lax.psum_scatter(
        jnp.dot(headed_low, out_weight, preferred_element_type=jnp.float32),
        "tensor",
        scatter_dimension=0,
        tiled=True,
    )
    hidden_res = local_in + attn_out
    mlp_in = rms_norm(hidden_res, second_scale).astype(jnp.bfloat16)
    mlp_all = lax.all_gather(mlp_in, "tensor", axis=0, tiled=True)
    gate_up_matrix = gate_up_weight.reshape(model_width, -1)
    gate_up = jnp.dot(mlp_all, gate_up_matrix, preferred_element_type=jnp.float32)
    hidden_units = gate_up.shape[1] // 2
    gate_pre = gate_up[:, :hidden_units]
    up_pre = gate_up[:, hidden_units:]
    sigmoid_gate = jax.nn.sigmoid(gate_pre)
    silu_gate = gate_pre * sigmoid_gate
    activated = (silu_gate * up_pre).astype(jnp.bfloat16)
    mlp_out = lax.psum_scatter(
        jnp.dot(activated, down_weight, preferred_element_type=jnp.float32).astype(jnp.bfloat16),
        "tensor",
        scatter_dimension=0,
        tiled=True,
    ).astype(jnp.float32)
    output = (hidden_res + mlp_out).astype(jnp.bfloat16)
    cot_piece = lax.all_gather(cotangent, "tensor", axis=0, tiled=True)
    down_sum = jnp.einsum("tf,td->fd", activated, cot_piece, preferred_element_type=jnp.float32)
    d_rows = jnp.einsum("td,fd->tf", cot_piece, down_weight, preferred_element_type=jnp.float32)
    d_activated = d_rows
    d_activated, down_grad = (d_activated, down_sum)
    d_gate = (d_activated * up_pre * sigmoid_gate * (1.0 + gate_pre * (1.0 - sigmoid_gate))).astype(
        jnp.bfloat16
    )
    d_up = (d_activated * silu_gate).astype(jnp.bfloat16)
    d_gate_up = jnp.concatenate([d_gate, d_up], axis=1)
    gate_up_grad = jnp.einsum(
        "td,tf->df", mlp_all, d_gate_up, preferred_element_type=jnp.float32
    ).reshape(gate_up_weight.shape)
    d_mlp_in = lax.psum_scatter(
        jnp.einsum(
            "tf,df->td", d_gate_up, gate_up_matrix, preferred_element_type=jnp.float32
        ).astype(jnp.bfloat16),
        "tensor",
        scatter_dimension=0,
        tiled=True,
    ).astype(jnp.float32)
    second_back = jax.vjp(rms_norm, hidden_res, second_scale)[1]
    d_from_mlp, mlp_gain_part = second_back(d_mlp_in)
    d_hidden = cotangent.astype(jnp.float32) + d_from_mlp
    d_attn = d_hidden.astype(jnp.bfloat16)
    grad_piece = lax.all_gather(d_attn, "tensor", axis=0, tiled=True)
    out_sum = jnp.einsum("tc,td->cd", headed_low, grad_piece, preferred_element_type=jnp.float32)
    d_rows = jnp.einsum("td,cd->tc", grad_piece, out_weight, preferred_element_type=jnp.float32)
    d_headed = d_rows
    d_headed, out_grad = (d_headed, out_sum)
    d_projected, d_beta_pre, conv_part, head_gain_part = mixer_back(d_headed)
    d_proj = d_projected.astype(jnp.bfloat16)
    d_beta = d_beta_pre.astype(jnp.bfloat16)
    qkv_grad = jnp.einsum(
        "td,tc->dc", attn_all, d_proj, preferred_element_type=jnp.float32
    ).reshape(qkv_weight.shape)
    beta_grad = jnp.einsum("td,th->dh", attn_all, d_beta, preferred_element_type=jnp.float32)
    conv_grad = conv_part.reshape(conv_weight.shape)
    summed = jnp.einsum("tc,dc->td", d_proj, qkv_matrix, preferred_element_type=jnp.float32)
    d_attn_in = lax.psum_scatter(
        (
            summed
            + jnp.einsum("th,dh->td", d_beta, beta_weight, preferred_element_type=jnp.float32)
        ).astype(jnp.bfloat16),
        "tensor",
        scatter_dimension=0,
        tiled=True,
    ).astype(jnp.float32)
    first_back = jax.vjp(rms_norm, local_in, first_scale)[1]
    d_from_attn, attn_gain_part = first_back(d_attn_in)
    input_grad = d_hidden + d_from_attn
    attn_gain_grad, head_gain_grad, mlp_gain_grad = lax.psum(
        (attn_gain_part, head_gain_part, mlp_gain_part), ("dp", "tensor")
    )
    qkv_grad, beta_grad, conv_grad, out_grad, gate_up_grad, down_grad = lax.psum(
        (qkv_grad, beta_grad, conv_grad, out_grad, gate_up_grad, down_grad), "dp"
    )
    return (
        output,
        input_grad,
        attn_gain_grad,
        qkv_grad,
        beta_grad,
        conv_grad,
        head_gain_grad,
        out_grad,
        mlp_gain_grad,
        gate_up_grad,
        down_grad,
    )


def solution(mesh):
    return jax.shard_map(
        on_device,
        mesh=mesh,
        in_specs=(
            P(("dp", "tensor"), None),
            P("dp", None),
            P(),
            P(None, None, "tensor"),
            P(None, "tensor"),
            P(None, None, "tensor"),
            P(),
            P("tensor", None),
            P(),
            P(None, None, "tensor"),
            P("tensor", None),
            P(("dp", "tensor"), None),
        ),
        out_specs=(
            P(("dp", "tensor"), None),
            P(("dp", "tensor"), None),
            P(),
            P(None, None, "tensor"),
            P(None, "tensor"),
            P(None, None, "tensor"),
            P(),
            P("tensor", None),
            P(),
            P(None, None, "tensor"),
            P("tensor", None),
        ),
        check_vma=False,
    )
```

profile of v0, /device:TPU:0, one launch (start us, length us, event | category | flops | bytes accessed | tf_op | source)
XLA Modules:
  0.0 1844.7 jit_solution(16004376885939951049)
XLA Ops:
  17.1 33.6 %all-gather.5.cloned.1.call-done = bf16[2048,1024]{1,0:T(8,128)(2,1)} async-done(((bf16[512,1024]{1,0:T(8,128)(2,1)}), bf16[2048,1024]{1,0:T(8,128)(2,1)}) %all-gather.5.cloned.1.call-update) | async-done | bytes 4194320 | tf_op jit(solution)/shard_map/all_gather | solution.py:122
  50.7 5.7 fusion.105
  56.5 9.1 fusion.42
  65.6 8.3 reshape.292
  73.9 4.1 fusion.99
  88.9 4.8 fusion.95
  93.7 4.7 fusion.106
  103.7 3.8 copy.183
  107.5 4.1 broadcast_select_fusion.1
  111.6 4.5 copy.185
  116.1 5.6 copy.176
  121.7 7.6 add_bitcast_fusion
  129.3 134.0 %custom-call.10 = f32[32,2,1,64,64]{0,3,4,2,1:T(8,128)} custom-call(f32[32,2,1,64,64]{0,4,3,2,1:T(8,128)} %add_bitcast_fusion), custom_call_target="InvertDiagBlocksLowerTriangular" | custom-call | tf_op jit(solution)/shard_map/jvp(jit(_solve_triangular))/vmap(vmap())/triangular_solve | solution.py:56
  263.3 5.3 copy.180
  268.6 7.4 fusion.44
  276.0 3.0 fusion.100
  281.0 225.9 %while.40 = (s32[]{:T(128)}, f32[2,128,128]{2,1,0:T(8,128)S(1)}, f32[32,2,64,128]{3,2,1,0:T(8,128)}, f32[32,2,128,128]{3,2,1,0:T(8,128)}, f32[32]{0:T(128)S(1)},...) while((s32[]{:T(128)}, f32[2,128,128]{2,1,0:T(8,128)S(1)}, ...), condition=%wide.region_4.5_spmd.clone, body=%wide.region_3.4_spmd.clone.sunk | while | flops 88375296 | bytes 1511605 | solution.py:76
  511.1 3.4 copy.186
  514.5 4.7 mul.515
  521.5 4.6 fusion.107
  526.8 71.2 %reduce-scatter.5.cloned.1.call-done = f32[512,1024]{1,0:T(8,128)} async-done(((f32[2048,1024]{1,0:T(8,128)}), f32[512,1024]{1,0:T(8,128)}) %reduce-scatter.5.cloned.1.call-update) | async-done | bytes 2097168 | tf_op jit(solution)/shard_map/reduce_scatter | solution.py:133
  603.4 34.0 %all-gather.7.cloned.1.call-done = bf16[2048,1024]{1,0:T(8,128)(2,1)} async-done(((bf16[512,1024]{1,0:T(8,128)(2,1)}), bf16[2048,1024]{1,0:T(8,128)(2,1)}) %all-gather.7.cloned.1.call-update) | async-done | bytes 4194320 | tf_op jit(solution)/shard_map/all_gather | solution.py:141
  637.4 11.4 fusion.108
  648.8 24.6 %all-gather.9.cloned.1.call-done = bf16[2048,1024]{1,0:T(8,128)(2,1)} async-done(((bf16[512,1024]{1,0:T(8,128)(2,1)}), bf16[2048,1024]{1,0:T(8,128)(2,1)}) %all-gather.9.cloned.1.call-update) | async-done | bytes 4194320 | tf_op jit(solution)/shard_map/all_gather | solution.py:157
  673.4 11.1 multiply_convert_fusion.1
  687.0 8.3 convolution_convert_fusion
  695.4 44.6 %reduce-scatter.9.cloned.1.call-done = bf16[512,1024]{1,0:T(8,128)(2,1)} async-done(((bf16[2048,1024]{1,0:T(8,128)(2,1)}), bf16[512,1024]{1,0:T(8,128)(2,1)}) %reduce-scatter.9.cloned.1.call-update) | async-done | bytes 1048592 | tf_op jit(solution)/shard_map/reduce_scatter | solution.py:170
  745.6 5.5 copy.195
  751.1 4.5 copy.196
  755.6 24.5 %all-gather.11.cloned.1.call-done = bf16[2048,1024]{1,0:T(8,128)(2,1)} async-done(((bf16[512,1024]{1,0:T(8,128)(2,1)}), bf16[2048,1024]{1,0:T(8,128)(2,1)}) %all-gather.11.cloned.1.call-update) | async-done | bytes 4194320 | tf_op jit(solution)/shard_map/all_gather | solution.py:182
  780.1 6.0 multiply_reduce_fusion.6
  786.2 3.4 reshape.296
  802.2 369.8 %while.41 = (s32[]{:T(128)}, f32[2,128,128]{2,1,0:T(8,128)S(1)}, f32[32,2,64,128]{3,2,1,0:T(8,128)}, f32[32,2,64,128]{3,2,1,0:T(8,128)}, f32[32,2,64,128]{3,2,1,...) while((s32[]{:T(128)}, f32[2,128,128]{2,1,0:T(8,128)S(1)}, ...), condition=%wide.region_13.14_spmd.clone, body=%wide.region_12.13_spmd.clone.sunk | while | flops 201621504 | bytes 3899675 | solution.py:76
  1172.0 8.2 fusion.47
  1180.2 3.4 fusion.109
  1183.6 4.6 multiply_reduce_fusion.5
  1191.7 3.9 copy.198
  1195.6 4.1 broadcast_select_fusion.2
  1199.7 4.2 copy.208
  1203.9 7.1 fusion.93
  1218.5 5.6 copy.203
  1224.1 6.5 multiply_reduce_fusion.4
  1230.8 4.3 copy.205
  1235.1 5.2 fusion.110
  1240.3 4.4 fusion.68
  1249.8 25.4 %copy.211 = f32[2048,3,2,128]{3,2,1,0:T(2,128)} copy(f32[2048,3,2,128]{3,0,2,1:T(8,128)S(1)} %pad_add_fusion) | data formatting | bytes 12582912 | tf_op jit(solution)/shard_map/transpose(jvp())/add_any | solution.py:87
  1275.2 9.4 reshape.302
  1284.7 15.8 multiply_reduce_fusion.3
  1300.5 3.9 select_multiply_fusion.3
  1304.5 5.9 fusion.39
  1310.4 5.4 fusion.111
  1315.8 3.3 add_convert_fusion
  1320.5 6.9 convolution_convert_fusion.1
  1327.7 8.5 fusion.114
  1336.2 9.5 fusion.46
  1345.7 5.3 fusion.112
  1351.0 3.7 copy.215
  1354.7 4.4 fusion.113
  1362.1 38.3 %all-reduce.16 = (f32[1024,2]{0,1:T(2,128)}, f32[4,3,256]{2,0,1:T(4,128)}) all-reduce(f32[1024,2]{0,1:T(2,128)S(1)} %fusion.101, f32[4,3,256]{2,0,1:T(4,128)S(1)} %bitcast.292), channel_id=1, replica_groups=mesh['dp'=8,'tensor'=4] {'dp'}, use_global_device_ids=true, to_apply=%region_23.24 | all-reduce | flops 5120 | bytes 40960 | tf_op jit(solution)/shard_map/psum | solution.py:211
  1402.9 39.1 %all-reduce.15 = (f32[1024]{0:T(1024)}, f32[128]{0:T(128)}, f32[1024]{0:T(1024)}) all-reduce(f32[1024]{0:T(1024)S(1)} %get-tuple-element.598, f32[128]{0:T(128)S(1)} %bitcast_reduce_fusion, f32[1024]{0:T(1024)S(1)} %copy-done.93), channel_id=1, replica_groups=mesh['dp'=8,'tensor'=4] {'dp','tensor'}, use_global_device_ids=true, to_apply=%region_21.22 | all-reduce | flops 2176 | bytes 17408 | tf_op jit(solution)/shard_map/psum | solution.py:208
  1442.1 4.3 fusion.63
  1446.5 379.7 %all-reduce.20.cloned.1.call-done = (f32[1024,3,256]{2,0,1:T(8,128)}, f32[256,1024]{1,0:T(8,128)}, f32[1024,2,704]{0,2,1:T(8,128)}, f32[704,1024]{1,0:T(8,128)}) async-done(((f32[1024,3,256]{2,0,1:T(8,128)}, f32[256,1024]{1,0:T(8,128)}, f32[1024,2,704]{0,2,1:T(8,128)}, f32[704,1024]{1,0:T(8,128)}), (f32[1024,3,256]{2,0,1:T(8,128)}, f32[256,1024]{1,0:T(8,128)}, f32[1024,2,704]{0,2,1:T(8,128)}, ...) | async-done | bytes 12845072 | tf_op jit(solution)/shard_map/psum | solution.py:211
  1826.2 3.9 copy.347
  1832.5 2.9 copy.349
  (1038 shorter events, 639.6 us)
Async XLA Ops:
  7.2 630.2 %copy-start = (bf16[1024,2,704]{0,2,1:T(8,128)(2,1)S(1)}, bf16[1024,2,704]{0,2,1:T(8,128)(2,1)}, u32[]{:S(2)}) copy-start(bf16[1024,2,704]{0,2,1:T(8,128)(2,1)} %param.25) | copy-start | bytes 8650756
  7.2 6.2 copy-start.105
  7.2 6.2 copy-start.96
  7.2 43.4 %all-gather.5.cloned.1.call-start = ((), (), s32[]{:S(2)}) async-start(), calls=%async_computation.4 | async-start | bytes 5242880 | tf_op jit(solution)/shard_map/all_gather | solution.py:122
  13.3 584.7 %reduce-scatter.5.cloned.1.call-start = ((), (), s32[]{:S(2)}) async-start(), calls=%async_computation.5 | async-start | bytes 10485760 | tf_op jit(solution)/shard_map/reduce_scatter | solution.py:133
  13.4 43.0 %copy-start.97 = (f32[128]{0:T(128)}, f32[128]{0:T(128)S(1)}, u32[]{:S(2)}) copy-start(f32[128]{0:T(128)S(1)} %convert_element_type.85) | copy-start | bytes 1540
  13.5 42.9 %copy-start.77 = (f32[768]{0:T(1024)}, f32[768]{0:T(1024)S(1)}, u32[]{:S(2)}) copy-start(f32[768]{0:T(1024)S(1)} %mul.491) | copy-start | bytes 9220
  13.5 42.9 %copy-start.71 = (f32[768]{0:T(1024)}, f32[768]{0:T(1024)S(1)}, u32[]{:S(2)}) copy-start(f32[768]{0:T(1024)S(1)} %mul.500) | copy-start | bytes 9220
  13.6 42.9 %copy-start.73 = (f32[768]{0:T(1024)}, f32[768]{0:T(1024)S(1)}, u32[]{:S(2)}) copy-start(f32[768]{0:T(1024)S(1)} %mul.497) | copy-start | bytes 9220
  13.6 42.9 %copy-start.75 = (f32[768]{0:T(1024)}, f32[768]{0:T(1024)S(1)}, u32[]{:S(2)}) copy-start(f32[768]{0:T(1024)S(1)} %mul.494) | copy-start | bytes 9220
  16.3 40.2 %copy-start.81 = (pred[2048]{0:T(1024)(128)(4,1)}, pred[2048]{0:T(1024)(128)(4,1)S(1)}, u32[]{:S(2)}) copy-start(pred[2048]{0:T(1024)(128)(4,1)S(1)} %get-tuple-element.693) | copy-start | bytes 6148
  16.3 40.2 %copy-start.83 = (pred[2048]{0:T(1024)(128)(4,1)}, pred[2048]{0:T(1024)(128)(4,1)S(1)}, u32[]{:S(2)}) copy-start(pred[2048]{0:T(1024)(128)(4,1)S(1)} %get-tuple-element.694) | copy-start | bytes 6148
  16.4 40.1 %copy-start.79 = (pred[2048]{0:T(1024)(128)(4,1)}, pred[2048]{0:T(1024)(128)(4,1)S(1)}, u32[]{:S(2)}) copy-start(pred[2048]{0:T(1024)(128)(4,1)S(1)} %get-tuple-element.696) | copy-start | bytes 6148
  16.4 40.1 %copy-start.85 = (pred[2048]{0:T(1024)(128)(4,1)}, pred[2048]{0:T(1024)(128)(4,1)S(1)}, u32[]{:S(2)}) copy-start(pred[2048]{0:T(1024)(128)(4,1)S(1)} %get-tuple-element.695) | copy-start | bytes 6148
  16.4 91.1 %copy-start.61 = (pred[64,64]{1,0:T(8,128)(4,1)}, pred[64,64]{1,0:T(8,128)(4,1)S(1)}, u32[]{:S(2)}) copy-start(pred[64,64]{1,0:T(8,128)(4,1)S(1)} %iota_compare_fusion) | copy-start | bytes 12292
  17.1 104.6 %copy-start.63 = (pred[64,64]{1,0:T(8,128)(4,1)}, pred[64,64]{1,0:T(8,128)(4,1)S(1)}, u32[]{:S(2)}) copy-start(pred[64,64]{1,0:T(8,128)(4,1)S(1)} %get-tuple-element.697) | copy-start | bytes 12292
  17.1 104.6 %copy-start.65 = (pred[64,64]{1,0:T(8,128)(4,1)}, pred[64,64]{1,0:T(8,128)(4,1)S(1)}, u32[]{:S(2)}) copy-start(pred[64,64]{1,0:T(8,128)(4,1)S(1)} %get-tuple-element.698) | copy-start | bytes 12292
  56.4 9.2 copy-start.17
  100.4 21.3 %copy-start.43 = (f32[32,64,2]{0,1,2:T(8,128)}, f32[32,64,2]{0,1,2:T(8,128)S(1)}, u32[]{:S(2)}) copy-start(f32[32,64,2]{0,1,2:T(8,128)S(1)} %copy.175) | copy-start | bytes 49156
  100.5 168.1 %copy-start.47 = (f32[32,2,64]{2,1,0:T(2,128)}, f32[32,2,64]{2,1,0:T(2,128)S(1)}, u32[]{:S(2)}) copy-start(f32[32,2,64]{2,1,0:T(2,128)S(1)} %copy.177) | copy-start | bytes 49156
  506.9 7.6 copy-start.106
  526.1 111.3 %all-gather.7.cloned.1.call-start = ((), (), s32[]{:S(2)}) async-start(), calls=%async_computation.6 | async-start | bytes 5242880 | tf_op jit(solution)/shard_map/all_gather | solution.py:141
  526.8 215.8 %copy-start.59 = (f32[1024]{0:T(1024)}, f32[1024]{0:T(1024)S(1)}, u32[]{:S(2)}) copy-start(f32[1024]{0:T(1024)S(1)} %convert_element_type.87) | copy-start | bytes 12292
  600.2 142.4 %copy-start.69 = (f32[512]{0:T(512)}, f32[512]{0:T(512)S(1)}, u32[]{:S(2)}) copy-start(f32[512]{0:T(512)S(1)} %fusion.87) | copy-start | bytes 6148
  602.8 70.6 %all-gather.9.cloned.1.call-start = ((), (), s32[]{:S(2)}) async-start(), calls=%async_computation.8 | async-start | bytes 5242880 | tf_op jit(solution)/shard_map/all_gather | solution.py:157
  603.3 136.7 %reduce-scatter.9.cloned.1.call-start = ((), (), s32[]{:S(2)}) async-start(), calls=%async_computation.9 | async-start | bytes 5242880 | tf_op jit(solution)/shard_map/reduce_scatter | solution.py:170
  695.3 44.7 %copy-start.5 = (f32[512,1024]{1,0:T(8,128)S(1)}, f32[512,1024]{1,0:T(8,128)}, u32[]{:S(2)}) copy-start(f32[512,1024]{1,0:T(8,128)} %copy-done.4) | copy-start | bytes 6291460
  695.3 84.8 %all-gather.11.cloned.1.call-start = ((), (), s32[]{:S(2)}) async-start(), calls=%async_computation.10 | async-start | bytes 5242880 | tf_op jit(solution)/shard_map/all_gather | solution.py:182
  745.5 654.9 %reduce-scatter.11.cloned.1.call-start = ((), (), s32[]{:S(2)}) async-start(), calls=%async_computation.11 | async-start | bytes 5242880 | tf_op jit(solution)/shard_map/reduce_scatter | solution.py:196
  751.1 29.1 %copy-start.15 = (f32[32,64,2,128]{3,2,1,0:T(2,128)S(1)}, f32[32,64,2,128]{3,2,1,0:T(2,128)}, u32[]{:S(2)}) copy-start(f32[32,64,2,128]{3,2,1,0:T(2,128)} %copy-done.14) | copy-start | bytes 6291460
  1172.0 8.2 copy-start.20
  1172.0 11.6 copy-start.30
  1172.0 11.6 copy-start.48
  1203.9 7.2 copy-start.26
  1203.9 7.2 copy-start.34
  1218.5 5.6 copy-start.44
  1218.5 5.6 copy-start.64
  1218.5 5.6 copy-start.66
  1275.2 9.4 copy-start.80
  1275.2 9.4 copy-start.82
  1275.2 9.4 copy-start.84
  1275.2 9.4 copy-start.86
  1284.7 15.8 copy-start.72
  1284.7 15.8 copy-start.74
  1284.7 15.8 copy-start.76
  1304.5 5.9 copy-start.42
  1319.1 123.0 %reduce-scatter.7.cloned.1.call-start = ((), (), s32[]{:S(2)}) async-start(), calls=%async_computation.7 | async-start | bytes 5242880 | tf_op jit(solution)/shard_map/reduce_scatter | solution.py:150
  1327.4 498.8 %all-reduce.20.cloned.1.call-start = ((), (), s32[]{:S(2)}) async-start(), calls=%async_computation.12 | async-start | bytes 25690112 | tf_op jit(solution)/shard_map/psum | solution.py:211
  1327.6 8.6 copy-start.103
  1327.6 8.5 copy-start.109
  1327.7 8.5 copy-start.111
  1336.2 9.5 copy-start.19
  1336.2 9.5 copy-start.39
  1359.2 41.2 %copy-start.101 = (f32[256]{0:T(256)S(1)}, f32[256]{0:T(256)}, u32[]{:S(2)}) copy-start(f32[256]{0:T(256)} %get-tuple-element.691) | copy-start | bytes 3076
  1359.2 41.2 %copy-start.68 = (f32[1024]{0:T(1024)S(1)}, f32[1024]{0:T(1024)}, u32[]{:S(2)}) copy-start(f32[1024]{0:T(1024)} %copy-done.67) | copy-start | bytes 12292
  1359.2 41.2 %copy-start.88 = (f32[512]{0:T(512)S(1)}, f32[512]{0:T(512)}, u32[]{:S(2)}) copy-start(f32[512]{0:T(512)} %copy-done.87) | copy-start | bytes 6148
  1362.1 40.8 %copy-start.93 = (f32[1024]{0:T(1024)S(1)}, f32[1024]{0:T(1024)}, u32[]{:S(2)}) copy-start(f32[1024]{0:T(1024)} %get-tuple-element.596) | copy-start | bytes 12292
  1362.1 80.0 %copy-start.92 = (f32[512]{0:T(512)S(1)}, f32[512]{0:T(512)}, u32[]{:S(2)}) copy-start(f32[512]{0:T(512)} %copy-done.91) | copy-start | bytes 6148
  1362.1 80.0 %copy-start.6 = (f32[512,1024]{1,0:T(8,128)S(1)}, f32[512,1024]{1,0:T(8,128)}, u32[]{:S(2)}) copy-start(f32[512,1024]{1,0:T(8,128)} %copy-done.4) | copy-start | bytes 6291460
  1362.1 80.0 %copy-start.60 = (f32[1024]{0:T(1024)S(1)}, f32[1024]{0:T(1024)}, u32[]{:S(2)}) copy-start(f32[1024]{0:T(1024)} %copy-done.59) | copy-start | bytes 12292
  1362.1 80.0 %copy-start.70 = (f32[512]{0:T(512)S(1)}, f32[512]{0:T(512)}, u32[]{:S(2)}) copy-start(f32[512]{0:T(512)} %copy-done.69) | copy-start | bytes 6148
  1362.1 80.0 %copy-start.90 = (f32[512]{0:T(512)S(1)}, f32[512]{0:T(512)}, u32[]{:S(2)}) copy-start(f32[512]{0:T(512)} %copy-done.89) | copy-start | bytes 6148
  1826.2 6.2 copy-start.35
  1832.5 5.5 copy-start.1
  (57 other events, 158.6 us)
Sparse Core Ops, SparseCore 0:
  13.5 37.1 all-gather.4
  526.2 71.7 reduce-scatter.4
  602.9 34.4 all-gather.6
  638.9 34.4 all-gather.8
  695.5 44.5 reduce-scatter.8
  745.6 34.4 all-gather.10
  1319.3 44.5 reduce-scatter.10
  1366.5 45.0 reduce-scatter.6
  1417.5 408.6 all-reduce.19
where the time goes:
time: 1860 us; the launch traced here: 1840 us
  waiting for transfers between devices  613 us (33%)
  matrix products  499 us (27%)
  local copies, waits for them, and re-layouts  343 us (18%)
  other arithmetic  251 us (13%)
  blocking collectives  77.4 us (4%)
  loops' own time  44.8 us (2%)
    psum x1, waiting for transfers between devices, on_device(): lax.psum((qkv_grad, beta_grad, conv_grad, out_grad, gate_up_grad, down_gr...  380 us
    another operation x3, other arithmetic, delta_rule(): jax.scipy.linalg.solve_triangular(system, right_hand, lower=True, unit_di...  142 us
    squeeze x160, local copies, waits for them, and re-layouts, delta_rule(): _, outputs = lax.scan(jax.checkpoint(advance), initial, inputs)  139 us
    dot_general x96, matrix products, advance(): jnp.einsum('hij,hje->hie', scores, residual, precision=precise)  107 us
    dot_general x128, matrix products, advance(): jnp.einsum('hcd,hde->hce', keys_solved, memory, precision=precise)  87.4 us
    dot_general x96, matrix products, advance(): outputs = jnp.einsum('hcd,hde->hce', query_block, memory, precision=precise)  79.3 us
    dot_general x96, matrix products, advance(): jnp.einsum('hcd,hce->hde', key_block, residual, precision=precise)  78.9 us
    reduce_scatter x1, waiting for transfers between devices, on_device(): lax.psum_scatter(jnp.dot(headed_low, out_weight, preferred_element_type=j...  71.2 us
  transfers between devices with their start and end apart: 9, of which 7 were waited for; matrix products, arithmetic and copies ran while one was open for 4% of the time, Pallas kernels for 0%

commit v1 on v0

v1 whole, which is shorter than its diff:
```python
import functools
import jax
import jax.numpy as jnp
from jax import lax
from jax.experimental import pallas as pl
from jax.experimental.pallas import tpu as pltpu
from jax.sharding import PartitionSpec as P

HEAD = 128
STEP = 128
SPAN = 64
STEPS = 4
ROWS = STEP * STEPS
NN = (((1,), (0,)), ((), ()))
NT = (((1,), (1,)), ((), ()))
TN = (((0,), (0,)), ((), ()))
f32 = jnp.float32
bf16 = jnp.bfloat16


def mm(a, b, dims=NN):
    return lax.dot_general(a.astype(bf16), b.astype(bf16), dims, preferred_element_type=f32)


def split(a):
    high = a.astype(bf16)
    return high, (a - high.astype(f32)).astype(bf16)


def stack(x):
    return jnp.concatenate([x[:, :HEAD], x[:, HEAD:]], axis=0)


def unstack(x):
    return jnp.concatenate([x[:STEP], x[STEP:]], axis=1)


def pair_masks():
    i = lax.broadcasted_iota(jnp.int32, (2 * STEP, 2 * STEP), 0)
    j = lax.broadcasted_iota(jnp.int32, (2 * STEP, 2 * STEP), 1)
    same = (i // STEP) == (j // STEP)
    cross = ((i % STEP) >= SPAN) & ((j % STEP) < SPAN)
    levels = []
    size = 1
    while size < STEP:
        levels.append(((i // (2 * size)) == (j // (2 * size))) & ((i // size) % 2 == 1) & ((j // size) % 2 == 0))
        size *= 2
    return same & (i > j), same & (i >= j), cross, levels, i == j


def tri_inverse(a, levels, eye):
    inv = jnp.where(eye, 1.0, jnp.where(levels[0], -a, 0.0))
    for level in levels[1:]:
        low = inv.astype(bf16)
        part = jnp.where(level, a, 0.0).astype(bf16)
        inv = inv - mm(mm(low, part), low)
    return inv


def row_masks(start_reset, mid_reset):
    r = lax.broadcasted_iota(jnp.int32, (2 * STEP, HEAD), 0) % STEP
    upper = r < SPAN
    enter = jnp.where(upper, 1.0 - start_reset, (1.0 - start_reset) * (1.0 - mid_reset))
    leave = jnp.where(upper, 1.0 - mid_reset, 1.0)
    keep = (1.0 - start_reset) * (1.0 - mid_reset)
    return enter, leave, keep


def resets(step_start, first):
    start = jnp.where((step_start == 0) | (step_start == first), 1.0, 0.0).astype(f32)
    mid = jnp.where(step_start + SPAN == first, 1.0, 0.0).astype(f32)
    return start, mid


def conv_masks(base, first, rows):
    r = lax.broadcasted_iota(jnp.int32, (rows, HEAD), 0) + base
    pos = jnp.where(r >= first, r - first, r)
    return [pos >= j for j in range(4)]


def mixer_fwd_kernel(first_ref, proj_ref, conv_ref, gain_ref, headed_ref, mixed_ref, state_out, res_out, wu_out, inv_out, state, buf):
    g = pl.program_id(0)
    first = first_ref[0]

    @pl.when(g == 0)
    def _():
        state[...] = jnp.zeros_like(state)
        buf[0:8, :] = jnp.zeros((8, buf.shape[1]), f32)

    width = buf.shape[1]
    buf[8:, :] = proj_ref[:, :width]
    valid = conv_masks(g * ROWS, first, ROWS)
    cols = []
    for c in range(width // HEAD):
        cs = slice(c * HEAD, (c + 1) * HEAD)
        total = buf[8:8 + ROWS, cs] * conv_ref[0:1, cs]
        for j in range(1, 4):
            total = total + jnp.where(valid[j], buf[8 - j:8 - j + ROWS, cs] * conv_ref[j:j + 1, cs], 0.0)
        cols.append(total * jax.nn.sigmoid(total))
    buf[0:8, :] = buf[ROWS:ROWS + 8, :]
    betas = jax.nn.sigmoid(proj_ref[:, width:])
    strict, causal, cross, levels, eye = pair_masks()
    mem = [state[0], state[1]]
    for s in range(STEPS):
        rs = slice(s * STEP, (s + 1) * STEP)
        start_reset, mid_reset = resets(g * ROWS + s * STEP, first)
        enter, leave, keep = row_masks(start_reset, mid_reset)
        gate = jnp.where(cross, 1.0 - mid_reset, 1.0)
        two = lambda n: jnp.concatenate([cols[2 * n][rs], cols[2 * n + 1][rs]], axis=0)
        q, k, v = two(0), two(1), two(2)
        q = q * lax.rsqrt(jnp.sum(q * q, axis=-1, keepdims=True) + 1e-6)
        k = k * lax.rsqrt(jnp.sum(k * k, axis=-1, keepdims=True) + 1e-6)
        b = jnp.concatenate([betas[rs, 0:1], betas[rs, 1:2]], axis=0)
        gp = mm(jnp.concatenate([k, q], axis=0), k, NT)
        a = jnp.where(strict, gate * gp[:2 * STEP], 0.0) * b
        p = jnp.where(causal, gate * gp[2 * STEP:], 0.0)
        inv = tri_inverse(a, levels, eye)
        wu = mm(inv, jnp.concatenate([b * k, b * v], axis=1))
        inv_out[s] = inv.astype(bf16)
        wu_out[s] = wu.astype(bf16)
        state_out[s, :HEAD] = mem[0].astype(bf16)
        state_out[s, HEAD:] = mem[1].astype(bf16)
        w = wu[:, :HEAD] * enter
        qe = q * enter
        ws, qs = [], []
        for h in range(2):
            hs = slice(h * STEP, (h + 1) * STEP)
            both = mm(jnp.concatenate([w[hs], qe[hs]], axis=0), mem[h])
            ws.append(both[:STEP])
            qs.append(both[STEP:])
        res = wu[:, HEAD:] - jnp.concatenate(ws, axis=0)
        res_out[s] = res.astype(bf16)
        ke = k * leave
        for h in range(2):
            hs = slice(h * STEP, (h + 1) * STEP)
            mem[h] = keep * mem[h] + mm(ke[hs], res[hs], TN)
        o = jnp.concatenate(qs, axis=0) + mm(p, res)
        mixed_ref[rs, :] = unstack(o)
        headed = o * lax.rsqrt(jnp.mean(o * o, axis=-1, keepdims=True) + 1e-5) * gain_ref[...]
        headed_ref[rs, :] = unstack(headed).astype(bf16)
    state[0] = mem[0]
    state[1] = mem[1]


def mixer_fwd(first, proj, conv, gain):
    rows, total = proj.shape
    width = conv.shape[1]
    n = rows // ROWS
    steps = rows // STEP
    return pl.pallas_call(
        mixer_fwd_kernel,
        grid_spec=pltpu.PrefetchScalarGridSpec(
            num_scalar_prefetch=1, grid=(n,),
            in_specs=[pl.BlockSpec((ROWS, total), lambda g, f: (g, 0)), pl.BlockSpec((4, width), lambda g, f: (0, 0)), pl.BlockSpec((1, HEAD), lambda g, f: (0, 0))],
            out_specs=[pl.BlockSpec((ROWS, 2 * HEAD), lambda g, f: (g, 0)), pl.BlockSpec((ROWS, 2 * HEAD), lambda g, f: (g, 0)),
                       pl.BlockSpec((STEPS, 2 * HEAD, HEAD), lambda g, f: (g, 0, 0)), pl.BlockSpec((STEPS, 2 * STEP, HEAD), lambda g, f: (g, 0, 0)),
                       pl.BlockSpec((STEPS, 2 * STEP, 2 * HEAD), lambda g, f: (g, 0, 0)), pl.BlockSpec((STEPS, 2 * STEP, 2 * STEP), lambda g, f: (g, 0, 0))],
            scratch_shapes=[pltpu.VMEM((2, HEAD, HEAD), f32), pltpu.VMEM((ROWS + 8, width), f32)]),
        out_shape=[jax.ShapeDtypeStruct((rows, 2 * HEAD), bf16), jax.ShapeDtypeStruct((rows, 2 * HEAD), f32),
                   jax.ShapeDtypeStruct((steps, 2 * HEAD, HEAD), bf16), jax.ShapeDtypeStruct((steps, 2 * STEP, HEAD), bf16),
                   jax.ShapeDtypeStruct((steps, 2 * STEP, 2 * HEAD), bf16), jax.ShapeDtypeStruct((steps, 2 * STEP, 2 * STEP), bf16)],
        compiler_params=pltpu.CompilerParams(dimension_semantics=("arbitrary",), vmem_limit_bytes=48 * 2**20),
    )(first, proj, conv, gain)


def mixer_bwd_kernel(first_ref, proj_ref, prev_ref, conv_ref, gain_ref, dh_ref, mixed_ref, state_in, res_in, wu_in, inv_in,
                     dcat_ref, dconv_ref, dgain_ref, dstate, buf, dbuf, cacc, gacc):
    g = pl.program_id(0)
    n = pl.num_programs(0)
    blk = n - 1 - g
    first = first_ref[0]
    width = buf.shape[1]

    @pl.when(g == 0)
    def _():
        dstate[...] = jnp.zeros_like(dstate)
        dbuf[ROWS:, :] = jnp.zeros((8, width), f32)
        cacc[...] = jnp.zeros_like(cacc)
        gacc[...] = jnp.zeros_like(gacc)

    buf[0:8, :] = prev_ref[:, :width]
    buf[8:, :] = proj_ref[:, :width]
    valid = conv_masks(blk * ROWS, first, ROWS + 8)
    cols, slopes = [], []
    for c in range(width // HEAD):
        cs = slice(c * HEAD, (c + 1) * HEAD)
        total = buf[8:8 + ROWS, cs] * conv_ref[0:1, cs]
        for j in range(1, 4):
            total = total + jnp.where(valid[j][:ROWS], buf[8 - j:8 - j + ROWS, cs] * conv_ref[j:j + 1, cs], 0.0)
        sig = jax.nn.sigmoid(total)
        cols.append(total * sig)
        slopes.append(sig * (1.0 + total * (1.0 - sig)))
    betas = jax.nn.sigmoid(proj_ref[:, width:])
    strict, causal, cross, _, _ = pair_masks()
    lane = lax.broadcasted_iota(jnp.int32, (STEP, HEAD), 1)
    dmem = [dstate[0], dstate[1]]
    for s in reversed(range(STEPS)):
        rs = slice(s * STEP, (s + 1) * STEP)
        start_reset, mid_reset = resets(blk * ROWS + s * STEP, first)
        enter, leave, keep = row_masks(start_reset, mid_reset)
        gate = jnp.where(cross, 1.0 - mid_reset, 1.0)
        two = lambda n: jnp.concatenate([cols[2 * n][rs], cols[2 * n + 1][rs]], axis=0)
        q, k, v = two(0), two(1), two(2)
        rq = lax.rsqrt(jnp.sum(q * q, axis=-1, keepdims=True) + 1e-6)
        rk = lax.rsqrt(jnp.sum(k * k, axis=-1, keepdims=True) + 1e-6)
        q = q * rq
        k = k * rk
        b = jnp.concatenate([betas[rs, 0:1], betas[rs, 1:2]], axis=0)
        gp = mm(jnp.concatenate([k, q], axis=0), k, NT)
        gram = jnp.where(strict, gate * gp[:2 * STEP], 0.0)
        p = jnp.where(causal, gate * gp[2 * STEP:], 0.0)
        o = stack(mixed_ref[rs, :])
        dh = stack(dh_ref[rs, :].astype(f32))
        ro = lax.rsqrt(jnp.mean(o * o, axis=-1, keepdims=True) + 1e-5)
        on = o * ro
        gacc[...] += jnp.sum((dh * on).reshape(2 * STEP // 8, 8, HEAD), axis=0)
        dn = dh * gain_ref[...]
        do = ro * (dn - on * jnp.mean(dn * on, axis=-1, keepdims=True))
        mem = state_in[s]
        res = res_in[s]
        wu = wu_in[s]
        inv = inv_in[s]
        do16 = do.astype(bf16)
        doe = (do * enter).astype(bf16)
        q16 = q.astype(bf16)
        k16 = k.astype(bf16)
        ke16 = (k * leave).astype(bf16)
        we = (wu[:, :HEAD].astype(f32) * enter).astype(bf16)
        dres = mm(p, do16, TN)
        hs = [slice(h * STEP, (h + 1) * STEP) for h in range(2)]
        dres = dres + jnp.concatenate([mm(ke16[hs[h]], dmem[h]) for h in range(2)], axis=0)
        dres16 = dres.astype(bf16)
        dke = jnp.concatenate([mm(res[hs[h]], dmem[h], NT) for h in range(2)], axis=0)
        for h in range(2):
            dmem[h] = keep * dmem[h] + mm(q16[hs[h]], doe[hs[h]], TN) - mm(we[hs[h]], dres16[hs[h]], TN)
        dp = jnp.where(causal, gate * mm(do16, res, NT), 0.0).astype(bf16)
        both = [mm(jnp.concatenate([do16[hs[h]], dres16[hs[h]]], axis=0), mem[h * HEAD:(h + 1) * HEAD], NT) for h in range(2)]
        dq = enter * jnp.concatenate([both[0][:STEP], both[1][:STEP]], axis=0) + mm(dp, k16)
        dw = -enter * jnp.concatenate([both[0][STEP:], both[1][STEP:]], axis=0)
        dk = mm(dp, q16, TN) + leave * dke
        db_kv = mm(inv, jnp.concatenate([dw, dres], axis=1), TN)
        da = -jnp.where(strict, gate * mm(db_kv, wu, NT), 0.0)
        dbk, dbv = db_kv[:, :HEAD], db_kv[:, HEAD:]
        dbeta = jnp.sum(da * gram, axis=-1, keepdims=True) + jnp.sum(dbk * k + dbv * v, axis=-1, keepdims=True)
        dg = (da * b).astype(bf16)
        dk = dk + mm(dg, k16) + mm(dg, k16, TN) + b * dbk
        dv = b * dbv
        dq = rq * (dq - q * jnp.sum(dq * q, axis=-1, keepdims=True))
        dk = rk * (dk - k * jnp.sum(dk * k, axis=-1, keepdims=True))
        dpre = dbeta * b * (1.0 - b)
        for i, x in enumerate((dq, dk, dv)):
            for h in range(2):
                c = 2 * i + h
                dbuf[rs, c * HEAD:(c + 1) * HEAD] = x[hs[h]] * slopes[c][rs]
        dcat_ref[rs, width:] = jnp.where(lane == 0, dpre[:STEP], jnp.where(lane == 1, dpre[STEP:], 0.0)).astype(bf16)
    dstate[0] = dmem[0]
    dstate[1] = dmem[1]
    for c in range(width // HEAD):
        cs = slice(c * HEAD, (c + 1) * HEAD)
        total = dbuf[:ROWS, cs] * conv_ref[0:1, cs]
        grads = [jnp.sum((buf[8:8 + ROWS, cs] * dbuf[:ROWS, cs]).reshape(ROWS // 8, 8, HEAD), axis=0)]
        for j in range(1, 4):
            total = total + jnp.where(shifted_valid(blk * ROWS, first, j), dbuf[j:j + ROWS, cs] * conv_ref[j:j + 1, cs], 0.0)
            grads.append(jnp.sum(jnp.where(valid[j][:ROWS], buf[8 - j:8 - j + ROWS, cs] * dbuf[:ROWS, cs], 0.0).reshape(ROWS // 8, 8, HEAD), axis=0))
        dcat_ref[:, cs] = total.astype(bf16)
        for j in range(4):
            cacc[j, :, cs] += grads[j]
    dbuf[ROWS:, :] = dbuf[0:8, :]

    @pl.when(g == n - 1)
    def _():
        for j in range(4):
            dconv_ref[j:j + 1, :] = jnp.sum(cacc[j], axis=0, keepdims=True)
        dgain_ref[...] = jnp.sum(gacc[...], axis=0, keepdims=True)


def shifted_valid(base, first, j):
    r = lax.broadcasted_iota(jnp.int32, (ROWS, HEAD), 0) + base + j
    pos = jnp.where(r >= first, r - first, r)
    return pos >= j


def mixer_bwd(first, proj, conv, gain, dheaded, saved):
    rows, total = proj.shape
    width = conv.shape[1]
    n = rows // ROWS
    mixed, st, res, wu, inv = saved
    m2 = lambda g, f: (n - 1 - g, 0)
    m3 = lambda g, f: (n - 1 - g, 0, 0)
    z2 = lambda g, f: (0, 0)
    return pl.pallas_call(
        mixer_bwd_kernel,
        grid_spec=pltpu.PrefetchScalarGridSpec(
            num_scalar_prefetch=1, grid=(n,),
            in_specs=[pl.BlockSpec((ROWS, total), m2),
                      pl.BlockSpec((8, total), lambda g, f: (jnp.maximum((n - 1 - g) * (ROWS // 8) - 1, 0), 0)),
                      pl.BlockSpec((4, width), z2), pl.BlockSpec((1, HEAD), z2),
                      pl.BlockSpec((ROWS, 2 * HEAD), m2), pl.BlockSpec((ROWS, 2 * HEAD), m2),
                      pl.BlockSpec((STEPS, 2 * HEAD, HEAD), m3), pl.BlockSpec((STEPS, 2 * STEP, HEAD), m3),
                      pl.BlockSpec((STEPS, 2 * STEP, 2 * HEAD), m3), pl.BlockSpec((STEPS, 2 * STEP, 2 * STEP), m3)],
            out_specs=[pl.BlockSpec((ROWS, total), m2), pl.BlockSpec((4, width), z2), pl.BlockSpec((1, HEAD), z2)],
            scratch_shapes=[pltpu.VMEM((2, HEAD, HEAD), f32), pltpu.VMEM((ROWS + 8, width), f32), pltpu.VMEM((ROWS + 8, width), f32),
                            pltpu.VMEM((4, 8, width), f32), pltpu.VMEM((8, HEAD), f32)]),
        out_shape=[jax.ShapeDtypeStruct((rows, total), bf16), jax.ShapeDtypeStruct((4, width), f32), jax.ShapeDtypeStruct((1, HEAD), f32)],
        compiler_params=pltpu.CompilerParams(dimension_semantics=("arbitrary",), vmem_limit_bytes=56 * 2**20),
    )(first, proj, proj, conv, gain, dheaded, mixed, st, res, wu, inv)


def rms_norm(values, scales):
    inverse = lax.rsqrt(jnp.mean(values * values, axis=-1, keepdims=True) + 1e-05)
    return values * inverse * scales


def gather(x):
    return lax.all_gather(x, "tensor", axis=0, tiled=True)


def scatter_sum(x):
    return lax.psum_scatter(x, "tensor", scatter_dimension=0, tiled=True)


def dot(a, b, dims=NN):
    return lax.dot_general(a, b, dims, preferred_element_type=f32)


def on_device(tokens, lengths, attn_gain, qkv_weight, beta_weight, conv_weight, head_gain, out_weight, mlp_gain, gate_up_weight, down_weight, cotangent):
    model_width = tokens.shape[1]
    width = qkv_weight.shape[1] * qkv_weight.shape[2]
    heads = beta_weight.shape[1]
    first = lengths[0, :1]
    local_in = tokens.astype(f32)
    first_scale = attn_gain.astype(f32)
    second_scale = mlp_gain.astype(f32)
    head_scale = head_gain.astype(f32)[None]
    conv = conv_weight.reshape(conv_weight.shape[0], -1).astype(f32)
    qkv_matrix = jnp.concatenate([qkv_weight.reshape(model_width, -1), jnp.pad(beta_weight, ((0, 0), (0, HEAD - heads)))], axis=1)
    out_all = gather(out_weight)
    attn_in = rms_norm(local_in, first_scale).astype(bf16)
    attn_all = gather(attn_in)
    proj = dot(attn_all, qkv_matrix)
    headed, *saved = mixer_fwd(first, proj, conv, head_scale)
    headed_rows = lax.all_to_all(headed, "tensor", split_axis=0, concat_axis=1, tiled=True)
    hidden_res = local_in + dot(headed_rows, out_all)
    mlp_in = rms_norm(hidden_res, second_scale).astype(bf16)
    mlp_all = gather(mlp_in)
    cot_all = gather(cotangent)
    gate_up_matrix = gate_up_weight.reshape(model_width, -1)
    gate_up = dot(mlp_all, gate_up_matrix)
    hidden_units = gate_up.shape[1] // 2
    gate_pre = gate_up[:, :hidden_units]
    up_pre = gate_up[:, hidden_units:]
    sigmoid_gate = jax.nn.sigmoid(gate_pre)
    silu_gate = gate_pre * sigmoid_gate
    activated = (silu_gate * up_pre).astype(bf16)
    d_activated = dot(cot_all, down_weight, NT)
    d_gate = (d_activated * up_pre * sigmoid_gate * (1.0 + gate_pre * (1.0 - sigmoid_gate))).astype(bf16)
    d_up = (d_activated * silu_gate).astype(bf16)
    d_gate_up = jnp.concatenate([d_gate, d_up], axis=1)
    d_mlp_in = scatter_sum(dot(d_gate_up, gate_up_matrix, NT).astype(bf16)).astype(f32)
    mlp_out = scatter_sum(dot(activated, down_weight).astype(bf16)).astype(f32)
    output = (hidden_res + mlp_out).astype(bf16)
    down_part = dot(activated, cot_all, TN).astype(bf16)
    gate_up_part = dot(mlp_all, d_gate_up, TN).astype(bf16)
    gate_up_sum, down_sum = lax.psum((gate_up_part, down_part), "dp")
    d_from_mlp, mlp_gain_part = jax.vjp(rms_norm, hidden_res, second_scale)[1](d_mlp_in)
    d_hidden = cotangent.astype(f32) + d_from_mlp
    d_attn = d_hidden.astype(bf16)
    d_headed_rows = dot(d_attn, out_all, NT).astype(bf16)
    d_headed = lax.all_to_all(d_headed_rows, "tensor", split_axis=1, concat_axis=0, tiled=True)
    d_attn_all = gather(d_attn)
    d_cat, conv_part, head_gain_part = mixer_bwd(first, proj, conv, head_scale, d_headed, saved)
    d_attn_in = scatter_sum(dot(d_cat, qkv_matrix, NT).astype(bf16)).astype(f32)
    d_from_attn, attn_gain_part = jax.vjp(rms_norm, local_in, first_scale)[1](d_attn_in)
    input_grad = d_hidden + d_from_attn
    d_cat, gate_up_sum, down_sum = lax.optimization_barrier((d_cat, gate_up_sum, down_sum))
    cat_part = dot(attn_all, d_cat, TN).astype(bf16)
    out_part = dot(headed, d_attn_all, TN).astype(bf16)
    cat_sum, out_sum, conv_sum = lax.psum((cat_part, out_part, conv_part.astype(bf16)), "dp")
    attn_gain_grad, head_gain_grad, mlp_gain_grad = lax.psum((attn_gain_part, head_gain_part[0], mlp_gain_part), ("dp", "tensor"))
    return (
        output,
        input_grad,
        attn_gain_grad,
        cat_sum[:, :width].astype(f32).reshape(qkv_weight.shape),
        cat_sum[:, width:width + heads].astype(f32),
        conv_sum.astype(f32).reshape(conv_weight.shape),
        head_gain_grad,
        out_sum.astype(f32),
        mlp_gain_grad,
        gate_up_sum.astype(f32).reshape(gate_up_weight.shape),
        down_sum.astype(f32),
    )


def solution(mesh):
    rows = P(("dp", "tensor"), None)
    last = P(None, None, "tensor")
    return jax.shard_map(
        on_device,
        mesh=mesh,
        in_specs=(rows, P("dp", None), P(), last, P(None, "tensor"), last, P(), P("tensor", None), P(), last, P("tensor", None), rows),
        out_specs=(rows, rows, P(), last, P(None, "tensor"), last, P(), P("tensor", None), P(), last, P("tensor", None)),
        check_vma=False,
    )
```

time: 1860 us -> 695 us (0.37)
  matrix products: 499 us -> 91 us
  local copies, waits for them, and re-layouts: 343 us -> 29 us
  waiting for transfers between devices: 613 us -> 363 us
  other arithmetic: 251 us -> 27 us
  Pallas kernels: 0 us -> 75.7 us
  loops' own time: 44.8 us -> 0 us
    dot_general x438 -> x12, matrix products: 484 us -> 91 us  [dot(): return lax.dot_general(a, b, dims, preferred_element_type=f32)]
    psum x1 -> x2, waiting for transfers between devices: 380 us -> 162 us  [the longest x1 99.8 us: on_device(): gate_up_sum, down_sum = lax.psum((gate_up_part, down_part), 'dp')]
    another operation x35 -> x0, other arithmetic: 142 us -> none  [the longest x3 142 us: delta_rule(): jax.scipy.linalg.solve_triangular(system, right_hand, lower=True, unit_di...]
    squeeze x161 -> x0, local copies, waits for them, and re-layouts: 141 us -> none  [the longest x160 139 us: delta_rule(): _, outputs = lax.scan(jax.checkpoint(advance), initial, inputs)]
    pallas_call x0 -> x2, Pallas kernels: none -> 75.7 us  [the longest x1 38.4 us: mixer_bwd(): pl.pallas_call(mixer_bwd_kernel, grid_spec=pltpu.PrefetchScalarGridSpec(n...]
    reduce_scatter x4 -> x3, waiting for transfers between devices: 116 us -> 66 us  [scatter_sum(): return lax.psum_scatter(x, 'tensor', scatter_dimension=0, tiled=True)]
    another operation x2 -> x0, loops' own time: 44.8 us -> none  [delta_rule(): _, outputs = lax.scan(jax.checkpoint(advance), initial, inputs)]
    dynamic_slice x64 -> x0, local copies, waits for them, and re-layouts: 37.4 us -> none  [delta_rule(): _, outputs = lax.scan(jax.checkpoint(advance), initial, inputs)]
  transfers between devices with their start and end apart: 9 -> 11, of which waited for: 7 -> 10; matrix products, arithmetic and copies ran while one was open for 4% -> 14% of each run, Pallas kernels for 0% -> 11%
where the time goes in v1:
time: 695 us; the launch traced here: 686 us
  waiting for transfers between devices  363 us (52%)
  matrix products  91 us (13%)
  blocking collectives  80.3 us (12%)
  Pallas kernels  75.7 us (11%)
  local copies, waits for them, and re-layouts  29 us (4%)
  other arithmetic  27 us (4%)
  between operations  14.8 us (2%)
    all_gather x5, waiting for transfers between devices, gather(): return lax.all_gather(x, 'tensor', axis=0, tiled=True)  119 us
    psum x1, waiting for transfers between devices, on_device(): gate_up_sum, down_sum = lax.psum((gate_up_part, down_part), 'dp')  99.8 us
    dot_general x12, matrix products, dot(): return lax.dot_general(a, b, dims, preferred_element_type=f32)  91 us
    reduce_scatter x3, waiting for transfers between devices, scatter_sum(): return lax.psum_scatter(x, 'tensor', scatter_dimension=0, tiled=True)  66 us
    psum x1, waiting for transfers between devices, on_device(): lax.psum((cat_part, out_part, conv_part.astype(bf16)), 'dp')  62.7 us
    psum x1, blocking collectives, on_device(): lax.psum((attn_gain_part, head_gain_part[0], mlp_gain_part), ('dp', 'tens...  39.8 us
    pallas_call x1, Pallas kernels, mixer_bwd(): pl.pallas_call(mixer_bwd_kernel, grid_spec=pltpu.PrefetchScalarGridSpec(n...  38.4 us
    pallas_call x1, Pallas kernels, mixer_fwd(): pl.pallas_call(mixer_fwd_kernel, grid_spec=pltpu.PrefetchScalarGridSpec(n...  37.3 us
  transfers between devices with their start and end apart: 11, of which 10 were waited for; matrix products, arithmetic and copies ran while one was open for 14% of the time, Pallas kernels for 11%

profile of v1, /device:TPU:0, one launch (start us, length us, event | category | flops | bytes accessed | tf_op | source)
XLA Modules:
  0.0 686.2 jit_solution(7471980760025238978)
XLA Ops:
  7.2 1.7 fusion.12
  8.9 0.7 convert_element_type.90
  9.6 2.5 fusion.6
  12.2 0.7 all-gather.8.cloned.1.call-update
  12.9 2.6 copy.30
  15.5 33.9 %all-gather.6.cloned.1.call-done = bf16[2048,1024]{1,0:T(8,128)(2,1)} async-done(((bf16[512,1024]{1,0:T(8,128)(2,1)}), bf16[2048,1024]{1,0:T(8,128)(2,1)}) %all-gather.6.cloned.1.call-update) | async-done | bytes 4194320 | tf_op jit(solution)/shard_map/all_gather | solution.py:315
  49.5 10.3 %fusion.16.proj_ref.prev_ref = f32[2048,896]{1,0:T(8,128)} fusion(bf16[2048,1024]{1,0:T(8,128)(2,1)} %all-gather.6.cloned.1.call-done, bf16[1024,2]{0,1:T(2,128)(2,1)S(1)} %copy-done.23, bf16[1024,768]{0,1:T(8,128)(2,1)} %bitcast.53), kind=kOutput, calls=%fused_computation.45 | convolution fusion | flops 3763601408 | bytes 13111296 | tf_op jit(solution)/shard_map/dot_general | solution.py:323
  59.7 37.3 %shard_map.203 = (bf16[2048,256]{1,0:T(8,128)(2,1)S(1)}, f32[2048,256]{1,0:T(8,128)S(1)}, bf16[16,256,128]{2,1,0:T(8,128)(2,1)S(1)}, bf16[16,256,128]{2,1,0:T(8,...) custom-call(s32[1]{0:T(128)S(1)} %bitcast.48, f32[2048,896]{1,0:T(8,128)} %fusion.16.proj_ref.prev_ref, ...), custom_call_target="tpu_custom_call" | custom-call | tf_op jit(solution)/shard_map/pallas_call | solution.py:150
  97.1 1.3 copy-done.2
  98.4 1.0 copy-done.3
  99.4 1.0 copy-done.4
  100.4 1.0 copy-done.5
  101.4 2.3 copy.31
  103.7 4.3 all-to-all-start
  108.0 0.5 all-gather.10.cloned.1.call-start
  108.5 14.0 %all-to-all-done = bf16[4,512,256]{1,2,0:T(8,128)(2,1)} async-done(((bf16[4,512,256]{1,2,0:T(8,128)(2,1)}), bf16[4,512,256]{1,2,0:T(8,128)(2,1)}, u32[]{:S(2)}, u32[]{:S(2)}) %all-to-all-start) | async-done | bytes 1048608 | tf_op jit(solution)/shard_map/all_to_all | solution.py:342
  122.5 3.5 multiply_reduce_fusion
  126.0 1.3 copy-done.10
  127.3 1.2 multiply_convert_fusion.3
  128.6 0.5 all-gather.12.cloned.1.call-update
  129.2 34.1 %all-gather.10.cloned.1.call-done = bf16[2048,1024]{1,0:T(8,128)(2,1)} async-done(((bf16[512,1024]{1,0:T(8,128)(2,1)}), bf16[2048,1024]{1,0:T(8,128)(2,1)}) %all-gather.10.cloned.1.call-update) | async-done | bytes 4194320 | tf_op jit(solution)/shard_map/all_gather | solution.py:315
  163.3 11.3 %fusion.29 = f32[2048,1408]{0,1:T(8,128)} fusion(bf16[2048,1024]{1,0:T(8,128)(2,1)} %all-gather.10.cloned.1.call-done, bf16[1024,1408]{0,1:T(8,128)(2,1)S(1)} %bitcast.44), kind=kOutput, calls=%fused_computation.63 | convolution fusion | flops 5905580032 | bytes 18612224 | tf_op jit(solution)/shard_map/dot_general | solution.py:323
  174.6 24.6 %all-gather.12.cloned.1.call-done = bf16[2048,1024]{1,0:T(8,128)(2,1)} async-done(((bf16[512,1024]{1,0:T(8,128)(2,1)}), bf16[2048,1024]{1,0:T(8,128)(2,1)}) %all-gather.12.cloned.1.call-update) | async-done | bytes 4194320 | tf_op jit(solution)/shard_map/all_gather | solution.py:315
  199.2 11.1 %multiply_convert_fusion.1 = (bf16[2048,704]{0,1:T(8,128)(2,1)S(1)}, bf16[2048,704]{0,1:T(8,128)(2,1)S(1)}, bf16[2048,704]{0,1:T(8,128)(2,1)}) fusion(f32[2048,1408]{0,1:T(8,128)} %fusion.29, bf16[2048,1024]{1,0:T(8,128)(2,1)} %all-gather.12.cloned.1.call-done, bf16[704,1024]{1,0:T(8,128)(2,1)} %param.22), kind=kOutput, calls=%fused_computation.2 | convolution fusion | flops 2974416896 | bytes 25821184 | tf_op jit(solution)/shard_map/dot_general | solution.py:323
  210.3 1.6 copy-done.26
  211.9 1.0 copy-done.28
  212.8 8.3 %convolution_convert_fusion.1 = bf16[2048,1024]{1,0:T(8,128)(2,1)} fusion(bf16[1024,1408]{0,1:T(8,128)(2,1)S(1)} %bitcast.45, bf16[2048,704]{0,1:T(8,128)(2,1)S(1)} %get-tuple-element.69, bf16[2048,704]{0,1:T(8,128)(2,1)S(1)} %get-tuple-element.68), kind=kOutput, calls=%fused_computation.12 | convolution fusion | flops 5919211520 | bytes 12845056 | tf_op jit(solution)/shard_map/dot_general | solution.py:323
  221.2 0.2 all-reduce.9.cloned.1.call-start
  221.4 1.6 copy-done.25
  222.9 6.6 convolution_convert_fusion.5
  229.5 8.1 %convolution_convert_fusion = bf16[1024,1408]{1,0:T(8,128)(2,1)} fusion(bf16[2048,1024]{1,0:T(8,128)(2,1)S(1)} %copy-done.21, bf16[2048,704]{0,1:T(8,128)(2,1)S(1)} %copy-done.29, bf16[2048,704]{0,1:T(8,128)(2,1)S(1)} %copy-done.27), kind=kOutput, calls=%fused_computation.11 | convolution fusion | flops 5918556160 | bytes 12845056 | tf_op jit(solution)/shard_map/dot_general | solution.py:323
  237.6 0.0 all-gather.14.cloned.1.call-start
  237.7 28.1 %reduce-scatter.6.cloned.1.call-done = bf16[512,1024]{1,0:T(8,128)(2,1)} async-done(((bf16[2048,1024]{1,0:T(8,128)(2,1)}), bf16[512,1024]{1,0:T(8,128)(2,1)}) %reduce-scatter.6.cloned.1.call-update) | async-done | bytes 1048592 | tf_op jit(solution)/shard_map/reduce_scatter | solution.py:319
  265.8 2.0 fusion.8
  267.8 2.8 fusion.28
  270.7 0.0 all-reduce.7.cloned.1.call-start
  270.7 3.2 convolution_convert_fusion.6
  274.0 0.1 copy.39
  274.0 17.8 %all_to_all.38 = bf16[512,4,256]{2,0,1:T(8,128)(2,1)} all-to-all(bf16[512,4,256]{2,0,1:T(8,128)(2,1)S(1)} %bitcast.52), channel_id=1, replica_groups=mesh['dp'=8,'tensor'=4] {'tensor'}, dimensions={1} | all-to-all | bytes 2097152 | tf_op jit(solution)/shard_map/all_to_all | solution.py:369
  291.8 38.4 %shard_map.204 = (bf16[2048,896]{1,0:T(8,128)(2,1)}, f32[4,768]{1,0:T(4,128)}, f32[1,128]{1,0:T(1,128)}) custom-call(s32[1]{0:T(128)} %bitcast.47, f32[2048,896]{1,0:T(8,128)} %fusion.16.proj_ref.prev_ref, f32[2048,896]{1,0:T(8,128)} %fusion.16.proj_ref.prev_ref, f32[4,768]{1,0:T(4,128)} %copy-done.7, f32[1,128]{1,0:T(1,128)} %copy-done.9, ...), custom_call_target="tpu_custom_call" | custom-call | tf_op jit(solution)/shard_map/pallas_call | solution.py:291
  330.2 99.8 %all-reduce.9.cloned.1.call-done = (bf16[1024,1408]{1,0:T(8,128)(2,1)}, bf16[704,1024]{1,0:T(8,128)(2,1)}) async-done(((bf16[1024,1408]{1,0:T(8,128)(2,1)}, bf16[704,1024]{1,0:T(8,128)(2,1)}), (bf16[1024,1408]{1,0:T(8,128)(2,1)}, bf16[704,1024]{1,0:T(8,128)(2,1)})) %all-reduce.9.cloned.1.call-update) | async-done | bytes 4325392 | tf_op jit(solution)/shard_map/psum | solution.py:364
  430.0 9.2 %convolution_convert_fusion.4 = bf16[1024,896]{1,0:T(8,128)(2,1)} fusion(bf16[2048,1024]{1,0:T(8,128)(2,1)} %all-gather.6.cloned.1.call-done, bf16[2048,896]{1,0:T(8,128)(2,1)} %get-tuple-element.30), kind=kOutput, calls=%fused_computation.39 | convolution fusion | flops 3759013888 | bytes 9699328 | tf_op jit(solution)/shard_map/dot_general | solution.py:323
  439.2 26.6 %all-gather.14.cloned.1.call-done = bf16[2048,1024]{1,0:T(8,128)(2,1)} async-done(((bf16[512,1024]{1,0:T(8,128)(2,1)}), bf16[2048,1024]{1,0:T(8,128)(2,1)}) %all-gather.14.cloned.1.call-update) | async-done | bytes 4194320 | tf_op jit(solution)/shard_map/all_gather | solution.py:315
  465.7 4.3 convolution_convert_fusion.7
  470.1 8.2 %convolution_convert_fusion.3 = bf16[2048,1024]{1,0:T(8,128)(2,1)} fusion(bf16[2048,896]{1,0:T(8,128)(2,1)} %get-tuple-element.30, bf16[1024,2]{0,1:T(2,128)(2,1)S(1)} %copy-done.23, bf16[1024,768]{0,1:T(8,128)(2,1)S(1)} %bitcast.54), kind=kOutput, calls=%fused_computation.14 | convolution fusion | flops 3765698560 | bytes 9441280 | tf_op jit(solution)/shard_map/dot_general | solution.py:323
  478.3 1.3 copy-done.22
  479.6 7.0 %convolution_convert_fusion.2 = bf16[2048,1024]{1,0:T(8,128)(2,1)} fusion(bf16[2048,704]{0,1:T(8,128)(2,1)} %get-tuple-element.70, bf16[704,1024]{1,0:T(8,128)(2,1)S(1)} %copy-done.22), kind=kOutput, calls=%fused_computation.13 | convolution fusion | flops 2954887168 | bytes 8519680 | tf_op jit(solution)/shard_map/dot_general | solution.py:323
  486.7 0.7 copy-done.17
  487.3 22.7 %psum.60 = bf16[4,3,256]{2,0,1:T(4,128)(2,1)S(1)} all-reduce(bf16[4,3,256]{2,0,1:T(4,128)(2,1)S(1)} %bitcast.56), channel_id=1, replica_groups=mesh['dp'=8,'tensor'=4] {'dp'}, use_global_device_ids=true, to_apply=%region_12.13 | all-reduce | flops 3072 | bytes 12288 | tf_op jit(solution)/shard_map/psum | solution.py:378
  510.1 0.6 reshape.100
  510.7 3.3 convert_element_type.116
  514.0 3.4 copy.34
  517.4 62.7 %all-reduce.7.cloned.1.call-done = (bf16[1024,896]{1,0:T(8,128)(2,1)}, bf16[256,1024]{1,0:T(8,128)(2,1)}) async-done(((bf16[1024,896]{1,0:T(8,128)(2,1)}, bf16[256,1024]{1,0:T(8,128)(2,1)}), (bf16[1024,896]{1,0:T(8,128)(2,1)}, bf16[256,1024]{1,0:T(8,128)(2,1)})) %all-reduce.7.cloned.1.call-update) | async-done | bytes 2359312 | tf_op jit(solution)/shard_map/psum | solution.py:378
  580.1 2.3 convert_element_type.115
  582.4 1.0 slice_convert_fusion.1
  583.3 0.8 copy.36
  584.1 1.9 slice_convert_fusion
  586.0 4.2 copy.33
  590.2 3.9 copy.35
  594.1 32.1 %reduce-scatter.8.cloned.1.call-done = bf16[512,1024]{1,0:T(8,128)(2,1)} async-done(((bf16[2048,1024]{1,0:T(8,128)(2,1)}), bf16[512,1024]{1,0:T(8,128)(2,1)}) %reduce-scatter.8.cloned.1.call-update) | async-done | bytes 1048592 | tf_op jit(solution)/shard_map/reduce_scatter | solution.py:319
  626.2 2.2 fusion.9
  628.4 39.8 %all-reduce.1 = (f32[1024]{0:T(1024)}, f32[128]{0:T(128)}, f32[1024]{0:T(1024)}) all-reduce(f32[1024]{0:T(1024)S(1)} %get-tuple-element.59, f32[128]{0:T(128)S(1)} %bitcast.58, f32[1024]{0:T(1024)S(1)} %get-tuple-element.57), channel_id=1, replica_groups=mesh['dp'=8,'tensor'=4] {'dp','tensor'}, use_global_device_ids=true, to_apply=%region_8.9 | all-reduce | flops 2176 | bytes 17408 | tf_op jit(solution)/shard_map/psum | solution.py:379
  668.2 5.8 reduce-scatter.4.cloned.1.call-done
  674.0 4.9 fusion.11
  (73 shorter events, 0.5 us)
Async XLA Ops:
  7.2 156.1 %copy-start = (bf16[1024,2,704]{0,2,1:T(8,128)(2,1)S(1)}, bf16[1024,2,704]{0,2,1:T(8,128)(2,1)}, u32[]{:S(2)}) copy-start(bf16[1024,2,704]{0,2,1:T(8,128)(2,1)} %param.21) | copy-start | bytes 8650756
  7.2 5.7 copy-start.18
  7.2 42.3 %all-gather.6.cloned.1.call-start = ((), (), s32[]{:S(2)}) async-start(), calls=%async_computation.5 | async-start | bytes 5242880 | tf_op jit(solution)/shard_map/all_gather | solution.py:315
  12.1 3.4 copy-start.24
  12.1 37.4 %copy-start.23 = (bf16[1024,2]{0,1:T(2,128)(2,1)S(1)}, bf16[1024,2]{0,1:T(2,128)(2,1)}, u32[]{:S(2)}) copy-start(bf16[1024,2]{0,1:T(2,128)(2,1)} %param.16) | copy-start | bytes 12292
  12.1 96.4 %all-gather.8.cloned.1.call-start = ((), (), s32[]{:S(2)}) async-start(), calls=%async_computation.6 | async-start | bytes 2621440 | tf_op jit(solution)/shard_map/all_gather | solution.py:315
  12.9 46.8 %copy-start.7 = (f32[4,768]{1,0:T(4,128)}, f32[4,768]{1,0:T(4,128)S(1)}, u32[]{:S(2)}) copy-start(f32[4,768]{1,0:T(4,128)S(1)} %convert.5.conv_ref) | copy-start | bytes 36868
  15.5 44.2 %copy-start.9 = (f32[1,128]{1,0:T(1,128)}, f32[1,128]{1,0:T(1,128)S(1)}, u32[]{:S(2)}) copy-start(f32[1,128]{1,0:T(1,128)S(1)} %bitcast_convert_fusion.gain_ref) | copy-start | bytes 1540
  49.5 10.3 %copy-start.8 = (s32[1,2]{1,0:T(1,128)S(1)}, s32[1,2]{1,0:T(1,128)}, u32[]{:S(2)}) copy-start(s32[1,2]{1,0:T(1,128)} %param.13) | copy-start | bytes 28
  97.1 1.3 copy-start.2
  98.4 1.0 copy-start.3
  99.4 1.0 copy-start.4
  100.4 1.0 copy-start.5
  101.4 7.1 %copy-start.19 = (bf16[1024]{0:T(1024)(128)(2,1)S(1)}, bf16[1024]{0:T(1024)(128)(2,1)}, u32[]{:S(2)}) copy-start(bf16[1024]{0:T(1024)(128)(2,1)} %param.20) | copy-start | bytes 6148
  103.7 18.8 %all-to-all-start = ((bf16[4,512,256]{1,2,0:T(8,128)(2,1)}), bf16[4,512,256]{1,2,0:T(8,128)(2,1)}, u32[]{:S(2)}, u32[]{:S(2)}) async-start(bf16[4,512,256]{1,2,0:T(8,128)(2,1)} %copy.31), calls=%async_computation | async-start | bytes 2097152 | tf_op jit(solution)/shard_map/all_to_all | solution.py:342
  108.0 55.3 %all-gather.10.cloned.1.call-start = ((), (), s32[]{:S(2)}) async-start(), calls=%async_computation.7 | async-start | bytes 5242880 | tf_op jit(solution)/shard_map/all_gather | solution.py:315
  126.0 1.3 copy-start.10
  128.6 70.6 %all-gather.12.cloned.1.call-start = ((), (), s32[]{:S(2)}) async-start(), calls=%async_computation.9 | async-start | bytes 5242880 | tf_op jit(solution)/shard_map/all_gather | solution.py:315
  129.1 136.7 %reduce-scatter.6.cloned.1.call-start = ((), (), s32[]{:S(2)}) async-start(), calls=%async_computation.10 | async-start | bytes 5242880 | tf_op jit(solution)/shard_map/reduce_scatter | solution.py:319
  210.3 1.6 copy-start.26
  210.3 2.5 copy-start.28
  221.1 1.8 copy-start.25
  221.2 208.8 %all-reduce.9.cloned.1.call-start = ((), (), s32[]{:S(2)}) async-start(), calls=%async_computation.14 | async-start | bytes 8650752 | tf_op jit(solution)/shard_map/psum | solution.py:364
  222.9 6.6 copy-start.21
  222.9 6.6 copy-start.27
  222.9 6.6 copy-start.29
  237.6 28.2 %copy-start.11 = (f32[512,1024]{1,0:T(8,128)S(1)}, f32[512,1024]{1,0:T(8,128)}, u32[]{:S(2)}) copy-start(f32[512,1024]{1,0:T(8,128)} %copy-done.10) | copy-start | bytes 6291460
  237.6 228.1 %all-gather.14.cloned.1.call-start = ((), (), s32[]{:S(2)}) async-start(), calls=%async_computation.12 | async-start | bytes 5242880 | tf_op jit(solution)/shard_map/all_gather | solution.py:315
  265.8 2.0 copy-start.13
  270.7 309.4 %all-reduce.7.cloned.1.call-start = ((), (), s32[]{:S(2)}) async-start(), calls=%async_computation.13 | async-start | bytes 4718592 | tf_op jit(solution)/shard_map/psum | solution.py:378
  430.0 35.8 %copy-start.6 = (bf16[2048,256]{1,0:T(8,128)(2,1)S(1)}, bf16[2048,256]{1,0:T(8,128)(2,1)}, u32[]{:S(2)}) copy-start(bf16[2048,256]{1,0:T(8,128)(2,1)} %copy-done.5) | copy-start | bytes 3145732
  439.2 30.9 %copy-start.16 = (bf16[1024,3,256]{0,2,1:T(8,128)(2,1)S(1)}, bf16[1024,3,256]{0,2,1:T(8,128)(2,1)}, u32[]{:S(2)}) copy-start(bf16[1024,3,256]{0,2,1:T(8,128)(2,1)} %copy.30) | copy-start | bytes 4718596
  470.0 156.2 %reduce-scatter.8.cloned.1.call-start = ((), (), s32[]{:S(2)}) async-start(), calls=%async_computation.11 | async-start | bytes 5242880 | tf_op jit(solution)/shard_map/reduce_scatter | solution.py:319
  478.3 1.4 copy-start.22
  478.3 195.7 %reduce-scatter.4.cloned.1.call-start = ((), (), s32[]{:S(2)}) async-start(), calls=%async_computation.8 | async-start | bytes 5242880 | tf_op jit(solution)/shard_map/reduce_scatter | solution.py:319
  486.6 0.7 copy-start.17
  486.7 27.3 %copy-start.14 = (bf16[1024,1408]{1,0:T(8,128)(2,1)S(1)}, bf16[1024,1408]{1,0:T(8,128)(2,1)}, u32[]{:S(2)}) copy-start(bf16[1024,1408]{1,0:T(8,128)(2,1)} %get-tuple-element.33) | copy-start | bytes 8650756
  580.1 4.0 copy-start.15
  590.2 36.0 %copy-start.12 = (bf16[512,1024]{1,0:T(8,128)(2,1)S(1)}, bf16[512,1024]{1,0:T(8,128)(2,1)}, u32[]{:S(2)}) copy-start(bf16[512,1024]{1,0:T(8,128)(2,1)} %param.12) | copy-start | bytes 3145732
  590.2 38.2 %copy-start.20 = (f32[1,128]{1,0:T(1,128)S(1)}, f32[1,128]{1,0:T(1,128)}, u32[]{:S(2)}) copy-start(f32[1,128]{1,0:T(1,128)} %get-tuple-element.32) | copy-start | bytes 1540
  668.2 10.7 %copy-start.1 = (bf16[1024,2,704]{0,2,1:T(8,128)(2,1)S(1)}, bf16[1024,2,704]{0,2,1:T(8,128)(2,1)}, u32[]{:S(2)}) copy-start(bf16[1024,2,704]{0,2,1:T(8,128)(2,1)} %param.21) | copy-start | bytes 8650756
Sparse Core Ops, SparseCore 0:
  12.3 37.1 all-gather.5
  51.0 22.5 all-gather.7
  128.7 34.5 all-gather.9
  164.7 34.4 all-gather.11
  221.3 44.4 reduce-scatter.5
  270.4 159.5 all-reduce.8
  432.2 33.4 all-gather.13
  470.3 109.7 all-reduce.6
  582.6 43.5 reduce-scatter.7
  628.7 45.2 reduce-scatter.3

commit v2 on v1

--- a/solution.py
+++ b/solution.py
@@ -306,6 +306,198 @@
     )(first, proj, proj, conv, gain, dheaded, mixed, st, res, wu, inv)
 
 
+MESH_ID = pl.DeviceIdType.MESH
+HALF = 2
+
+
+def places():
+    d = lax.axis_index("dp")
+    t = lax.axis_index("tensor")
+    beside = t + 1 - 2 * lax.rem(t, 2)
+    across = lax.rem(t + 2, 4)
+    corner = lax.rem(beside + 2, 4)
+    return d, t, beside, across, corner
+
+
+def push(src, dst, send, recv, device):
+    copy = pltpu.make_async_remote_copy(src_ref=src, dst_ref=dst, send_sem=send, recv_sem=recv, device_id=device, device_id_type=MESH_ID)
+    copy.start()
+    return copy
+
+
+def greet(devices):
+    barrier = pltpu.get_barrier_semaphore()
+    for device in devices:
+        pl.semaphore_signal(barrier, inc=1, device_id=device, device_id_type=MESH_ID)
+    pl.semaphore_wait(barrier, len(devices))
+
+
+def row_block(owner, part, owner_rows, part_rows):
+    return pl.ds(pl.multiple_of(owner * owner_rows + part * part_rows, part_rows), part_rows)
+
+
+def mlp_kernel(x_ref, cot_ref, gate_w, up_w, down_w, all_ref, act_ref, dgate_ref, dup_ref, out_ref, sum_ref, mine, to_beside, from_beside, to_across, from_across, to_own, from_own, send, recv):
+    d, t, beside, across, corner = places()
+    rows = x_ref.shape[0]
+    part = rows // HALF
+    greet([(d, beside), (d, across)])
+    copies = []
+    arrive_beside, arrive_across = [], []
+    for s in range(HALF):
+        src = x_ref.at[pl.ds(s * part, part)]
+        dst = all_ref.at[row_block(t, s, rows, part)]
+        arrive_across.append(push(src, dst, send.at[0, s], recv.at[0, s], (d, across)))
+        arrive_beside.append(push(src, dst, send.at[1, s], recv.at[1, s], (d, beside)))
+    all_ref[pl.ds(pl.multiple_of(t * rows, rows), rows), :] = x_ref[...]
+    copies += arrive_across + arrive_beside
+
+    def work(owner, s):
+        at = row_block(owner, s, rows, part)
+        x = all_ref[at, :]
+        gate = lax.dot_general(x, gate_w[...], NN, preferred_element_type=f32)
+        up = lax.dot_general(x, up_w[...], NN, preferred_element_type=f32)
+        sig = jax.nn.sigmoid(gate)
+        silu = gate * sig
+        act = (silu * up).astype(bf16)
+        act_ref[at, :] = act
+        d_act = lax.dot_general(cot_ref[at, :], down_w[...], NT, preferred_element_type=f32)
+        d_gate = (d_act * up * sig * (1.0 + gate * (1.0 - sig))).astype(bf16)
+        d_up = (d_act * silu).astype(bf16)
+        dgate_ref[at, :] = d_gate
+        dup_ref[at, :] = d_up
+        out_ref[at, :] = lax.dot_general(act, down_w[...], NN, preferred_element_type=f32).astype(bf16)
+        return lax.dot_general(d_gate, gate_w[...], NT, preferred_element_type=f32) + lax.dot_general(d_up, up_w[...], NT, preferred_element_type=f32)
+
+    for s in range(HALF):
+        mine[pl.ds(s * part, part), :] = work(t, s)
+    own_copies = []
+    for s in range(HALF):
+        arrive_beside[s].wait_recv()
+        at = pl.ds(s * part, part)
+        to_own[at, :] = work(beside, s).astype(bf16)
+        own_copies.append(push(to_own.at[at], from_own.at[at], send.at[2, s], recv.at[2, s], (d, beside)))
+    passed, sums = [], []
+    for s in range(HALF):
+        at = pl.ds(s * part, part)
+        arrive_across[s].wait_recv()
+        block = all_ref.at[row_block(across, s, rows, part)]
+        passed.append(push(block, block, send.at[3, s], recv.at[3, s], (d, beside)))
+        passed[s].wait_recv()
+        to_beside[at, :] = work(corner, s).astype(bf16)
+        handed = push(to_beside.at[at], from_beside.at[at], send.at[4, s], recv.at[4, s], (d, beside))
+        total = work(across, s)
+        handed.wait_recv()
+        to_across[at, :] = (total + from_beside[at, :].astype(f32)).astype(bf16)
+        sums.append(push(to_across.at[at], from_across.at[at], send.at[5, s], recv.at[5, s], (d, across)))
+        copies.append(handed)
+    for s in range(HALF):
+        at = pl.ds(s * part, part)
+        own_copies[s].wait_recv()
+        sums[s].wait_recv()
+        sum_ref[at, :] = mine[at, :] + from_own[at, :].astype(f32) + from_across[at, :].astype(f32)
+    for copy in copies + own_copies + passed + sums:
+        copy.wait_send()
+
+
+def mlp(x, cot, gate_w, up_w, down_w):
+    rows, width = x.shape
+    total = cot.shape[0]
+    units = gate_w.shape[1]
+    vmem = pl.BlockSpec(memory_space=pltpu.VMEM)
+    half = lambda: pltpu.VMEM((rows, width), bf16)
+    return pl.pallas_call(
+        mlp_kernel,
+        in_specs=[vmem] * 5,
+        out_specs=[vmem] * 6,
+        out_shape=[jax.ShapeDtypeStruct((total, width), bf16), jax.ShapeDtypeStruct((total, units), bf16), jax.ShapeDtypeStruct((total, units), bf16),
+                   jax.ShapeDtypeStruct((total, units), bf16), jax.ShapeDtypeStruct((total, width), bf16), jax.ShapeDtypeStruct((rows, width), f32)],
+        scratch_shapes=[pltpu.VMEM((rows, width), f32), half(), half(), half(), half(), half(), half(),
+                        pltpu.SemaphoreType.DMA((6, HALF)), pltpu.SemaphoreType.DMA((6, HALF))],
+        compiler_params=pltpu.CompilerParams(collective_id=1, has_side_effects=True, vmem_limit_bytes=60 * 2**20),
+    )(x, cot, gate_w, up_w, down_w)
+
+
+def final_kernel(n_dp, dcat_ref, w_ref, tok_ref, dhid_ref, gain_ref, small_ref, dx_ref, small_out, mine, to_beside, from_beside, to_across, from_across, to_own, from_own,
+                 group_send, group_land, all_send, all_land, gain_acc, send, recv, send_g, recv_g, send_a, recv_a):
+    d, t, beside, across, corner = places()
+    rows = tok_ref.shape[0]
+    part = rows // HALF
+    others = [lax.rem(d + k, n_dp) for k in range(1, n_dp)]
+    greet([(d, beside), (d, across), (d, corner)] + [(o, t) for o in others])
+
+    def work(owner, s):
+        return lax.dot_general(dcat_ref[row_block(owner, s, rows, part), :], w_ref[...], NT, preferred_element_type=f32)
+
+    handed, sums, owns = [], [], []
+    for s in range(HALF):
+        at = pl.ds(s * part, part)
+        to_beside[at, :] = work(corner, s).astype(bf16)
+        handed.append(push(to_beside.at[at], from_beside.at[at], send.at[0, s], recv.at[0, s], (d, beside)))
+        total = work(across, s)
+        handed[s].wait_recv()
+        to_across[at, :] = (total + from_beside[at, :].astype(f32)).astype(bf16)
+        sums.append(push(to_across.at[at], from_across.at[at], send.at[1, s], recv.at[1, s], (d, across)))
+    for s in range(HALF):
+        at = pl.ds(s * part, part)
+        to_own[at, :] = work(beside, s).astype(bf16)
+        owns.append(push(to_own.at[at], from_own.at[at], send.at[2, s], recv.at[2, s], (d, beside)))
+        mine[at, :] = work(t, s)
+    gain_acc[...] = jnp.zeros_like(gain_acc)
+    gain = gain_ref[...]
+    piece = 64
+    for s in range(HALF):
+        owns[s].wait_recv()
+        sums[s].wait_recv()
+
+        def finish(i, carry, s=s):
+            at = pl.ds(pl.multiple_of(s * part + i * piece, piece), piece)
+            grad = mine[at, :] + from_own[at, :].astype(f32) + from_across[at, :].astype(f32)
+            tok = tok_ref[at, :].astype(f32)
+            r = lax.rsqrt(jnp.mean(tok * tok, axis=-1, keepdims=True) + 1e-5)
+            scaled = gain * grad
+            dx_ref[at, :] = dhid_ref[at, :] + r * scaled - tok * (r * r * r * jnp.mean(tok * scaled, axis=-1, keepdims=True))
+            gain_acc[...] += jnp.sum((grad * tok * r).reshape(piece // 8, 8, grad.shape[1]), axis=0)
+            return carry
+
+        lax.fori_loop(0, part // piece, finish, 0)
+    line = lax.broadcasted_iota(jnp.int32, small_ref.shape, 0)
+    small = jnp.where(line == 0, jnp.sum(gain_acc[...], axis=0, keepdims=True), small_ref[...])
+    group_send[...] = small
+    grouped = [push(group_send, group_land.at[i], send_g.at[i], recv_g.at[i], (d, peer)) for i, peer in enumerate((beside, across, corner))]
+    for copy in grouped:
+        copy.wait_recv()
+    both = small + group_land[0]
+    both = both + (group_land[1] + group_land[2])
+    small = jnp.where(line < 3, both, small)
+    all_send[...] = small
+    spread = [push(all_send, all_land.at[i], send_a.at[i], recv_a.at[i], (o, t)) for i, o in enumerate(others)]
+    for i, copy in enumerate(spread):
+        copy.wait_recv()
+        small = small + all_land[i]
+    small_out[...] = small
+    for copy in handed + sums + owns + grouped + spread:
+        copy.wait_send()
+
+
+def final(n_dp, dcat, w, tokens, dhid, gain, small):
+    rows, width = tokens.shape
+    vmem = pl.BlockSpec(memory_space=pltpu.VMEM)
+    half = lambda: pltpu.VMEM((rows, width), bf16)
+    line = small.shape
+    dma = pltpu.SemaphoreType.DMA
+    return pl.pallas_call(
+        functools.partial(final_kernel, n_dp),
+        in_specs=[vmem] * 6,
+        out_specs=[vmem] * 2,
+        out_shape=[jax.ShapeDtypeStruct((rows, width), f32), jax.ShapeDtypeStruct(line, f32)],
+        scratch_shapes=[pltpu.VMEM((rows, width), f32), half(), half(), half(), half(), half(), half(),
+                        pltpu.VMEM(line, f32), pltpu.VMEM((3,) + line, f32), pltpu.VMEM(line, f32), pltpu.VMEM((n_dp - 1,) + line, f32), pltpu.VMEM((8, width), f32),
+                        dma((3, HALF)), dma((3, HALF)), dma((3,)), dma((3,)), dma((n_dp - 1,)), dma((n_dp - 1,))],
+        compiler_params=pltpu.CompilerParams(collective_id=2, has_side_effects=True, vmem_limit_bytes=48 * 2**20),
+        cost_estimate=pl.CostEstimate(flops=2 * dcat.shape[0] * dcat.shape[1] * width, bytes_accessed=12 * 2**20, transcendentals=0),
+    )(dcat, w, tokens, dhid, gain, small)
+
+
 def rms_norm(values, scales):
     inverse = lax.rsqrt(jnp.mean(values * values, axis=-1, keepdims=True) + 1e-05)
     return values * inverse * scales
@@ -313,10 +505,6 @@
 
 def gather(x):
     return lax.all_gather(x, "tensor", axis=0, tiled=True)
-
-
-def scatter_sum(x):
-    return lax.psum_scatter(x, "tensor", scatter_dimension=0, tiled=True)
 
 
 def dot(a, b, dims=NN):
@@ -334,60 +522,50 @@
     head_scale = head_gain.astype(f32)[None]
     conv = conv_weight.reshape(conv_weight.shape[0], -1).astype(f32)
     qkv_matrix = jnp.concatenate([qkv_weight.reshape(model_width, -1), jnp.pad(beta_weight, ((0, 0), (0, HEAD - heads)))], axis=1)
-    out_all = gather(out_weight)
     attn_in = rms_norm(local_in, first_scale).astype(bf16)
     attn_all = gather(attn_in)
+    out_all = gather(out_weight)
+    cot_all = gather(cotangent)
     proj = dot(attn_all, qkv_matrix)
     headed, *saved = mixer_fwd(first, proj, conv, head_scale)
     headed_rows = lax.all_to_all(headed, "tensor", split_axis=0, concat_axis=1, tiled=True)
     hidden_res = local_in + dot(headed_rows, out_all)
     mlp_in = rms_norm(hidden_res, second_scale).astype(bf16)
-    mlp_all = gather(mlp_in)
-    cot_all = gather(cotangent)
-    gate_up_matrix = gate_up_weight.reshape(model_width, -1)
-    gate_up = dot(mlp_all, gate_up_matrix)
-    hidden_units = gate_up.shape[1] // 2
-    gate_pre = gate_up[:, :hidden_units]
-    up_pre = gate_up[:, hidden_units:]
-    sigmoid_gate = jax.nn.sigmoid(gate_pre)
-    silu_gate = gate_pre * sigmoid_gate
-    activated = (silu_gate * up_pre).astype(bf16)
-    d_activated = dot(cot_all, down_weight, NT)
-    d_gate = (d_activated * up_pre * sigmoid_gate * (1.0 + gate_pre * (1.0 - sigmoid_gate))).astype(bf16)
-    d_up = (d_activated * silu_gate).astype(bf16)
-    d_gate_up = jnp.concatenate([d_gate, d_up], axis=1)
-    d_mlp_in = scatter_sum(dot(d_gate_up, gate_up_matrix, NT).astype(bf16)).astype(f32)
-    mlp_out = scatter_sum(dot(activated, down_weight).astype(bf16)).astype(f32)
-    output = (hidden_res + mlp_out).astype(bf16)
-    down_part = dot(activated, cot_all, TN).astype(bf16)
-    gate_up_part = dot(mlp_all, d_gate_up, TN).astype(bf16)
-    gate_up_sum, down_sum = lax.psum((gate_up_part, down_part), "dp")
+    gate_w, up_w = gate_up_weight[:, 0], gate_up_weight[:, 1]
+    mlp_all, activated, d_gate, d_up, out_parts, d_mlp_in = mlp(mlp_in, cot_all, gate_w, up_w, down_weight)
     d_from_mlp, mlp_gain_part = jax.vjp(rms_norm, hidden_res, second_scale)[1](d_mlp_in)
     d_hidden = cotangent.astype(f32) + d_from_mlp
-    d_attn = d_hidden.astype(bf16)
-    d_headed_rows = dot(d_attn, out_all, NT).astype(bf16)
-    d_headed = lax.all_to_all(d_headed_rows, "tensor", split_axis=1, concat_axis=0, tiled=True)
-    d_attn_all = gather(d_attn)
+    d_attn_all = gather(d_hidden.astype(bf16))
+    down_part = dot(activated, cot_all, TN).astype(bf16)
+    gate_part = dot(mlp_all, d_gate, TN).astype(bf16)
+    up_part = dot(mlp_all, d_up, TN).astype(bf16)
+    d_attn_all, gate_part, up_part, down_part, out_parts = lax.optimization_barrier((d_attn_all, gate_part, up_part, down_part, out_parts))
+    gate_sum, up_sum, down_sum = lax.psum((gate_part, up_part, down_part), "dp")
+    d_headed = dot(d_attn_all, out_weight, NT).astype(bf16)
     d_cat, conv_part, head_gain_part = mixer_bwd(first, proj, conv, head_scale, d_headed, saved)
-    d_attn_in = scatter_sum(dot(d_cat, qkv_matrix, NT).astype(bf16)).astype(f32)
-    d_from_attn, attn_gain_part = jax.vjp(rms_norm, local_in, first_scale)[1](d_attn_in)
-    input_grad = d_hidden + d_from_attn
-    d_cat, gate_up_sum, down_sum = lax.optimization_barrier((d_cat, gate_up_sum, down_sum))
     cat_part = dot(attn_all, d_cat, TN).astype(bf16)
     out_part = dot(headed, d_attn_all, TN).astype(bf16)
-    cat_sum, out_sum, conv_sum = lax.psum((cat_part, out_part, conv_part.astype(bf16)), "dp")
-    attn_gain_grad, head_gain_grad, mlp_gain_grad = lax.psum((attn_gain_part, head_gain_part[0], mlp_gain_part), ("dp", "tensor"))
+    out_parts = lax.optimization_barrier((out_parts, d_cat))[0]
+    mlp_out = lax.psum_scatter(out_parts, "tensor", scatter_dimension=0, tiled=True).astype(f32)
+    output = (hidden_res + mlp_out).astype(bf16)
+    cat_part, out_part, gate_sum, up_sum, down_sum = lax.optimization_barrier((cat_part, out_part, gate_sum, up_sum, down_sum))
+    cat_sum, out_sum = lax.psum((cat_part, out_part), "dp")
+    small = jnp.concatenate([
+        jnp.zeros((1, model_width), f32), mlp_gain_part[None], jnp.pad(head_gain_part, ((0, 0), (0, model_width - HEAD))),
+        conv_part.reshape(-1, model_width), jnp.zeros((5 - conv_part.size // model_width, model_width), f32)], axis=0)
+    input_grad, small = final(lax.axis_size("dp"), d_cat, qkv_matrix, tokens, d_hidden, first_scale[None], small)
+    conv_lines = conv_part.size // model_width
     return (
         output,
         input_grad,
-        attn_gain_grad,
+        small[0],
         cat_sum[:, :width].astype(f32).reshape(qkv_weight.shape),
         cat_sum[:, width:width + heads].astype(f32),
-        conv_sum.astype(f32).reshape(conv_weight.shape),
-        head_gain_grad,
+        small[3:3 + conv_lines].reshape(conv_weight.shape),
+        small[2, :HEAD],
         out_sum.astype(f32),
-        mlp_gain_grad,
-        gate_up_sum.astype(f32).reshape(gate_up_weight.shape),
+        small[1],
+        jnp.stack([gate_sum, up_sum], axis=1).astype(f32),
         down_sum.astype(f32),
     )
 

time: 695 us -> 571 us (0.82)
  waiting for transfers between devices: 363 us -> 255 us
  Pallas kernels: 75.7 us -> 180 us
  blocking collectives: 80.3 us -> 0 us
  matrix products: 91 us -> 43.4 us
    pallas_call x0 -> x2, Pallas kernels: none -> 103 us  [the longest x1 58.7 us: mlp(): pl.pallas_call(mlp_kernel, in_specs=[vmem] * 5, out_specs=[vmem] * 6, out...]
    all_gather x5 -> x4, waiting for transfers between devices: 119 us -> 50.4 us  [gather(): return lax.all_gather(x, 'tensor', axis=0, tiled=True)]
    psum x2 -> x0, blocking collectives: 62.5 us -> none  [the longest x1 39.8 us: on_device(): lax.psum((attn_gain_part, head_gain_part[0], mlp_gain_part), ('dp', 'tens...]
    dot_general x12 -> x8, matrix products: 91 us -> 43.4 us  [dot(): return lax.dot_general(a, b, dims, preferred_element_type=f32)]
    reduce_scatter x3 -> x1, waiting for transfers between devices: 66 us -> 31.6 us  [on_device(): lax.psum_scatter(out_parts, 'tensor', scatter_dimension=0, tiled=True)]
    all_to_all x1 -> x0, blocking collectives: 17.8 us -> none  [on_device(): lax.all_to_all(d_headed_rows, 'tensor', split_axis=1, concat_axis=0, tile...]
    all_to_all x1, waiting for transfers between devices: 14 us -> 6.25 us  [on_device(): lax.all_to_all(headed, 'tensor', split_axis=0, concat_axis=1, tiled=True)]
    convert_element_type x2 -> x3, other arithmetic: 2.84 us -> 9.91 us  [the longest x1 3.83 us: on_device(): d_attn_all = gather(d_hidden.astype(bf16))]
  transfers between devices with their start and end apart: 11 -> 8, of which waited for: 10 -> 6; matrix products, arithmetic and copies ran while one was open for 14% -> 15% of each run, Pallas kernels for 11% -> 22%
where the time goes in v2:
time: 571 us; the launch traced here: 562 us
  waiting for transfers between devices  255 us (45%)
  Pallas kernels  180 us (32%)
  matrix products  43.4 us (8%)
  local copies, waits for them, and re-layouts  32.4 us (6%)
  other arithmetic  31.7 us (6%)
  between operations  14.9 us (3%)
    psum x1, waiting for transfers between devices, on_device(): gate_sum, up_sum, down_sum = lax.psum((gate_part, up_part, down_part), 'dp')  109 us
    pallas_call x1, Pallas kernels, mlp(): pl.pallas_call(mlp_kernel, in_specs=[vmem] * 5, out_specs=[vmem] * 6, out...  58.7 us
    psum x1, waiting for transfers between devices, on_device(): cat_sum, out_sum = lax.psum((cat_part, out_part), 'dp')  55.9 us
    all_gather x4, waiting for transfers between devices, gather(): return lax.all_gather(x, 'tensor', axis=0, tiled=True)  50.4 us
    pallas_call x1, Pallas kernels, final(): pl.pallas_call(functools.partial(final_kernel, n_dp), in_specs=[vmem] * 6...  44.7 us
    dot_general x8, matrix products, dot(): return lax.dot_general(a, b, dims, preferred_element_type=f32)  43.4 us
    pallas_call x1, Pallas kernels, mixer_bwd(): pl.pallas_call(mixer_bwd_kernel, grid_spec=pltpu.PrefetchScalarGridSpec(n...  38.8 us
    pallas_call x1, Pallas kernels, mixer_fwd(): pl.pallas_call(mixer_fwd_kernel, grid_spec=pltpu.PrefetchScalarGridSpec(n...  37.7 us
  transfers between devices with their start and end apart: 8, of which 6 were waited for; matrix products, arithmetic and copies ran while one was open for 15% of the time, Pallas kernels for 22%

profile of v2, /device:TPU:0, one launch (start us, length us, event | category | flops | bytes accessed | tf_op | source)
XLA Modules:
  0.0 561.8 jit_solution(18224767044111890967)
XLA Ops:
  7.2 0.0 all-gather.5.cloned.1.call-start
  7.2 1.5 fusion.1
  8.7 0.7 convert_element_type.69
  9.4 2.6 fusion.3
  12.1 0.0 all-gather.7.cloned.1.call-start
  12.1 0.7 all-gather.7.cloned.1.call-update
  12.8 0.0 all-gather.9.cloned.1.call-start
  12.9 0.7 all-gather.9.cloned.1.call-update
  13.6 0.2 copy.32
  13.8 1.7 copy.31
  15.6 1.7 copy.33
  17.4 32.0 %all-gather.5.cloned.1.call-done = bf16[2048,1024]{1,0:T(8,128)(2,1)} async-done(((bf16[512,1024]{1,0:T(8,128)(2,1)}), bf16[2048,1024]{1,0:T(8,128)(2,1)}) %all-gather.5.cloned.1.call-update) | async-done | bytes 4194320 | tf_op jit(solution)/shard_map/all_gather | solution.py:507
  49.4 8.7 %fusion.7.proj_ref.prev_ref = f32[2048,896]{1,0:T(8,128)} fusion(bf16[2048,1024]{1,0:T(8,128)(2,1)} %all-gather.5.cloned.1.call-done, bf16[1024,2]{1,0:T(8,128)(2,1)S(1)} %copy.32, bf16[1024,768]{1,0:T(8,128)(2,1)S(1)} %copy.33), kind=kOutput, calls=%fused_computation.31 | convolution fusion | flops 3763601408 | bytes 13111296 | tf_op jit(solution)/shard_map/dot_general | solution.py:511
  58.2 37.7 %shard_map.203 = (bf16[2048,256]{1,0:T(8,128)(2,1)S(1)}, f32[2048,256]{1,0:T(8,128)S(1)}, bf16[16,256,128]{2,1,0:T(8,128)(2,1)S(1)}, bf16[16,256,128]{2,1,0:T(8,...) custom-call(s32[1]{0:T(128)S(1)} %bitcast.41, f32[2048,896]{1,0:T(8,128)} %fusion.7.proj_ref.prev_ref, ...), custom_call_target="tpu_custom_call" | custom-call | tf_op jit(solution)/shard_map/pallas_call | solution.py:150
  95.8 1.4 copy-done.1
  97.2 1.0 copy-done.3
  98.2 1.0 copy-done.4
  99.2 1.3 copy.34
  100.5 3.5 all-to-all-start
  104.0 0.0 all-gather.11.cloned.1.call-start
  104.1 3.6 fusion.11
  107.7 2.6 copy.42
  110.3 2.8 copy.41
  113.1 6.2 %all-to-all-done = bf16[4,512,256]{1,2,0:T(8,128)(2,1)S(1)} async-done(((bf16[4,512,256]{1,2,0:T(8,128)(2,1)}), bf16[4,512,256]{1,2,0:T(8,128)(2,1)S(1)}, u32[]{:S(2)}, u32[]{:S(2)}) %all-to-all-start) | async-done | bytes 1048608 | tf_op jit(solution)/shard_map/all_to_all | solution.py:531
  119.4 4.2 multiply_reduce_fusion.2
  123.6 2.8 multiply_convert_fusion.x_ref
  126.4 58.7 %shard_map.204 = (bf16[2048,1024]{1,0:T(8,128)(2,1)}, bf16[2048,704]{1,0:T(8,128)(2,1)}, bf16[2048,704]{1,0:T(8,128)(2,1)}, bf16[2048,704]{1,0:T(8,128)(2,1)}, b...) custom-call(bf16[512,1024]{1,0:T(8,128)(2,1)} %multiply_convert_fusion.x_ref, ...), custom_call_target="tpu_custom_call" | custom-call | tf_op jit(solution)/shard_map/pallas_call | solution.py:408
  185.1 2.9 multiply_reduce_fusion
  188.1 0.2 copy-done.12
  188.2 3.8 fusion.9
  192.1 0.2 all-reduce.9.cloned.1.call-start
  192.3 7.6 %convolution_convert_fusion.4 = bf16[1024,704]{0,1:T(8,128)(2,1)} fusion(bf16[2048,1024]{1,0:T(8,128)(2,1)} %get-tuple-element.41, bf16[2048,704]{1,0:T(8,128)(2,1)} %get-tuple-element.42), kind=kOutput, calls=%fused_computation.21 | convolution fusion | flops 2953510912 | bytes 8519680 | tf_op jit(solution)/shard_map/dot_general | solution.py:511
  199.9 4.4 convolution_convert_fusion.3
  204.3 4.3 convolution_convert_fusion.2
  208.5 18.3 %all-gather.11.cloned.1.call-done = bf16[2048,1024]{1,0:T(8,128)(2,1)} async-done(((bf16[512,1024]{1,0:T(8,128)(2,1)}), bf16[2048,1024]{1,0:T(8,128)(2,1)}) %all-gather.11.cloned.1.call-update) | async-done | bytes 4194320 | tf_op jit(solution)/shard_map/all_gather | solution.py:507
  226.9 0.0 all-reduce.7.cloned.1.call-start
  226.9 1.0 copy-done.16
  227.9 4.5 convolution_convert_fusion.dh_ref
  232.4 38.8 %shard_map.205 = (bf16[2048,896]{1,0:T(8,128)(2,1)}, f32[4,768]{1,0:T(4,128)}, f32[1,128]{1,0:T(1,128)}) custom-call(s32[1]{0:T(128)} %bitcast.40, f32[2048,896]{1,0:T(8,128)} %fusion.7.proj_ref.prev_ref, f32[2048,896]{1,0:T(8,128)} %fusion.7.proj_ref.prev_ref, f32[4,768]{1,0:T(4,128)} %copy-done.5, f32[1,128]{1,0:T(1,128)} %copy-done.7, ...), custom_call_target="tpu_custom_call" | custom-call | tf_op jit(solution)/shard_map/pallas_call | solution.py:291
  271.2 2.1 convolution_convert_fusion.5
  273.2 0.2 copy-done.22
  273.4 7.8 %convolution_convert_fusion.1 = bf16[1024,896]{1,0:T(8,128)(2,1)} fusion(bf16[2048,1024]{1,0:T(8,128)(2,1)S(1)} %copy-done.22, bf16[2048,896]{1,0:T(8,128)(2,1)} %get-tuple-element.53.dcat_ref), kind=kOutput, calls=%fused_computation.18 | convolution fusion | flops 3759013888 | bytes 9699328 | tf_op jit(solution)/shard_map/dot_general | solution.py:511
  281.2 109.4 %all-reduce.9.cloned.1.call-done = (bf16[1024,704]{0,1:T(8,128)(2,1)}, bf16[1024,704]{0,1:T(8,128)(2,1)}, bf16[704,1024]{1,0:T(8,128)(2,1)}) async-done(((bf16[1024,704]{0,1:T(8,128)(2,1)}, bf16[1024,704]{0,1:T(8,128)(2,1)}, bf16[704,1024]{1,0:T(8,128)(2,1)}), (bf16[1024,704]{0,1:T(8,128)(2,1)}, bf16[1024,704]{0,1:T(8,128)(2,1)}, bf16[704,1024]{1,0:T(8,128)(2,1)})) %all-reduce.9.cloned.1.call-update) | async-done | bytes 4325392 | tf_op jit(solution)/shard_map/psum | solution.py:543
  390.7 0.3 reduce-scatter.2.cloned.1.call-start
  391.0 0.4 reduce-scatter.2.cloned.1.call-update
  391.4 0.6 copy-done.10
  392.1 1.4 fusion.5.w_ref
  393.6 1.5 copy-done.2
  395.1 44.7 %shard_map.206 = (f32[512,1024]{1,0:T(8,128)S(1)}, f32[8,1024]{1,0:T(8,128)S(1)}) custom-call(bf16[2048,896]{1,0:T(8,128)(2,1)} %get-tuple-element.53.dcat_ref, bf16[1024,896]{1,0:T(8,128)(2,1)S(1)} %copy-done.2, bf16[512,1024]{1,0:T(8,128)(2,1)S(1)} %copy-done, f32[512,1024]{1,0:T(8,128)} %get-tuple-element.97.dhid_ref, f32[1,1024]{1,0:T(1,128)S(1)} %bitcast.39, ...), custom_call_target="tpu_custom_call" | custom-call | flops 3758096384 | bytes 12582912 | tf_op jit(solution)/shard_map/pallas_call | solution.py:488
  439.8 0.6 copy.40
  440.4 0.5 slice_bitcast_fusion
  440.9 0.6 fusion.12
  441.5 3.5 convert_element_type.88
  445.0 2.9 maximum_convert_fusion
  447.9 55.9 %all-reduce.7.cloned.1.call-done = (bf16[1024,896]{1,0:T(8,128)(2,1)}, bf16[256,1024]{1,0:T(8,128)(2,1)}) async-done(((bf16[1024,896]{1,0:T(8,128)(2,1)}, bf16[256,1024]{1,0:T(8,128)(2,1)}), (bf16[1024,896]{1,0:T(8,128)(2,1)}, bf16[256,1024]{1,0:T(8,128)(2,1)})) %all-reduce.7.cloned.1.call-update) | async-done | bytes 2359312 | tf_op jit(solution)/shard_map/psum | solution.py:552
  503.8 2.1 convert_element_type.86
  505.9 1.0 slice_convert_fusion.1
  506.9 0.8 copy.39
  507.7 3.3 slice_convert_fusion
  511.0 3.8 copy.37
  514.8 3.7 copy.38
  518.5 31.6 %reduce-scatter.2.cloned.1.call-done = bf16[512,1024]{1,0:T(8,128)(2,1)} async-done(((bf16[2048,1024]{1,0:T(8,128)(2,1)}), bf16[512,1024]{1,0:T(8,128)(2,1)}) %reduce-scatter.2.cloned.1.call-update) | async-done | bytes 1048592 | tf_op jit(solution)/shard_map/reduce_scatter | solution.py:549
  550.0 3.2 add_convert_fusion
  553.2 1.3 copy.49
  (67 shorter events, 0.3 us)
Async XLA Ops:
  7.2 42.2 %all-gather.5.cloned.1.call-start = ((), (), s32[]{:S(2)}) async-start(), calls=%async_computation.2 | async-start | bytes 5242880 | tf_op jit(solution)/shard_map/all_gather | solution.py:507
  9.4 4.1 copy-start.18
  9.4 4.2 copy-start.19
  9.4 4.4 copy-start.13
  12.1 101.1 %all-gather.7.cloned.1.call-start = ((), (), s32[]{:S(2)}) async-start(), calls=%async_computation.3 | async-start | bytes 2621440 | tf_op jit(solution)/shard_map/all_gather | solution.py:507
  12.8 113.5 %all-gather.9.cloned.1.call-start = ((), (), s32[]{:S(2)}) async-start(), calls=%async_computation.4 | async-start | bytes 5242880 | tf_op jit(solution)/shard_map/all_gather | solution.py:507
  13.6 44.6 %copy-start.5 = (f32[4,768]{1,0:T(4,128)}, f32[4,768]{1,0:T(4,128)S(1)}, u32[]{:S(2)}) copy-start(f32[4,768]{1,0:T(4,128)S(1)} %convert.3.conv_ref) | copy-start | bytes 36868
  15.6 1.7 copy-start.27
  17.3 40.8 %copy-start.9 = (bf16[1024,768]{1,0:T(8,128)(2,1)}, bf16[1024,768]{1,0:T(8,128)(2,1)S(1)}, u32[]{:S(2)}) copy-start(bf16[1024,768]{1,0:T(8,128)(2,1)S(1)} %copy.33) | copy-start | bytes 4718596
  17.4 40.8 %copy-start.7 = (f32[1,128]{1,0:T(1,128)}, f32[1,128]{1,0:T(1,128)S(1)}, u32[]{:S(2)}) copy-start(f32[1,128]{1,0:T(1,128)S(1)} %bitcast_convert_fusion.gain_ref) | copy-start | bytes 1540
  17.4 40.8 %copy-start.6 = (s32[1,2]{1,0:T(1,128)S(1)}, s32[1,2]{1,0:T(1,128)}, u32[]{:S(2)}) copy-start(s32[1,2]{1,0:T(1,128)} %param.13) | copy-start | bytes 28
  95.8 1.4 copy-start.1
  97.2 1.0 copy-start.3
  98.2 1.0 copy-start.4
  99.2 4.9 copy-start.20
  100.5 18.9 %all-to-all-start = ((bf16[4,512,256]{1,2,0:T(8,128)(2,1)}), bf16[4,512,256]{1,2,0:T(8,128)(2,1)S(1)}, u32[]{:S(2)}, u32[]{:S(2)}) async-start(bf16[4,512,256]{1,2,0:T(8,128)(2,1)} %copy.34), calls=%async_computation | async-start | bytes 2097152 | tf_op jit(solution)/shard_map/all_to_all | solution.py:531
  104.0 122.9 %all-gather.11.cloned.1.call-start = ((), (), s32[]{:S(2)}) async-start(), calls=%async_computation.5 | async-start | bytes 5242880 | tf_op jit(solution)/shard_map/all_gather | solution.py:507
  110.3 9.1 %copy-start = (bf16[512,1024]{1,0:T(8,128)(2,1)S(1)}, bf16[512,1024]{1,0:T(8,128)(2,1)}, u32[]{:S(2)}) copy-start(bf16[512,1024]{1,0:T(8,128)(2,1)} %tok_ref.1) | copy-start | bytes 3145732
  185.1 3.0 copy-start.8
  185.1 3.1 copy-start.12
  192.1 198.6 %all-reduce.9.cloned.1.call-start = ((), (), s32[]{:S(2)}) async-start(), calls=%async_computation.8 | async-start | bytes 8650752 | tf_op jit(solution)/shard_map/psum | solution.py:543
  192.3 7.6 %copy-start.24 = (bf16[2048,1024]{1,0:T(8,128)(2,1)S(1)}, bf16[2048,1024]{1,0:T(8,128)(2,1)}, u32[]{:S(2)}) copy-start(bf16[2048,1024]{1,0:T(8,128)(2,1)} %get-tuple-element.41) | copy-start | bytes 12582916
  192.3 7.6 %copy-start.26 = (bf16[2048,704]{1,0:T(8,128)(2,1)S(1)}, bf16[2048,704]{1,0:T(8,128)(2,1)}, u32[]{:S(2)}) copy-start(bf16[2048,704]{1,0:T(8,128)(2,1)} %get-tuple-element.43) | copy-start | bytes 8650756
  199.9 4.4 copy-start.11
  199.9 4.4 copy-start.25
  226.9 1.0 copy-start.16
  226.9 276.9 %all-reduce.7.cloned.1.call-start = ((), (), s32[]{:S(2)}) async-start(), calls=%async_computation.7 | async-start | bytes 4718592 | tf_op jit(solution)/shard_map/psum | solution.py:552
  232.4 38.8 %copy-start.23 = (bf16[2048,1024]{1,0:T(8,128)(2,1)S(1)}, bf16[2048,1024]{1,0:T(8,128)(2,1)}, u32[]{:S(2)}) copy-start(bf16[2048,1024]{1,0:T(8,128)(2,1)} %all-gather.11.cloned.1.call-done) | copy-start | bytes 12582916
  271.1 2.3 copy-start.22
  390.7 1.4 copy-start.10
  390.7 159.3 %reduce-scatter.2.cloned.1.call-start = ((), (), s32[]{:S(2)}) async-start(), calls=%async_computation.6 | async-start | bytes 5242880 | tf_op jit(solution)/shard_map/reduce_scatter | solution.py:549
  392.1 1.4 copy-start.17
  392.1 1.4 copy-start.21
  393.6 1.5 copy-start.2
  441.5 3.5 copy-start.14
  441.5 3.5 copy-start.15
Sparse Core Ops, SparseCore 0:
  12.2 37.1 all-gather.4
  51.0 22.5 all-gather.6
  75.2 35.5 all-gather.8
  192.2 34.6 all-gather.10
  230.6 159.9 all-reduce.8
  394.7 109.0 all-reduce.6
  506.4 43.5 reduce-scatter.1

commit v3 on v2

v3 whole, which is shorter than its diff:
```python
import functools
import jax
import jax.numpy as jnp
from jax import lax
from jax.experimental import pallas as pl
from jax.experimental.pallas import tpu as pltpu
from jax.sharding import PartitionSpec as P

HEAD = 128
STEP = 128
SPAN = 64
STEPS = 4
ROWS = STEP * STEPS
BACK_STEPS = 2
BACK_ROWS = STEP * BACK_STEPS
RING = 8
ROUNDS = 2 * RING - 2
NN = (((1,), (0,)), ((), ()))
NT = (((1,), (1,)), ((), ()))
TN = (((0,), (0,)), ((), ()))
f32 = jnp.float32
bf16 = jnp.bfloat16


def mm(a, b, dims=NN):
    return lax.dot_general(a.astype(bf16), b.astype(bf16), dims, preferred_element_type=f32)


def split(a):
    high = a.astype(bf16)
    return high, (a - high.astype(f32)).astype(bf16)


def stack(x):
    return jnp.concatenate([x[:, :HEAD], x[:, HEAD:]], axis=0)


def unstack(x):
    return jnp.concatenate([x[:STEP], x[STEP:]], axis=1)


def pair_masks():
    i = lax.broadcasted_iota(jnp.int32, (2 * STEP, 2 * STEP), 0)
    j = lax.broadcasted_iota(jnp.int32, (2 * STEP, 2 * STEP), 1)
    same = (i // STEP) == (j // STEP)
    cross = ((i % STEP) >= SPAN) & ((j % STEP) < SPAN)
    levels = []
    size = 1
    while size < STEP:
        levels.append(((i // (2 * size)) == (j // (2 * size))) & ((i // size) % 2 == 1) & ((j // size) % 2 == 0))
        size *= 2
    return same & (i > j), same & (i >= j), cross, levels, i == j


def tri_inverses(systems, levels, eye):
    invs = [jnp.where(eye, 1.0, jnp.where(levels[0], -a, 0.0)) for a in systems]
    for level in levels[1:]:
        lows = [inv.astype(bf16) for inv in invs]
        parts = [mm(low, jnp.where(level, a, 0.0)) for low, a in zip(lows, systems)]
        parts = [mm(part, low) for part, low in zip(parts, lows)]
        invs = [inv - part for inv, part in zip(invs, parts)]
    return invs


def row_masks(start_reset, mid_reset):
    r = lax.broadcasted_iota(jnp.int32, (2 * STEP, HEAD), 0) % STEP
    upper = r < SPAN
    enter = jnp.where(upper, 1.0 - start_reset, (1.0 - start_reset) * (1.0 - mid_reset))
    leave = jnp.where(upper, 1.0 - mid_reset, 1.0)
    keep = (1.0 - start_reset) * (1.0 - mid_reset)
    return enter, leave, keep


def resets(flags, step):
    return flags[2 * step], flags[2 * step + 1]


def sigmoid(x):
    return 0.5 * jnp.tanh(0.5 * x) + 0.5


def span_masks(flags, span, count):
    row = lax.broadcasted_iota(jnp.int32, (8, HEAD), 0)
    heads, tails = [], []
    for i in range(count):
        heads.append([None] + [jnp.where(row >= j, 1.0, 1.0 - flags[span + i]) for j in range(1, 4)])
        tails.append([None] + [jnp.where(row + j < 8, 1.0, 1.0 - flags[span + i + 1]) for j in range(1, 4)])
    return heads, tails


def conv_column(buf, conv_ref, heads, cs):
    out = []
    for i in range(len(heads)):
        at = 8 + i * SPAN
        total = buf[at:at + SPAN, cs] * conv_ref[0:1, cs]
        for j in range(1, 4):
            lead = buf[at - j:at - j + 8, cs] * heads[i][j]
            rest = buf[at - j + 8:at - j + SPAN, cs]
            total = total + jnp.concatenate([lead, rest], axis=0) * conv_ref[j:j + 1, cs]
        out.append(total)
    return jnp.concatenate(out, axis=0)


def conv_column_back(buf, dbuf, conv_ref, tails, cs):
    out, grads = [], [0.0] * 4
    for i in range(len(tails)):
        at = i * SPAN
        x = buf[8 + at:8 + at + SPAN, cs]
        for j in range(4):
            if j == 0:
                grad = dbuf[at:at + SPAN, cs]
                total = grad * conv_ref[0:1, cs]
            else:
                most = dbuf[at + j:at + j + SPAN - 8, cs]
                last = dbuf[at + j + SPAN - 8:at + j + SPAN, cs] * tails[i][j]
                grad = jnp.concatenate([most, last], axis=0)
                total = total + grad * conv_ref[j:j + 1, cs]
            grads[j] = grads[j] + jnp.sum((x * grad).reshape(SPAN // 8, 8, HEAD), axis=0)
        out.append(total)
    return jnp.concatenate(out, axis=0), grads


def mixer_fwd_kernel(flags, proj_ref, conv_ref, gain_ref, headed_ref, mixed_ref, state_out, res_out, wu_out, inv_out, state, buf):
    g = pl.program_id(0)

    @pl.when(g == 0)
    def _():
        state[...] = jnp.zeros_like(state)
        buf[0:8, :] = jnp.zeros((8, buf.shape[1]), f32)

    width = buf.shape[1]
    buf[8:, :] = proj_ref[:, :width]
    heads, _ = span_masks(flags, g * (ROWS // SPAN), ROWS // SPAN)
    cols = []
    for c in range(width // HEAD):
        total = conv_column(buf, conv_ref, heads, slice(c * HEAD, (c + 1) * HEAD))
        cols.append(total * sigmoid(total))
    buf[0:8, :] = buf[ROWS:ROWS + 8, :]
    betas = sigmoid(proj_ref[:, width:])
    strict, causal, cross, levels, eye = pair_masks()
    todo = []
    for s in range(STEPS):
        rs = slice(s * STEP, (s + 1) * STEP)
        start_reset, mid_reset = resets(flags, g * STEPS + s)
        gate = jnp.where(cross, 1.0 - mid_reset, 1.0)
        two = lambda n: jnp.concatenate([cols[2 * n][rs], cols[2 * n + 1][rs]], axis=0)
        q, k, v = two(0), two(1), two(2)
        q = q * lax.rsqrt(jnp.sum(q * q, axis=-1, keepdims=True) + 1e-6)
        k = k * lax.rsqrt(jnp.sum(k * k, axis=-1, keepdims=True) + 1e-6)
        b = jnp.concatenate([betas[rs, 0:1], betas[rs, 1:2]], axis=0)
        gp = mm(jnp.concatenate([k, q], axis=0), k, NT)
        a = jnp.where(strict, gate * gp[:2 * STEP], 0.0) * b
        p = jnp.where(causal, gate * gp[2 * STEP:], 0.0)
        todo.append((q, k, v, b, a, p, row_masks(start_reset, mid_reset)))
    invs = tri_inverses([x[4] for x in todo], levels, eye)
    wus = [mm(inv, jnp.concatenate([x[3] * x[1], x[3] * x[2]], axis=1)) for inv, x in zip(invs, todo)]
    mem = [state[0], state[1]]
    for s in range(STEPS):
        rs = slice(s * STEP, (s + 1) * STEP)
        q, k, v, b, a, p, (enter, leave, keep) = todo[s]
        wu = wus[s]
        inv_out[s] = invs[s].astype(bf16)
        wu_out[s] = wu.astype(bf16)
        state_out[s, :HEAD] = mem[0].astype(bf16)
        state_out[s, HEAD:] = mem[1].astype(bf16)
        w = wu[:, :HEAD] * enter
        qe = q * enter
        ws, qs = [], []
        for h in range(2):
            hs = slice(h * STEP, (h + 1) * STEP)
            both = mm(jnp.concatenate([w[hs], qe[hs]], axis=0), mem[h])
            ws.append(both[:STEP])
            qs.append(both[STEP:])
        res = wu[:, HEAD:] - jnp.concatenate(ws, axis=0)
        res_out[s] = res.astype(bf16)
        ke = k * leave
        for h in range(2):
            hs = slice(h * STEP, (h + 1) * STEP)
            mem[h] = keep * mem[h] + mm(ke[hs], res[hs], TN)
        o = jnp.concatenate(qs, axis=0) + mm(p, res)
        mixed_ref[rs, :] = unstack(o)
        headed = o * lax.rsqrt(jnp.mean(o * o, axis=-1, keepdims=True) + 1e-5) * gain_ref[...]
        headed_ref[rs, :] = unstack(headed).astype(bf16)
    state[0] = mem[0]
    state[1] = mem[1]


def mixer_fwd(flags, proj, conv, gain):
    rows, total = proj.shape
    width = conv.shape[1]
    n = rows // ROWS
    steps = rows // STEP
    return pl.pallas_call(
        mixer_fwd_kernel,
        grid_spec=pltpu.PrefetchScalarGridSpec(
            num_scalar_prefetch=1, grid=(n,),
            in_specs=[pl.BlockSpec((ROWS, total), lambda g, f: (g, 0)), pl.BlockSpec((4, width), lambda g, f: (0, 0)), pl.BlockSpec((1, HEAD), lambda g, f: (0, 0))],
            out_specs=[pl.BlockSpec((ROWS, 2 * HEAD), lambda g, f: (g, 0)), pl.BlockSpec((ROWS, 2 * HEAD), lambda g, f: (g, 0)),
                       pl.BlockSpec((STEPS, 2 * HEAD, HEAD), lambda g, f: (g, 0, 0)), pl.BlockSpec((STEPS, 2 * STEP, HEAD), lambda g, f: (g, 0, 0)),
                       pl.BlockSpec((STEPS, 2 * STEP, 2 * HEAD), lambda g, f: (g, 0, 0)), pl.BlockSpec((STEPS, 2 * STEP, 2 * STEP), lambda g, f: (g, 0, 0))],
            scratch_shapes=[pltpu.VMEM((2, HEAD, HEAD), f32), pltpu.VMEM((ROWS + 8, width), f32)]),
        out_shape=[jax.ShapeDtypeStruct((rows, 2 * HEAD), bf16), jax.ShapeDtypeStruct((rows, 2 * HEAD), f32),
                   jax.ShapeDtypeStruct((steps, 2 * HEAD, HEAD), bf16), jax.ShapeDtypeStruct((steps, 2 * STEP, HEAD), bf16),
                   jax.ShapeDtypeStruct((steps, 2 * STEP, 2 * HEAD), bf16), jax.ShapeDtypeStruct((steps, 2 * STEP, 2 * STEP), bf16)],
        compiler_params=pltpu.CompilerParams(dimension_semantics=("arbitrary",), vmem_limit_bytes=48 * 2**20),
    )(flags, proj, conv, gain)


MESH_ID = pl.DeviceIdType.MESH
HALF = 2


def places():
    d = lax.axis_index("dp")
    t = lax.axis_index("tensor")
    beside = t + 1 - 2 * lax.rem(t, 2)
    across = lax.rem(t + 2, 4)
    corner = lax.rem(beside + 2, 4)
    return d, t, beside, across, corner


def push(src, dst, send, recv, device):
    copy = pltpu.make_async_remote_copy(src_ref=src, dst_ref=dst, send_sem=send, recv_sem=recv, device_id=device, device_id_type=MESH_ID)
    copy.start()
    return copy


def greet(devices):
    barrier = pltpu.get_barrier_semaphore()
    for device in devices:
        pl.semaphore_signal(barrier, inc=1, device_id=device, device_id_type=MESH_ID)
    pl.semaphore_wait(barrier, len(devices))


def row_block(owner, part, owner_rows, part_rows):
    return pl.ds(pl.multiple_of(owner * owner_rows + part * part_rows, part_rows), part_rows)


def mlp_kernel(x_ref, cot_ref, gate_w, up_w, down_w, all_ref, act_ref, dgate_ref, dup_ref, out_ref, sum_ref, mine, to_beside, from_beside, to_across, from_across, to_own, from_own, send, recv):
    d, t, beside, across, corner = places()
    rows = x_ref.shape[0]
    part = rows // HALF
    greet([(d, beside), (d, across)])
    copies = []
    arrive_beside, arrive_across = [], []
    for s in range(HALF):
        src = x_ref.at[pl.ds(s * part, part)]
        dst = all_ref.at[row_block(t, s, rows, part)]
        arrive_across.append(push(src, dst, send.at[0, s], recv.at[0, s], (d, across)))
        arrive_beside.append(push(src, dst, send.at[1, s], recv.at[1, s], (d, beside)))
    all_ref[pl.ds(pl.multiple_of(t * rows, rows), rows), :] = x_ref[...]
    copies += arrive_across + arrive_beside

    def work(owner, s):
        at = row_block(owner, s, rows, part)
        x = all_ref[at, :]
        gate = lax.dot_general(x, gate_w[...], NN, preferred_element_type=f32)
        up = lax.dot_general(x, up_w[...], NN, preferred_element_type=f32)
        sig = jax.nn.sigmoid(gate)
        silu = gate * sig
        act = (silu * up).astype(bf16)
        act_ref[at, :] = act
        d_act = lax.dot_general(cot_ref[at, :], down_w[...], NT, preferred_element_type=f32)
        d_gate = (d_act * up * sig * (1.0 + gate * (1.0 - sig))).astype(bf16)
        d_up = (d_act * silu).astype(bf16)
        dgate_ref[at, :] = d_gate
        dup_ref[at, :] = d_up
        out_ref[at, :] = lax.dot_general(act, down_w[...], NN, preferred_element_type=f32).astype(bf16)
        return lax.dot_general(d_gate, gate_w[...], NT, preferred_element_type=f32) + lax.dot_general(d_up, up_w[...], NT, preferred_element_type=f32)

    for s in range(HALF):
        mine[pl.ds(s * part, part), :] = work(t, s)
    own_copies = []
    for s in range(HALF):
        arrive_beside[s].wait_recv()
        at = pl.ds(s * part, part)
        to_own[at, :] = work(beside, s).astype(bf16)
        own_copies.append(push(to_own.at[at], from_own.at[at], send.at[2, s], recv.at[2, s], (d, beside)))
    passed, sums = [], []
    for s in range(HALF):
        at = pl.ds(s * part, part)
        arrive_across[s].wait_recv()
        block = all_ref.at[row_block(across, s, rows, part)]
        passed.append(push(block, block, send.at[3, s], recv.at[3, s], (d, beside)))
        passed[s].wait_recv()
        to_beside[at, :] = work(corner, s).astype(bf16)
        handed = push(to_beside.at[at], from_beside.at[at], send.at[4, s], recv.at[4, s], (d, beside))
        total = work(across, s)
        handed.wait_recv()
        to_across[at, :] = (total + from_beside[at, :].astype(f32)).astype(bf16)
        sums.append(push(to_across.at[at], from_across.at[at], send.at[5, s], recv.at[5, s], (d, across)))
        copies.append(handed)
    for s in range(HALF):
        at = pl.ds(s * part, part)
        own_copies[s].wait_recv()
        sums[s].wait_recv()
        sum_ref[at, :] = mine[at, :] + from_own[at, :].astype(f32) + from_across[at, :].astype(f32)
    for copy in copies + own_copies + passed + sums:
        copy.wait_send()


def mlp(x, cot, gate_w, up_w, down_w):
    rows, width = x.shape
    total = cot.shape[0]
    units = gate_w.shape[1]
    vmem = pl.BlockSpec(memory_space=pltpu.VMEM)
    half = lambda: pltpu.VMEM((rows, width), bf16)
    return pl.pallas_call(
        mlp_kernel,
        in_specs=[vmem] * 5,
        out_specs=[vmem] * 6,
        out_shape=[jax.ShapeDtypeStruct((total, width), bf16), jax.ShapeDtypeStruct((total, units), bf16), jax.ShapeDtypeStruct((total, units), bf16),
                   jax.ShapeDtypeStruct((total, units), bf16), jax.ShapeDtypeStruct((total, width), bf16), jax.ShapeDtypeStruct((rows, width), f32)],
        scratch_shapes=[pltpu.VMEM((rows, width), f32), half(), half(), half(), half(), half(), half(),
                        pltpu.SemaphoreType.DMA((6, HALF)), pltpu.SemaphoreType.DMA((6, HALF))],
        compiler_params=pltpu.CompilerParams(collective_id=1, has_side_effects=True, vmem_limit_bytes=60 * 2**20),
    )(x, cot, gate_w, up_w, down_w)


def mixer_bwd_block(blk, width, flags, proj_ref, prev_ref, conv_ref, gain_ref, mixed_ref, state_in, res_in, wu_in, inv_in, dheaded, dcat, dstate, buf, dbuf, cacc, gacc):
    buf[0:8, :] = prev_ref[:, :width]
    buf[8:, :] = proj_ref[:, :width]
    heads, tails = span_masks(flags, blk * (BACK_ROWS // SPAN), BACK_ROWS // SPAN)
    cols, slopes = [], []
    for c in range(width // HEAD):
        total = conv_column(buf, conv_ref, heads, slice(c * HEAD, (c + 1) * HEAD))
        sig = sigmoid(total)
        cols.append(total * sig)
        slopes.append(sig * (1.0 + total * (1.0 - sig)))
    betas = sigmoid(proj_ref[:, width:])
    strict, causal, cross, _, _ = pair_masks()
    lane = lax.broadcasted_iota(jnp.int32, (STEP, HEAD), 1)
    order = list(reversed(range(BACK_STEPS)))
    hs = [slice(h * STEP, (h + 1) * STEP) for h in range(2)]
    spans = [slice(s * STEP, (s + 1) * STEP) for s in range(BACK_STEPS)]
    edge = [resets(flags, blk * BACK_STEPS + s) for s in range(BACK_STEPS)]
    enter, leave, keep = zip(*[row_masks(*e) for e in edge])
    gate = [jnp.where(cross, 1.0 - e[1], 1.0) for e in edge]
    both = lambda n: [jnp.concatenate([cols[2 * n][rs], cols[2 * n + 1][rs]], axis=0) for rs in spans]
    q, k, v = both(0), both(1), both(2)
    rq = [lax.rsqrt(jnp.sum(x * x, axis=-1, keepdims=True) + 1e-6) for x in q]
    rk = [lax.rsqrt(jnp.sum(x * x, axis=-1, keepdims=True) + 1e-6) for x in k]
    q = [x * r for x, r in zip(q, rq)]
    k = [x * r for x, r in zip(k, rk)]
    q16 = [x.astype(bf16) for x in q]
    k16 = [x.astype(bf16) for x in k]
    b = [jnp.concatenate([betas[rs, 0:1], betas[rs, 1:2]], axis=0) for rs in spans]
    gp = [mm(jnp.concatenate([x, y], axis=0), x, NT) for x, y in zip(k16, q16)]
    gram = [jnp.where(strict, m * x[:2 * STEP], 0.0) for m, x in zip(gate, gp)]
    p = [jnp.where(causal, m * x[2 * STEP:], 0.0).astype(bf16) for m, x in zip(gate, gp)]
    do = []
    for s in range(BACK_STEPS):
        o = stack(mixed_ref[spans[s], :])
        dh = stack(dheaded[pl.ds(pl.multiple_of(blk * BACK_ROWS + s * STEP, STEP), STEP), :].astype(f32))
        ro = lax.rsqrt(jnp.mean(o * o, axis=-1, keepdims=True) + 1e-5)
        on = o * ro
        gacc[...] += jnp.sum((dh * on).reshape(2 * STEP // 8, 8, HEAD), axis=0)
        dn = dh * gain_ref[...]
        do.append(ro * (dn - on * jnp.mean(dn * on, axis=-1, keepdims=True)))
    do16 = [x.astype(bf16) for x in do]
    doe = [(x * e).astype(bf16) for x, e in zip(do, enter)]
    ke16 = [(x * e).astype(bf16) for x, e in zip(k, leave)]
    we = [(wu_in[s][:, :HEAD].astype(f32) * enter[s]).astype(bf16) for s in range(BACK_STEPS)]
    dres = [mm(x, y, TN) for x, y in zip(p, do16)]
    qdo = [[mm(x[r], y[r], TN) for r in hs] for x, y in zip(q16, doe)]
    dmem = [dstate[0], dstate[1]]
    dres16, after = [None] * BACK_STEPS, [None] * BACK_STEPS
    for s in order:
        low = [m.astype(bf16) for m in dmem]
        after[s] = low
        dres[s] = dres[s] + jnp.concatenate([mm(ke16[s][hs[h]], low[h]) for h in range(2)], axis=0)
        dres16[s] = dres[s].astype(bf16)
        for h in range(2):
            dmem[h] = keep[s] * dmem[h] + qdo[s][h] - mm(we[s][hs[h]], dres16[s][hs[h]], TN)
    dp = [mm(do16[s], res_in[s], NT) for s in order]
    dke = [jnp.concatenate([mm(res_in[s, hs[h]], after[s][h], NT) for h in range(2)], axis=0) for s in order]
    ds = [[mm(jnp.concatenate([do16[s][hs[h]], dres16[s][hs[h]]], axis=0), state_in[s, h * HEAD:(h + 1) * HEAD], NT) for h in range(2)] for s in order]
    dp = [jnp.where(causal, gate[s] * x, 0.0).astype(bf16) for s, x in zip(order, dp)]
    dw = [-enter[s] * jnp.concatenate([x[0][STEP:], x[1][STEP:]], axis=0) for s, x in zip(order, ds)]
    db_kv = [mm(inv_in[s], jnp.concatenate([x, dres[s]], axis=1), TN) for s, x in zip(order, dw)]
    dq = [enter[s] * jnp.concatenate([x[0][:STEP], x[1][:STEP]], axis=0) + mm(y, k16[s]) for s, x, y in zip(order, ds, dp)]
    dk = [mm(y, q16[s], TN) + leave[s] * x for s, x, y in zip(order, dke, dp)]
    da = [-jnp.where(strict, gate[s] * mm(x, wu_in[s], NT), 0.0) for s, x in zip(order, db_kv)]
    dg = [(x * b[s]).astype(bf16) for s, x in zip(order, da)]
    dk = [x + mm(y, k16[s]) + mm(y, k16[s], TN) + b[s] * z[:, :HEAD] for s, x, y, z in zip(order, dk, dg, db_kv)]
    for i, s in enumerate(order):
        rs = spans[s]
        dbeta = jnp.sum(da[i] * gram[s], axis=-1, keepdims=True) + jnp.sum(db_kv[i][:, :HEAD] * k[s] + db_kv[i][:, HEAD:] * v[s], axis=-1, keepdims=True)
        dv = b[s] * db_kv[i][:, HEAD:]
        dqs = rq[s] * (dq[i] - q[s] * jnp.sum(dq[i] * q[s], axis=-1, keepdims=True))
        dks = rk[s] * (dk[i] - k[s] * jnp.sum(dk[i] * k[s], axis=-1, keepdims=True))
        dpre = dbeta * b[s] * (1.0 - b[s])
        for n, x in enumerate((dqs, dks, dv)):
            for h in range(2):
                c = 2 * n + h
                dbuf[rs, c * HEAD:(c + 1) * HEAD] = x[hs[h]] * slopes[c][rs]
        dcat[pl.ds(pl.multiple_of(blk * BACK_ROWS + s * STEP, STEP), STEP), width:] = jnp.where(lane == 0, dpre[:STEP], jnp.where(lane == 1, dpre[STEP:], 0.0)).astype(bf16)
    dstate[0] = dmem[0]
    dstate[1] = dmem[1]
    for c in range(width // HEAD):
        cs = slice(c * HEAD, (c + 1) * HEAD)
        total, grads = conv_column_back(buf, dbuf, conv_ref, tails, cs)
        dcat[pl.ds(pl.multiple_of(blk * BACK_ROWS, BACK_ROWS), BACK_ROWS), cs] = total.astype(bf16)
        for j in range(4):
            cacc[j, :, cs] += grads[j]
    dbuf[BACK_ROWS:, :] = dbuf[0:8, :]


class Ring:
    def __init__(self, here, after, before, sources, results, lands, by_rows, send, recv):
        self.here, self.targets = here, (after, before)
        self.sources, self.results, self.lands, self.by_rows, self.send, self.recv = sources, results, lands, by_rows, send, recv

    def shard(self, way, k):
        return lax.rem(self.here + (k if way else 2 * RING - k), RING)

    def view(self, ref, i, way, k):
        shard = self.shard(way, k)
        rows, cols = ref.shape
        if self.by_rows[i]:
            piece = rows // (2 * RING)
            return ref.at[pl.ds(pl.multiple_of((2 * shard + way) * piece, piece), piece)]
        piece = cols // RING
        return ref.at[pl.ds(way * (rows // 2), rows // 2), pl.ds(pl.multiple_of(shard * piece, piece), piece)]

    def copy(self, i, way, r):
        if r == 0:
            src, dst = self.view(self.sources[i], i, way, 0), self.lands[i].at[way, 0]
        elif r < RING - 1:
            src, dst = self.lands[i].at[way, r - 1], self.lands[i].at[way, r]
        else:
            src = dst = self.view(self.results[i], i, way, r)
        return pltpu.make_async_remote_copy(src_ref=src, dst_ref=dst, send_sem=self.send.at[i, way], recv_sem=self.recv.at[i, way, r], device_id=self.targets[way], device_id_type=MESH_ID)

    def round(self, r):
        for i in range(len(self.sources)):
            for way in range(2):
                if r > 0:
                    last = self.copy(i, way, r - 1)
                    last.wait_send()
                    last.wait_recv()
                if 0 < r < RING:
                    land = self.lands[i].at[way, r - 1]
                    total = (land[...].astype(f32) + self.view(self.sources[i], i, way, r)[...].astype(f32)).astype(bf16)
                    if r < RING - 1:
                        land[...] = total
                    else:
                        done = self.view(self.results[i], i, way, r)
                        done[...] = total
                if r < ROUNDS:
                    self.copy(i, way, r).start()


def ring_place(d):
    base = d // RING * RING
    inner = lax.rem(d, RING)
    line = inner // 2
    here = jnp.where(lax.rem(inner, 2) == 0, line, RING - 1 - line)

    def device(place):
        return base + jnp.where(place < RING // 2, 2 * place, 2 * (RING - 1 - place) + 1)

    return here, device(lax.rem(here + 1, RING)), device(lax.rem(here + RING - 1, RING))


def ring_lands(shapes, by_rows):
    pieces = [(s[0] // (2 * RING), s[1]) if rows else (s[0] // 2, s[1] // RING) for s, rows in zip(shapes, by_rows)]
    return [pltpu.VMEM((2, RING - 1) + p, bf16) for p in pieces]


def back_kernel(n_dp, flags, proj_ref, prev_ref, conv_ref, gain_ref, mixed_ref, state_in, res_in, wu_in, inv_in,
                headed_hbm, attn_hbm, dattn_hbm, out_w_hbm, w_hbm, tok_hbm, dhid_hbm, first_gain, small_ref, gate_hbm, up_hbm, down_hbm,
                dx_hbm, small_out, gate_out, up_out, down_out, cat_out, outw_out,
                headed, attn, dattn_all, out_w, w, tok, dhid, gate_src, up_src, down_src, cat_src, outw_src,
                gate_res, up_res, down_res, cat_res, outw_res, gate_land, up_land, down_land, cat_land, outw_land,
                dheaded, dcat, dstate, buf, dbuf, cacc, gacc, mine, to_beside, from_beside, to_across, from_across, to_own, from_own,
                group_send, group_land, all_send, all_land, gain_acc,
                load, store, send_m, recv_m, send_c, recv_c, send_x, recv_x, send_g, recv_g, send_a, recv_a):
    g = pl.program_id(0)
    n = pl.num_programs(0)
    d, t, beside, across, corner = places()
    here, after, before = ring_place(d)
    rows = tok.shape[0]
    part = rows // HALF
    width = buf.shape[1]
    others = [d // RING * RING + lax.rem(d + k, RING) for k in range(1, RING)]
    mlp_ring = Ring(here, (after, t), (before, t), [gate_src, up_src, down_src], [gate_res, up_res, down_res], [gate_land, up_land, down_land], [True, True, False], send_m, recv_m)
    cat_ring = Ring(here, (after, t), (before, t), [cat_src, outw_src], [cat_res, outw_res], [cat_land, outw_land], [True, True], send_c, recv_c)
    loads = [(gate_hbm, gate_src), (up_hbm, up_src), (down_hbm, down_src), (dattn_hbm, dattn_all.at[pl.ds(pl.multiple_of(t * rows, rows), rows)]), (out_w_hbm, out_w), (headed_hbm, headed), (attn_hbm, attn), (w_hbm, w), (tok_hbm, tok), (dhid_hbm, dhid)]
    stores = [(gate_res, gate_out), (up_res, up_out), (down_res, down_out), (mine, dx_hbm), (cat_res, cat_out), (outw_res, outw_out)]

    def loaded(i):
        return pltpu.make_async_copy(loads[i][0], loads[i][1], load.at[i])

    def stored(i):
        return pltpu.make_async_copy(stores[i][0], stores[i][1], store.at[i])

    def pushed(src, dst, i, s, peer):
        return pltpu.make_async_remote_copy(src_ref=src, dst_ref=dst, send_sem=send_x.at[i, s], recv_sem=recv_x.at[i, s], device_id=(d, peer), device_id_type=MESH_ID)

    def block_at(owner, s):
        return row_block(owner, s, rows, part)

    def rows_to(i, s, peer):
        block = dattn_all.at[block_at(t, s)]
        return pushed(block, block, i, s, peer)

    def passed(s):
        block = dattn_all.at[block_at(across, s)]
        return pushed(block, block, 2, s, beside)

    def head_grad(owner, s):
        at = block_at(owner, s)
        dheaded[at, :] = lax.dot_general(dattn_all[at, :], out_w[...], NT, preferred_element_type=f32).astype(bf16)

    @pl.when(g == 0)
    def _():
        for i in range(len(loads)):
            loaded(i).start()
        greet([(d, beside), (d, across), (d, corner)] + [(o, t) for o in others])
        for i in range(4):
            loaded(i).wait()
        for s in range(HALF):
            rows_to(0, s, across).start()
            rows_to(1, s, beside).start()
        mlp_ring.round(0)
        loaded(4).wait()
        dstate[...] = jnp.zeros_like(dstate)
        dbuf[BACK_ROWS:, :] = jnp.zeros((8, width), f32)
        cacc[...] = jnp.zeros_like(cacc)
        gacc[...] = jnp.zeros_like(gacc)
        gain_acc[...] = jnp.zeros_like(gain_acc)
        for s in range(HALF):
            head_grad(t, s)
        for s in range(HALF):
            rows_to(1, s, beside).wait_recv()
            head_grad(beside, s)
        mlp_ring.round(1)
        rows_to(0, 0, across).wait_recv()
        passed(0).start()
        head_grad(across, 0)
        mlp_ring.round(2)
        passed(0).wait_recv()
        head_grad(corner, 0)
        mlp_ring.round(3)
        rows_to(0, 1, across).wait_recv()
        passed(1).start()
        head_grad(across, 1)
        passed(1).wait_recv()
        head_grad(corner, 1)
        mlp_ring.round(4)

    for at, r in ((1, 5), (3, 6), (5, 7), (6, 8)):
        @pl.when(g == at)
        def _(r=r):
            mlp_ring.round(r)

    blk = n - 1 - g
    mixer_bwd_block(blk, width, flags, proj_ref, prev_ref, conv_ref, gain_ref, mixed_ref, state_in, res_in, wu_in, inv_in, dheaded, dcat, dstate, buf, dbuf, cacc, gacc)

    def work(owner, s):
        return lax.dot_general(dcat[block_at(owner, s), :], w[...], NT, preferred_element_type=f32)

    def handed(s):
        at = pl.ds(s * part, part)
        return pushed(to_beside.at[at], from_beside.at[at], 3, s, beside)

    def summed(s):
        at = pl.ds(s * part, part)
        return pushed(to_across.at[at], from_across.at[at], 4, s, across)

    def owned(s):
        at = pl.ds(s * part, part)
        return pushed(to_own.at[at], from_own.at[at], 5, s, beside)

    def grouped(i, peer):
        return pltpu.make_async_remote_copy(src_ref=group_send, dst_ref=group_land.at[i], send_sem=send_g.at[i], recv_sem=recv_g.at[i], device_id=(d, peer), device_id_type=MESH_ID)

    def spread(i, o):
        return pltpu.make_async_remote_copy(src_ref=all_send, dst_ref=all_land.at[i], send_sem=send_a.at[i], recv_sem=recv_a.at[i], device_id=(o, t), device_id_type=MESH_ID)

    piece = 64

    def finish(s):
        gain = first_gain[...]

        def chunk(i, carry):
            at = pl.ds(pl.multiple_of(s * part + i * piece, piece), piece)
            grad = mine[at, :] + from_own[at, :].astype(f32) + from_across[at, :].astype(f32)
            x = tok[at, :].astype(f32)
            r = lax.rsqrt(jnp.mean(x * x, axis=-1, keepdims=True) + 1e-5)
            scaled = gain * grad
            mine[at, :] = dhid[at, :] + r * scaled - x * (r * r * r * jnp.mean(x * scaled, axis=-1, keepdims=True))
            gain_acc[...] += jnp.sum((grad * x * r).reshape(piece // 8, 8, grad.shape[1]), axis=0)
            return carry

        lax.fori_loop(0, part // piece, chunk, 0)

    @pl.when(g == n - 1)
    def _():
        for i in range(5, len(loads)):
            loaded(i).wait()
        mlp_ring.round(9)

        def cat_chunk(i):
            at = pl.ds(i * 256, 256)
            cat_src[at, :] = lax.dot_general(attn[:, i * 256:(i + 1) * 256], dcat[...], TN, preferred_element_type=f32).astype(bf16)

        count = attn.shape[1] // 256
        for i in range(count):
            cat_chunk(i)
            if i == count // 2 - 1:
                mlp_ring.round(10)
        outw_src[...] = lax.dot_general(headed[...], dattn_all[...], TN, preferred_element_type=f32).astype(bf16)
        cat_ring.round(0)
        mlp_ring.round(11)
        for s in range(HALF):
            at = pl.ds(s * part, part)
            to_beside[at, :] = work(corner, s).astype(bf16)
            handed(s).start()
            total = work(across, s)
            handed(s).wait_recv()
            to_across[at, :] = (total + from_beside[at, :].astype(f32)).astype(bf16)
            summed(s).start()
        cat_ring.round(1)
        mlp_ring.round(12)
        for s in range(HALF):
            at = pl.ds(s * part, part)
            to_own[at, :] = work(beside, s).astype(bf16)
            owned(s).start()
            mine[at, :] = work(t, s)
        cat_ring.round(2)
        mlp_ring.round(13)
        cat_ring.round(3)
        cat_ring.round(4)
        mlp_ring.round(14)
        for i in range(3):
            stored(i).start()
        cat_ring.round(5)
        owned(0).wait_recv()
        summed(0).wait_recv()
        finish(0)
        cat_ring.round(6)
        cat_ring.round(7)
        owned(1).wait_recv()
        summed(1).wait_recv()
        finish(1)
        stored(3).start()
        cat_ring.round(8)
        line = lax.broadcasted_iota(jnp.int32, small_ref.shape, 0)
        small = jnp.where(line == 0, jnp.sum(gain_acc[...], axis=0, keepdims=True), small_ref[...])
        head_part = jnp.sum(gacc[...], axis=0, keepdims=True)
        small = jnp.where(line == 2, jnp.concatenate([head_part] + [jnp.zeros_like(head_part)] * (small.shape[1] // HEAD - 1), axis=1), small)
        group_send[...] = small
        for j in range(4):
            group_send[3 + j:4 + j, :width] = jnp.sum(cacc[j], axis=0, keepdims=True)
        for i, peer in enumerate((beside, across, corner)):
            grouped(i, peer).start()
        cat_ring.round(9)
        small = group_send[...]
        for i, peer in enumerate((beside, across, corner)):
            grouped(i, peer).wait_recv()
        both = (small + group_land[0]) + (group_land[1] + group_land[2])
        small = jnp.where(line < 3, both, small)
        all_send[...] = small
        for i, o in enumerate(others):
            spread(i, o).start()
        cat_ring.round(10)
        cat_ring.round(11)
        for i, o in enumerate(others):
            spread(i, o).wait_recv()
            small = small + all_land[i]
        small_out[...] = small
        cat_ring.round(12)
        cat_ring.round(13)
        cat_ring.round(14)
        for i in range(4, 6):
            stored(i).start()
        for s in range(HALF):
            for copy in (rows_to(0, s, across), rows_to(1, s, beside), passed(s), handed(s), summed(s), owned(s)):
                copy.wait_send()
        for i, peer in enumerate((beside, across, corner)):
            grouped(i, peer).wait_send()
        for i, o in enumerate(others):
            spread(i, o).wait_send()
        for i in range(len(stores)):
            stored(i).wait()


def backward(n_dp, flags, proj, conv, gain, saved, headed, attn_all, d_attn, out_w, w, tokens, d_hidden, first_gain, small, gate_part, up_part, down_part):
    mixed, states, res, wu, inv = saved
    total_rows, total = proj.shape
    width = conv.shape[1]
    rows, model = tokens.shape
    n = total_rows // BACK_ROWS
    m2 = lambda g: (n - 1 - g, 0)
    m3 = lambda g: (n - 1 - g, 0, 0)
    z2 = lambda g: (0, 0)
    hbm = pl.BlockSpec(memory_space=pl.ANY)
    dma = pltpu.SemaphoreType.DMA
    like = lambda x: pltpu.VMEM(x.shape, x.dtype)
    mlp_parts = (gate_part, up_part, down_part)
    cat_shapes = [(model, total), (headed.shape[1], model)]
    half = lambda: pltpu.VMEM((rows, model), bf16)
    line = small.shape
    out = lambda shape, kind: jax.ShapeDtypeStruct(shape, kind)
    return pl.pallas_call(
        functools.partial(back_kernel, n_dp),
        grid=(n,),
        in_specs=[pl.BlockSpec(memory_space=pltpu.SMEM), pl.BlockSpec((BACK_ROWS, total), m2),
                  pl.BlockSpec((8, total), lambda g: (jnp.maximum((n - 1 - g) * (BACK_ROWS // 8) - 1, 0), 0)),
                  pl.BlockSpec((4, width), z2), pl.BlockSpec((1, HEAD), z2), pl.BlockSpec((BACK_ROWS, 2 * HEAD), m2),
                  pl.BlockSpec((BACK_STEPS, 2 * HEAD, HEAD), m3), pl.BlockSpec((BACK_STEPS, 2 * STEP, HEAD), m3),
                  pl.BlockSpec((BACK_STEPS, 2 * STEP, 2 * HEAD), m3), pl.BlockSpec((BACK_STEPS, 2 * STEP, 2 * STEP), m3)]
        + [hbm] * 7 + [pl.BlockSpec((1, model), z2), pl.BlockSpec(line, z2)] + [hbm] * 3,
        out_specs=[hbm, pl.BlockSpec(line, z2)] + [hbm] * 5,
        out_shape=[out((rows, model), f32), out(line, f32)] + [out(x.shape, bf16) for x in mlp_parts] + [out(s, bf16) for s in cat_shapes],
        scratch_shapes=[like(headed), like(attn_all), like(attn_all), like(out_w), like(w), like(tokens), like(d_hidden)]
        + [like(x) for x in mlp_parts] + [pltpu.VMEM(s, bf16) for s in cat_shapes]
        + [like(x) for x in mlp_parts] + [pltpu.VMEM(s, bf16) for s in cat_shapes]
        + ring_lands([x.shape for x in mlp_parts], [True, True, False]) + ring_lands(cat_shapes, [True, True])
        + [pltpu.VMEM((total_rows, 2 * HEAD), bf16), pltpu.VMEM((total_rows, total), bf16), pltpu.VMEM((2, HEAD, HEAD), f32),
           pltpu.VMEM((BACK_ROWS + 8, width), f32), pltpu.VMEM((BACK_ROWS + 8, width), f32), pltpu.VMEM((4, 8, width), f32), pltpu.VMEM((8, HEAD), f32),
           pltpu.VMEM((rows, model), f32), half(), half(), half(), half(), half(), half(),
           pltpu.VMEM(line, f32), pltpu.VMEM((3,) + line, f32), pltpu.VMEM(line, f32), pltpu.VMEM((RING - 1,) + line, f32), pltpu.VMEM((8, model), f32),
           dma((10,)), dma((6,)), dma((3, 2)), dma((3, 2, ROUNDS)), dma((2, 2)), dma((2, 2, ROUNDS)), dma((6, HALF)), dma((6, HALF)),
           dma((3,)), dma((3,)), dma((RING - 1,)), dma((RING - 1,))],
        compiler_params=pltpu.CompilerParams(dimension_semantics=("arbitrary",), collective_id=2, has_side_effects=True, vmem_limit_bytes=62 * 2**20),
    )(flags, proj, proj, conv, gain, mixed, states, res, wu, inv, headed, attn_all, d_attn, out_w, w, tokens, d_hidden, first_gain, small, gate_part, up_part, down_part)


def rms_norm(values, scales):
    inverse = lax.rsqrt(jnp.mean(values * values, axis=-1, keepdims=True) + 1e-05)
    return values * inverse * scales


def gather(x):
    return lax.all_gather(x, "tensor", axis=0, tiled=True)


def dot(a, b, dims=NN):
    return lax.dot_general(a, b, dims, preferred_element_type=f32)


def on_device(tokens, lengths, attn_gain, qkv_weight, beta_weight, conv_weight, head_gain, out_weight, mlp_gain, gate_up_weight, down_weight, cotangent):
    model_width = tokens.shape[1]
    width = qkv_weight.shape[1] * qkv_weight.shape[2]
    heads = beta_weight.shape[1]
    group_rows = tokens.shape[0] * lax.axis_size("tensor")
    starts = jnp.arange(group_rows // SPAN + 8, dtype=jnp.int32) * SPAN
    flags = jnp.where((starts == 0) | (starts == lengths[0, 0]), 1.0, 0.0).astype(f32)
    local_in = tokens.astype(f32)
    first_scale = attn_gain.astype(f32)
    second_scale = mlp_gain.astype(f32)
    head_scale = head_gain.astype(f32)[None]
    conv = conv_weight.reshape(conv_weight.shape[0], -1).astype(f32)
    qkv_matrix = jnp.concatenate([qkv_weight.reshape(model_width, -1), jnp.pad(beta_weight, ((0, 0), (0, HEAD - heads)))], axis=1)
    attn_in = rms_norm(local_in, first_scale).astype(bf16)
    attn_all = gather(attn_in)
    out_all = gather(out_weight)
    cot_all = gather(cotangent)
    proj = dot(attn_all, qkv_matrix)
    headed, *saved = mixer_fwd(flags, proj, conv, head_scale)
    headed_rows = lax.all_to_all(headed, "tensor", split_axis=0, concat_axis=1, tiled=True)
    hidden_res = local_in + dot(headed_rows, out_all)
    mlp_in = rms_norm(hidden_res, second_scale).astype(bf16)
    gate_w, up_w = gate_up_weight[:, 0], gate_up_weight[:, 1]
    mlp_all, activated, d_gate, d_up, out_parts, d_mlp_in = mlp(mlp_in, cot_all, gate_w, up_w, down_weight)
    d_from_mlp, mlp_gain_part = jax.vjp(rms_norm, hidden_res, second_scale)[1](d_mlp_in)
    d_hidden = cotangent.astype(f32) + d_from_mlp
    d_attn = d_hidden.astype(bf16)
    down_part = dot(activated, cot_all, TN).astype(bf16)
    gate_part = dot(mlp_all, d_gate, TN).astype(bf16)
    up_part = dot(mlp_all, d_up, TN).astype(bf16)
    mlp_out = lax.psum_scatter(out_parts, "tensor", scatter_dimension=0, tiled=True).astype(f32)
    output = (hidden_res + mlp_out).astype(bf16)
    small = jnp.zeros((8, model_width), f32).at[1].set(mlp_gain_part)
    n_dp = lax.axis_size("dp")
    input_grad, small, *sums = backward(
        n_dp, flags, proj, conv, head_scale, saved, headed, attn_all, d_attn, out_weight, qkv_matrix, tokens, d_hidden, first_scale[None], small, gate_part, up_part, down_part)
    if n_dp > RING:
        groups = [list(range(i, n_dp, RING)) for i in range(RING)]
        small, *sums = lax.psum((small, *sums), "dp", axis_index_groups=groups)
    gate_sum, up_sum, down_sum, cat_sum, out_sum = sums
    return (
        output,
        input_grad,
        small[0],
        cat_sum[:, :width].astype(f32).reshape(qkv_weight.shape),
        cat_sum[:, width:width + heads].astype(f32),
        small[3:7, :width].reshape(conv_weight.shape),
        small[2, :HEAD],
        out_sum.astype(f32),
        small[1],
        jnp.stack([gate_sum, up_sum], axis=1).astype(f32),
        down_sum.astype(f32),
    )


def solution(mesh):
    rows = P(("dp", "tensor"), None)
    last = P(None, None, "tensor")
    return jax.shard_map(
        on_device,
        mesh=mesh,
        in_specs=(rows, P("dp", None), P(), last, P(None, "tensor"), last, P(), P("tensor", None), P(), last, P("tensor", None), rows),
        out_specs=(rows, rows, P(), last, P(None, "tensor"), last, P(), P("tensor", None), P(), last, P("tensor", None)),
        check_vma=False,
    )
```

time: 571 us -> 453 us (0.79)
  waiting for transfers between devices: 255 us -> 72.8 us
  Pallas kernels: 180 us -> 258 us
  matrix products: 43.4 us -> 30.4 us
  local copies, waits for them, and re-layouts: 32.4 us -> 38.6 us
    psum x2 -> x0, waiting for transfers between devices: 165 us -> none  [the longest x1 109 us: on_device(): gate_sum, up_sum, down_sum = lax.psum((gate_part, up_part, down_part), 'dp')]
    pallas_call x2 -> x1, Pallas kernels: 83.4 us -> 168 us  [backward(): pl.pallas_call(functools.partial(back_kernel, n_dp), grid=(n,), in_specs=...]
    all_gather x4 -> x3, waiting for transfers between devices: 50.4 us -> 33.6 us  [gather(): return lax.all_gather(x, 'tensor', axis=0, tiled=True)]
    pallas_call x1, Pallas kernels: 37.7 us -> 21.6 us  [mixer_fwd(): pl.pallas_call(mixer_fwd_kernel, grid_spec=pltpu.PrefetchScalarGridSpec(n...]
    all_to_all x1, waiting for transfers between devices: 6.25 us -> 20.3 us  [on_device(): lax.all_to_all(headed, 'tensor', split_axis=0, concat_axis=1, tiled=True)]
    reduce_scatter x1, waiting for transfers between devices: 31.6 us -> 17.5 us  [on_device(): lax.psum_scatter(out_parts, 'tensor', scatter_dimension=0, tiled=True)]
    dot_general x8 -> x5, matrix products: 43.4 us -> 30.4 us  [dot(): return lax.dot_general(a, b, dims, preferred_element_type=f32)]
    pallas_call x1, Pallas kernels: 58.7 us -> 68.9 us  [mlp(): pl.pallas_call(mlp_kernel, in_specs=[vmem] * 5, out_specs=[vmem] * 6, out...]
  transfers between devices with their start and end apart: 8 -> 5, of which waited for: 6 -> 4; matrix products, arithmetic and copies ran while one was open for 15% -> 12% of each run, Pallas kernels for 22% -> 5%
where the time goes in v3:
time: 453 us; the launch traced here: 446 us
  Pallas kernels  258 us (57%)
  waiting for transfers between devices  72.8 us (16%)
  local copies, waits for them, and re-layouts  38.6 us (9%)
  matrix products  30.4 us (7%)
  other arithmetic  26.9 us (6%)
  between operations  14.2 us (3%)
    pallas_call x1, Pallas kernels, backward(): pl.pallas_call(functools.partial(back_kernel, n_dp), grid=(n,), in_specs=...  168 us
    pallas_call x1, Pallas kernels, mlp(): pl.pallas_call(mlp_kernel, in_specs=[vmem] * 5, out_specs=[vmem] * 6, out...  68.9 us
    all_gather x3, waiting for transfers between devices, gather(): return lax.all_gather(x, 'tensor', axis=0, tiled=True)  33.6 us
    dot_general x5, matrix products, dot(): return lax.dot_general(a, b, dims, preferred_element_type=f32)  30.4 us
    unnamed x54, local copies, waits for them, and re-layouts  23.3 us
    pallas_call x1, Pallas kernels, mixer_fwd(): pl.pallas_call(mixer_fwd_kernel, grid_spec=pltpu.PrefetchScalarGridSpec(n...  21.6 us
    all_to_all x1, waiting for transfers between devices, on_device(): lax.all_to_all(headed, 'tensor', split_axis=0, concat_axis=1, tiled=True)  20.3 us
    reduce_scatter x1, waiting for transfers between devices, on_device(): lax.psum_scatter(out_parts, 'tensor', scatter_dimension=0, tiled=True)  17.5 us
  transfers between devices with their start and end apart: 5, of which 4 were waited for; matrix products, arithmetic and copies ran while one was open for 12% of the time, Pallas kernels for 5%

profile of v3, /device:TPU:0, one launch (start us, length us, event | category | flops | bytes accessed | tf_op | source)
XLA Modules:
  0.0 445.5 jit_solution(1304283273156399730)
XLA Ops:
  7.2 0.0 all-gather.4.cloned.1.call-start
  7.2 1.5 fusion.1
  8.7 0.7 convert_element_type.58
  9.4 2.6 fusion.3
  12.1 0.0 all-gather.4.cloned.1.call-update
  12.1 0.0 all-gather.6.cloned.1.call-start
  12.1 0.7 all-gather.6.cloned.1.call-update
  12.8 0.0 all-gather.8.cloned.1.call-start
  12.9 0.7 all-gather.8.cloned.1.call-update
  13.6 0.0 copy-done.18
  13.6 0.0 copy-start.4
  13.6 0.2 copy.47
  13.8 1.7 copy.46
  15.6 1.7 copy.48
  17.4 0.0 copy-done.22
  17.4 0.0 copy-start.5
  17.4 0.0 copy-start.6
  17.4 32.0 %all-gather.4.cloned.1.call-done.attn_hbm = bf16[2048,1024]{1,0:T(8,128)(2,1)} async-done(((bf16[512,1024]{1,0:T(8,128)(2,1)}), bf16[2048,1024]{1,0:T(8,128)(2,1)}) %all-gather.4.cloned.1.call-update) | async-done | bytes 4194320 | tf_op jit(solution)/shard_map/all_gather | solution.py:738
  49.4 8.8 %fusion.7.proj_ref.prev_ref = f32[2048,896]{1,0:T(8,128)} fusion(bf16[2048,1024]{1,0:T(8,128)(2,1)} %all-gather.4.cloned.1.call-done.attn_hbm, bf16[1024,2]{1,0:T(8,128)(2,1)S(1)} %copy.47, bf16[1024,768]{1,0:T(8,128)(2,1)S(1)} %copy.48), kind=kOutput, calls=%fused_computation.29 | convolution fusion | flops 3763601408 | bytes 13111296 | tf_op jit(solution)/shard_map/dot_general | solution.py:742
  58.2 0.0 copy-done.8
  58.2 21.6 %shard_map.203 = (bf16[2048,256]{1,0:T(8,128)(2,1)S(1)}, f32[2048,256]{1,0:T(8,128)S(1)}, bf16[16,256,128]{2,1,0:T(8,128)(2,1)S(1)}, bf16[16,256,128]{2,1,0:T(8,...) custom-call(f32[40]{0:T(128)S(1)} %or_select_fusion.flags, ...), custom_call_target="tpu_custom_call" | custom-call | tf_op jit(solution)/shard_map/pallas_call | solution.py:193
  79.8 1.3 copy-done.1
  81.2 1.0 copy-done.2
  82.2 1.0 copy-done.3
  83.1 1.3 copy.49
  84.5 4.3 all-to-all-start
  88.8 0.0 reduce-scatter.2.cloned.1.call-start
  88.8 2.1 fusion.11
  91.0 1.6 copy.59
  92.6 1.9 copy.58
  94.5 0.0 all-gather.6.cloned.1.call-done
  94.5 20.3 %all-to-all-done = bf16[4,512,256]{1,2,0:T(8,128)(2,1)} async-done(((bf16[4,512,256]{1,2,0:T(8,128)(2,1)}), bf16[4,512,256]{1,2,0:T(8,128)(2,1)}, u32[]{:S(2)}, u32[]{:S(2)}) %all-to-all-start) | async-done | bytes 1048608 | tf_op jit(solution)/shard_map/all_to_all | solution.py:764
  114.8 3.3 multiply_reduce_fusion.2
  118.1 1.2 multiply_convert_fusion.x_ref
  119.4 1.6 all-gather.8.cloned.1.call-done.cot_ref
  120.9 68.9 %shard_map.204 = (bf16[2048,1024]{1,0:T(8,128)(2,1)}, bf16[2048,704]{1,0:T(8,128)(2,1)}, bf16[2048,704]{1,0:T(8,128)(2,1)}, bf16[2048,704]{1,0:T(8,128)(2,1)}, b...) custom-call(bf16[512,1024]{1,0:T(8,128)(2,1)} %multiply_convert_fusion.x_ref, ...), custom_call_target="tpu_custom_call" | custom-call | tf_op jit(solution)/shard_map/pallas_call | solution.py:308
  189.8 0.0 reduce-scatter.2.cloned.1.call-update
  189.8 0.0 copy-start.20
  189.8 3.0 fusion.5.w_hbm
  192.8 5.4 %convolution_convert_fusion.1 = bf16[1024,704]{0,1:T(8,128)(2,1)S(1)} fusion(bf16[2048,1024]{1,0:T(8,128)(2,1)} %get-tuple-element.50, bf16[2048,704]{1,0:T(8,128)(2,1)S(1)} %copy-done.20), kind=kOutput, calls=%fused_computation.18 | convolution fusion | flops 2953510912 | bytes 8519680 | tf_op jit(solution)/shard_map/dot_general | solution.py:742
  198.2 1.6 copy.53.up_hbm
  199.8 6.7 %convolution_convert_fusion.2 = bf16[1024,704]{0,1:T(8,128)(2,1)S(1)} fusion(bf16[2048,1024]{1,0:T(8,128)(2,1)} %get-tuple-element.50, bf16[2048,704]{1,0:T(8,128)(2,1)} %get-tuple-element.51), kind=kOutput, calls=%fused_computation.19 | convolution fusion | flops 2953510912 | bytes 8519680 | tf_op jit(solution)/shard_map/dot_general | solution.py:742
  206.5 1.6 copy.52.gate_hbm
  208.1 2.7 multiply_reduce_fusion
  210.8 0.6 scatter.4.small_ref
  211.4 0.2 copy-done.9
  211.6 6.2 %convolution_convert_fusion.down_hbm = bf16[704,1024]{1,0:T(8,128)(2,1)} fusion(bf16[2048,704]{1,0:T(8,128)(2,1)} %get-tuple-element.53, bf16[2048,1024]{1,0:T(8,128)(2,1)S(1)} %copy-done.9), kind=kOutput, calls=%fused_computation.17 | convolution fusion | flops 2953510912 | bytes 8519680 | tf_op jit(solution)/shard_map/dot_general | solution.py:742
  217.9 17.5 %reduce-scatter.2.cloned.1.call-done = bf16[512,1024]{1,0:T(8,128)(2,1)} async-done(((bf16[2048,1024]{1,0:T(8,128)(2,1)}), bf16[512,1024]{1,0:T(8,128)(2,1)}) %reduce-scatter.2.cloned.1.call-update) | async-done | bytes 1048592 | tf_op jit(solution)/shard_map/reduce_scatter | solution.py:775
  235.4 4.6 %fusion.9 = (bf16[512,1024]{1,0:T(8,128)(2,1)}, f32[512,1024]{1,0:T(8,128)}, bf16[512,1024]{1,0:T(8,128)(2,1)}) fusion(f32[512,1024]{1,0:T(8,128)S(1)} %get-tuple-element.104, f32[512]{0:T(512)S(1)} %multiply_multiply_fusion, f32[512]{0:T(512)S(1)} %fusion.6, f32[512,1024]{1,0:T(8,128)} %get-tuple-element.49, f32[1024]{0:T(1024)S(1)} %convert_element_type.62, ...), kind=kLoop, calls=%fused_computation.30 | loop fusion | flops 5767168 | bytes 10493952 | tf_op jit(solution)/shard_map/convert_element_type | solution.py:771
  239.9 167.6 %shard_map.205 = (f32[512,1024]{1,0:T(8,128)}, f32[8,1024]{1,0:T(8,128)}, bf16[1024,704]{1,0:T(8,128)(2,1)}, bf16[1024,704]{1,0:T(8,128)(2,1)}, bf16[704,1024]{1...) custom-call(f32[40]{0:T(128)} %copy-done.5, f32[2048,896]{1,0:T(8,128)} %fusion.7.proj_ref.prev_ref, ...), custom_call_target="tpu_custom_call" | custom-call | tf_op jit(solution)/shard_map/pallas_call | solution.py:707
  407.6 1.2 slice_bitcast_fusion
  408.8 1.4 fusion.12
  410.2 1.3 slice.47
  411.5 1.8 slice_convert_fusion.1
  413.3 1.6 slice_convert_fusion
  415.0 1.8 copy.56
  416.8 2.1 convert_element_type.72
  418.9 2.4 copy.54
  421.3 3.7 copy.55
  424.9 1.9 convert_element_type.74
  426.9 1.0 copy-done.13
  427.8 3.1 maximum_convert_fusion
  431.0 6.5 %copy.57 = f32[1024,2,704]{0,2,1:T(8,128)} copy(f32[1024,2,704]{2,0,1:T(8,128)} %maximum_convert_fusion) | data formatting | bytes 11534336
  437.5 1.3 copy.61
  (41 shorter events, 0.1 us)
Async XLA Ops:
  7.2 42.2 %all-gather.4.cloned.1.call-start = ((), (), s32[]{:S(2)}) async-start(), calls=%async_computation.2 | async-start | bytes 5242880 | tf_op jit(solution)/shard_map/all_gather | solution.py:738
  9.4 4.2 copy-start.16
  9.4 4.2 copy-start.17
  9.4 4.2 copy-start.18
  9.4 4.4 copy-start.14
  12.1 82.4 %all-gather.6.cloned.1.call-start = ((), (), s32[]{:S(2)}) async-start(), calls=%async_computation.3 | async-start | bytes 2621440 | tf_op jit(solution)/shard_map/all_gather | solution.py:738
  12.8 108.1 %all-gather.8.cloned.1.call-start = ((), (), s32[]{:S(2)}) async-start(), calls=%async_computation.4 | async-start | bytes 5242880 | tf_op jit(solution)/shard_map/all_gather | solution.py:738
  13.6 44.6 %copy-start.4 = (f32[4,768]{1,0:T(4,128)}, f32[4,768]{1,0:T(4,128)S(1)}, u32[]{:S(2)}) copy-start(f32[4,768]{1,0:T(4,128)S(1)} %convert.3.conv_ref) | copy-start | bytes 36868
  15.6 1.8 copy-start.21
  15.6 1.8 copy-start.22
  17.3 40.9 %copy-start.8 = (bf16[1024,768]{1,0:T(8,128)(2,1)}, bf16[1024,768]{1,0:T(8,128)(2,1)S(1)}, u32[]{:S(2)}) copy-start(bf16[1024,768]{1,0:T(8,128)(2,1)S(1)} %copy.48) | copy-start | bytes 4718596
  17.4 40.8 %copy-start.5 = (f32[40]{0:T(128)}, f32[40]{0:T(128)S(1)}, u32[]{:S(2)}) copy-start(f32[40]{0:T(128)S(1)} %or_select_fusion.flags) | copy-start | bytes 484
  17.4 40.8 %copy-start.6 = (f32[1,128]{1,0:T(1,128)}, f32[1,128]{1,0:T(1,128)S(1)}, u32[]{:S(2)}) copy-start(f32[1,128]{1,0:T(1,128)S(1)} %bitcast_convert_fusion.gain_ref) | copy-start | bytes 1540
  79.8 1.3 copy-start.1
  81.2 1.0 copy-start.2
  82.2 1.0 copy-start.3
  83.1 1.4 copy-start
  83.1 5.7 %copy-start.19 = (bf16[1024]{0:T(1024)(128)(2,1)S(1)}, bf16[1024]{0:T(1024)(128)(2,1)}, u32[]{:S(2)}) copy-start(bf16[1024]{0:T(1024)(128)(2,1)} %param.22) | copy-start | bytes 6148
  84.5 30.3 %all-to-all-start = ((bf16[4,512,256]{1,2,0:T(8,128)(2,1)}), bf16[4,512,256]{1,2,0:T(8,128)(2,1)}, u32[]{:S(2)}, u32[]{:S(2)}) async-start(bf16[4,512,256]{1,2,0:T(8,128)(2,1)} %copy.49), calls=%async_computation | async-start | bytes 2097152 | tf_op jit(solution)/shard_map/all_to_all | solution.py:764
  88.8 146.6 %reduce-scatter.2.cloned.1.call-start = ((), (), s32[]{:S(2)}) async-start(), calls=%async_computation.5 | async-start | bytes 5242880 | tf_op jit(solution)/shard_map/reduce_scatter | solution.py:775
  92.6 22.3 %copy-start.7 = (bf16[512,1024]{1,0:T(8,128)(2,1)S(1)}, bf16[512,1024]{1,0:T(8,128)(2,1)}, u32[]{:S(2)}) copy-start(bf16[512,1024]{1,0:T(8,128)(2,1)} %tok_hbm.1) | copy-start | bytes 3145732
  189.8 3.0 copy-start.20
  208.1 3.5 copy-start.9
  211.6 23.7 %copy-start.10 = (bf16[512,1024]{1,0:T(8,128)(2,1)S(1)}, bf16[512,1024]{1,0:T(8,128)(2,1)}, u32[]{:S(2)}) copy-start(bf16[512,1024]{1,0:T(8,128)(2,1)} %param.25) | copy-start | bytes 3145732
  421.3 3.7 copy-start.15
  424.9 2.0 copy-start.12
  424.9 2.9 copy-start.13
  431.0 6.5 %copy-start.11 = (f32[512,1024]{1,0:T(8,128)S(1)}, f32[512,1024]{1,0:T(8,128)}, u32[]{:S(2)}) copy-start(f32[512,1024]{1,0:T(8,128)} %get-tuple-element.117) | copy-start | bytes 6291460
Sparse Core Ops, SparseCore 0:
  12.2 37.1 all-gather.3
  51.0 22.5 all-gather.5
  75.2 45.7 all-gather.7
  190.0 45.3 reduce-scatter.1

commit v4 on v3

--- a/solution.py
+++ b/solution.py
@@ -236,85 +236,192 @@
     return pl.ds(pl.multiple_of(owner * owner_rows + part * part_rows, part_rows), part_rows)
 
 
-def mlp_kernel(x_ref, cot_ref, gate_w, up_w, down_w, all_ref, act_ref, dgate_ref, dup_ref, out_ref, sum_ref, mine, to_beside, from_beside, to_across, from_across, to_own, from_own, send, recv):
+def mlp_kernel(headed_hbm, out_hbm, tok_hbm, gain_ref, gu_hbm, down_hbm, cot_hbm,
+               dhid_hbm, dattn_hbm, gain_out, gu_out, downg_out, own_hbm, across_hbm,
+               headed, out_w, tok, gu_w, down_w, cot, hidden, all_rows, act, d_gate, d_up, mine, keep, to_beside, from_beside, to_across, from_across, to_own, from_own,
+               out_own, out_keep, from_beside_out, from_own_out, gu_acc, down_acc, gu_sum, down_sum, dattn, load, store, send, recv):
     d, t, beside, across, corner = places()
-    rows = x_ref.shape[0]
+    rows = tok.shape[0]
     part = rows // HALF
+    units = down_w.shape[0]
+    loads = [(headed_hbm, headed), (out_hbm, out_w), (tok_hbm, tok), (gu_hbm, gu_w), (down_hbm, down_w), (cot_hbm, cot)]
+    stores = [(mine, dhid_hbm), (dattn, dattn_hbm), (gu_sum, gu_out), (down_sum, downg_out), (out_own, own_hbm), (out_keep, across_hbm)]
+
+    def loaded(i):
+        return pltpu.make_async_copy(loads[i][0], loads[i][1], load.at[i])
+
+    def stored(i):
+        return pltpu.make_async_copy(stores[i][0], stores[i][1], store.at[i])
+
+    def pushed(src, dst, i, s, peer):
+        return pltpu.make_async_remote_copy(src_ref=src, dst_ref=dst, send_sem=send.at[i, s], recv_sem=recv.at[i, s], device_id=(d, peer), device_id_type=MESH_ID)
+
+    def half(ref, s):
+        return ref.at[pl.ds(s * part, part)]
+
+    def rows_to(i, s, peer):
+        block = all_rows.at[row_block(t, s, rows, part)]
+        return pushed(block, block, i, s, peer)
+
+    def passed(s):
+        block = all_rows.at[row_block(across, s, rows, part)]
+        return pushed(block, block, 2, s, beside)
+
+    def handed(s):
+        return pushed(half(to_beside, s), half(from_beside, s), 3, s, beside)
+
+    def summed(s):
+        return pushed(half(to_across, s), half(from_across, s), 4, s, across)
+
+    def owned(s):
+        return pushed(half(to_own, s), half(from_own, s), 5, s, beside)
+
+    def handed_out(s):
+        return pushed(half(headed, s), half(from_beside_out, s), 6, s, beside)
+
+    def owned_out(s):
+        return pushed(half(dattn, s), half(from_own_out, s), 7, s, beside)
+
+    for i in range(len(loads)):
+        loaded(i).start()
     greet([(d, beside), (d, across)])
-    copies = []
-    arrive_beside, arrive_across = [], []
+    for i in range(3):
+        loaded(i).wait()
+    gain = gain_ref[...]
     for s in range(HALF):
-        src = x_ref.at[pl.ds(s * part, part)]
-        dst = all_ref.at[row_block(t, s, rows, part)]
-        arrive_across.append(push(src, dst, send.at[0, s], recv.at[0, s], (d, across)))
-        arrive_beside.append(push(src, dst, send.at[1, s], recv.at[1, s], (d, beside)))
-    all_ref[pl.ds(pl.multiple_of(t * rows, rows), rows), :] = x_ref[...]
-    copies += arrive_across + arrive_beside
+        at = pl.ds(s * part, part)
+        x = tok[at, :].astype(f32) + lax.dot_general(headed[at, :], out_w[...], NN, preferred_element_type=f32)
+        hidden[at, :] = x
+        all_rows[row_block(t, s, rows, part), :] = (x * lax.rsqrt(jnp.mean(x * x, axis=-1, keepdims=True) + 1e-5) * gain).astype(bf16)
+        rows_to(0, s, across).start()
+        rows_to(1, s, beside).start()
+    for i in range(3, len(loads)):
+        loaded(i).wait()
 
     def work(owner, s):
         at = row_block(owner, s, rows, part)
-        x = all_ref[at, :]
-        gate = lax.dot_general(x, gate_w[...], NN, preferred_element_type=f32)
-        up = lax.dot_general(x, up_w[...], NN, preferred_element_type=f32)
-        sig = jax.nn.sigmoid(gate)
+        x = all_rows[at, :]
+        gate = lax.dot_general(x, gu_w[:units, :], NT, preferred_element_type=f32)
+        up = lax.dot_general(x, gu_w[units:, :], NT, preferred_element_type=f32)
+        sig = sigmoid(gate)
         silu = gate * sig
-        act = (silu * up).astype(bf16)
-        act_ref[at, :] = act
-        d_act = lax.dot_general(cot_ref[at, :], down_w[...], NT, preferred_element_type=f32)
-        d_gate = (d_act * up * sig * (1.0 + gate * (1.0 - sig))).astype(bf16)
-        d_up = (d_act * silu).astype(bf16)
-        dgate_ref[at, :] = d_gate
-        dup_ref[at, :] = d_up
-        out_ref[at, :] = lax.dot_general(act, down_w[...], NN, preferred_element_type=f32).astype(bf16)
-        return lax.dot_general(d_gate, gate_w[...], NT, preferred_element_type=f32) + lax.dot_general(d_up, up_w[...], NT, preferred_element_type=f32)
-
-    for s in range(HALF):
-        mine[pl.ds(s * part, part), :] = work(t, s)
-    own_copies = []
-    for s in range(HALF):
-        arrive_beside[s].wait_recv()
-        at = pl.ds(s * part, part)
-        to_own[at, :] = work(beside, s).astype(bf16)
-        own_copies.append(push(to_own.at[at], from_own.at[at], send.at[2, s], recv.at[2, s], (d, beside)))
-    passed, sums = [], []
+        low = (silu * up).astype(bf16)
+        act[at, :] = low
+        d_act = lax.dot_general(cot[at, :], down_w[...], NT, preferred_element_type=f32)
+        dg = (d_act * up * sig * (1.0 + gate * (1.0 - sig))).astype(bf16)
+        du = (d_act * silu).astype(bf16)
+        d_gate[at, :] = dg
+        d_up[at, :] = du
+        out = lax.dot_general(low, down_w[...], NN, preferred_element_type=f32)
+        return lax.dot_general(dg, gu_w[:units, :], NN, preferred_element_type=f32) + lax.dot_general(du, gu_w[units:, :], NN, preferred_element_type=f32), out
+
+    def weight_grads(pair, last):
+        at = pl.ds(pl.multiple_of(pair * 2 * rows, 2 * rows), 2 * rows)
+
+        def put(acc, total, where, value):
+            if last:
+                total[where, :] = (acc[where, :] + value).astype(bf16)
+            else:
+                acc[where, :] = value
+
+        for c in range(0, units, 256):
+            size = min(256, units - c)
+            put(gu_acc, gu_sum, pl.ds(c, size), lax.dot_general(d_gate[at, c:c + size], all_rows[at, :], TN, preferred_element_type=f32))
+            put(gu_acc, gu_sum, pl.ds(units + c, size), lax.dot_general(d_up[at, c:c + size], all_rows[at, :], TN, preferred_element_type=f32))
+            put(down_acc, down_sum, pl.ds(c, size), lax.dot_general(act[at, c:c + size], cot[at, :], TN, preferred_element_type=f32))
+
     for s in range(HALF):
         at = pl.ds(s * part, part)
-        arrive_across[s].wait_recv()
-        block = all_ref.at[row_block(across, s, rows, part)]
-        passed.append(push(block, block, send.at[3, s], recv.at[3, s], (d, beside)))
-        passed[s].wait_recv()
-        to_beside[at, :] = work(corner, s).astype(bf16)
-        handed = push(to_beside.at[at], from_beside.at[at], send.at[4, s], recv.at[4, s], (d, beside))
-        total = work(across, s)
-        handed.wait_recv()
-        to_across[at, :] = (total + from_beside[at, :].astype(f32)).astype(bf16)
-        sums.append(push(to_across.at[at], from_across.at[at], send.at[5, s], recv.at[5, s], (d, across)))
-        copies.append(handed)
+        mine[at, :], out = work(t, s)
+        out_own[at, :] = hidden[at, :] + out
     for s in range(HALF):
         at = pl.ds(s * part, part)
-        own_copies[s].wait_recv()
-        sums[s].wait_recv()
-        sum_ref[at, :] = mine[at, :] + from_own[at, :].astype(f32) + from_across[at, :].astype(f32)
-    for copy in copies + own_copies + passed + sums:
-        copy.wait_send()
-
-
-def mlp(x, cot, gate_w, up_w, down_w):
-    rows, width = x.shape
+        rows_to(1, s, beside).wait_recv()
+        total, out = work(beside, s)
+        to_own[at, :] = total.astype(bf16)
+        owned(s).start()
+        dattn[at, :] = out.astype(bf16)
+        owned_out(s).start()
+    for s in range(HALF):
+        at = pl.ds(s * part, part)
+        rows_to(0, s, across).wait_recv()
+        passed(s).start()
+        keep[...], out = work(across, s)
+        out_keep[at, :] = out.astype(bf16)
+        passed(s).wait_recv()
+        total, out = work(corner, s)
+        to_beside[at, :] = total.astype(bf16)
+        handed(s).start()
+        headed[at, :] = out.astype(bf16)
+        handed_out(s).start()
+        handed(s).wait_recv()
+        to_across[at, :] = (keep[...] + from_beside[at, :].astype(f32)).astype(bf16)
+        summed(s).start()
+        if s == 0:
+            weight_grads(t // 2, False)
+    weight_grads(1 - t // 2, True)
+    stored(2).start()
+    stored(3).start()
+    for s in range(HALF):
+        at = pl.ds(s * part, part)
+        handed_out(s).wait_recv()
+        out_keep[at, :] = (out_keep[at, :].astype(f32) + from_beside_out[at, :].astype(f32)).astype(bf16)
+        owned_out(s).wait_recv()
+        out_own[at, :] = out_own[at, :] + from_own_out[at, :].astype(f32)
+        owned_out(s).wait_send()
+    stored(4).start()
+    stored(5).start()
+    gain_out[...] = jnp.zeros_like(gain_out)
+    piece = 64
+    for s in range(HALF):
+        owned(s).wait_recv()
+        summed(s).wait_recv()
+
+        def chunk(i, carry, s=s):
+            at = pl.ds(pl.multiple_of(s * part + i * piece, piece), piece)
+            grad = mine[at, :] + from_own[at, :].astype(f32) + from_across[at, :].astype(f32)
+            x = hidden[at, :]
+            r = lax.rsqrt(jnp.mean(x * x, axis=-1, keepdims=True) + 1e-5)
+            scaled = gain * grad
+            cot_rows = cot[pl.ds(pl.multiple_of(t * rows + s * part + i * piece, piece), piece), :].astype(f32)
+            full = cot_rows + r * scaled - x * (r * r * r * jnp.mean(x * scaled, axis=-1, keepdims=True))
+            mine[at, :] = full
+            dattn[at, :] = full.astype(bf16)
+            gain_out[...] += jnp.sum((grad * x * r).reshape(piece // 8, 8, grad.shape[1]), axis=0)
+            return carry
+
+        lax.fori_loop(0, part // piece, chunk, 0)
+    stored(0).start()
+    stored(1).start()
+    for s in range(HALF):
+        for copy in (rows_to(0, s, across), rows_to(1, s, beside), passed(s), handed(s), summed(s), owned(s), handed_out(s)):
+            copy.wait_send()
+    for i in range(len(stores)):
+        stored(i).wait()
+
+
+def mlp(headed, out_all, tokens, gain, gate_up, down, cot):
+    rows, width = tokens.shape
     total = cot.shape[0]
-    units = gate_w.shape[1]
+    units = down.shape[0]
+    hbm = pl.BlockSpec(memory_space=pl.ANY)
     vmem = pl.BlockSpec(memory_space=pltpu.VMEM)
+    like = lambda x: pltpu.VMEM(x.shape, x.dtype)
     half = lambda: pltpu.VMEM((rows, width), bf16)
+    wide = lambda: pltpu.VMEM((rows, width), f32)
+    unit = lambda: pltpu.VMEM((total, units), bf16)
+    out = lambda shape, kind: jax.ShapeDtypeStruct(shape, kind)
+    dma = pltpu.SemaphoreType.DMA
     return pl.pallas_call(
         mlp_kernel,
-        in_specs=[vmem] * 5,
-        out_specs=[vmem] * 6,
-        out_shape=[jax.ShapeDtypeStruct((total, width), bf16), jax.ShapeDtypeStruct((total, units), bf16), jax.ShapeDtypeStruct((total, units), bf16),
-                   jax.ShapeDtypeStruct((total, units), bf16), jax.ShapeDtypeStruct((total, width), bf16), jax.ShapeDtypeStruct((rows, width), f32)],
-        scratch_shapes=[pltpu.VMEM((rows, width), f32), half(), half(), half(), half(), half(), half(),
-                        pltpu.SemaphoreType.DMA((6, HALF)), pltpu.SemaphoreType.DMA((6, HALF))],
-        compiler_params=pltpu.CompilerParams(collective_id=1, has_side_effects=True, vmem_limit_bytes=60 * 2**20),
-    )(x, cot, gate_w, up_w, down_w)
+        in_specs=[hbm] * 3 + [vmem] + [hbm] * 3,
+        out_specs=[hbm] * 2 + [vmem] + [hbm] * 4,
+        out_shape=[out((rows, width), f32), out((rows, width), bf16), out((8, width), f32), out(gate_up.shape, bf16), out(down.shape, bf16), out((rows, width), f32), out((rows, width), bf16)],
+        scratch_shapes=[like(headed), like(out_all), like(tokens), like(gate_up), like(down), like(cot), wide(), pltpu.VMEM((total, width), bf16), unit(), unit(), unit(),
+                        wide(), pltpu.VMEM((rows // HALF, width), f32), half(), half(), half(), half(), half(), half(), wide(), half(), half(), half(),
+                        pltpu.VMEM(gate_up.shape, f32), pltpu.VMEM(down.shape, f32), like(gate_up), like(down), half(), dma((6,)), dma((6,)), dma((8, HALF)), dma((8, HALF))],
+        compiler_params=pltpu.CompilerParams(collective_id=1, has_side_effects=True, vmem_limit_bytes=62 * 2**20),
+    )(headed, out_all, tokens, gain, gate_up, down, cot)
 
 
 def mixer_bwd_block(blk, width, flags, proj_ref, prev_ref, conv_ref, gain_ref, mixed_ref, state_in, res_in, wu_in, inv_in, dheaded, dcat, dstate, buf, dbuf, cacc, gacc):
@@ -469,12 +576,12 @@
 
 
 def back_kernel(n_dp, flags, proj_ref, prev_ref, conv_ref, gain_ref, mixed_ref, state_in, res_in, wu_in, inv_in,
-                headed_hbm, attn_hbm, dattn_hbm, out_w_hbm, w_hbm, tok_hbm, dhid_hbm, first_gain, small_ref, gate_hbm, up_hbm, down_hbm,
-                dx_hbm, small_out, gate_out, up_out, down_out, cat_out, outw_out,
-                headed, attn, dattn_all, out_w, w, tok, dhid, gate_src, up_src, down_src, cat_src, outw_src,
-                gate_res, up_res, down_res, cat_res, outw_res, gate_land, up_land, down_land, cat_land, outw_land,
+                headed_hbm, attn_hbm, dattn_hbm, out_w_hbm, qkv_hbm, beta_hbm, tok_hbm, dhid_hbm, first_gain, second_grad, gu_hbm, down_hbm, across_hbm,
+                dx_hbm, small_out, gu_out, down_out, cat_out, outw_out, landed_hbm,
+                headed, attn, dattn_all, out_w, w, tok, dhid, gu_src, down_src, cat_src, outw_src,
+                gu_res, down_res, cat_res, outw_res, gate_land, up_land, down_land, cat_land, outw_land,
                 dheaded, dcat, dstate, buf, dbuf, cacc, gacc, mine, to_beside, from_beside, to_across, from_across, to_own, from_own,
-                group_send, group_land, all_send, all_land, gain_acc,
+                group_send, group_land, all_send, all_land, gain_acc, beta_grad,
                 load, store, send_m, recv_m, send_c, recv_c, send_x, recv_x, send_g, recv_g, send_a, recv_a):
     g = pl.program_id(0)
     n = pl.num_programs(0)
@@ -484,10 +591,13 @@
     part = rows // HALF
     width = buf.shape[1]
     others = [d // RING * RING + lax.rem(d + k, RING) for k in range(1, RING)]
-    mlp_ring = Ring(here, (after, t), (before, t), [gate_src, up_src, down_src], [gate_res, up_res, down_res], [gate_land, up_land, down_land], [True, True, False], send_m, recv_m)
+    units = down_src.shape[0]
+    gate_up = lambda ref: [ref.at[pl.ds(0, units)], ref.at[pl.ds(units, units)]]
+    mlp_ring = Ring(here, (after, t), (before, t), gate_up(gu_src) + [down_src], gate_up(gu_res) + [down_res], [gate_land, up_land, down_land], [False] * 3, send_m, recv_m)
     cat_ring = Ring(here, (after, t), (before, t), [cat_src, outw_src], [cat_res, outw_res], [cat_land, outw_land], [True, True], send_c, recv_c)
-    loads = [(gate_hbm, gate_src), (up_hbm, up_src), (down_hbm, down_src), (dattn_hbm, dattn_all.at[pl.ds(pl.multiple_of(t * rows, rows), rows)]), (out_w_hbm, out_w), (headed_hbm, headed), (attn_hbm, attn), (w_hbm, w), (tok_hbm, tok), (dhid_hbm, dhid)]
-    stores = [(gate_res, gate_out), (up_res, up_out), (down_res, down_out), (mine, dx_hbm), (cat_res, cat_out), (outw_res, outw_out)]
+    loads = [(gu_hbm, gu_src), (down_hbm, down_src), (dattn_hbm, dattn_all.at[pl.ds(pl.multiple_of(t * rows, rows), rows)]), (out_w_hbm, out_w), (headed_hbm, headed), (attn_hbm, attn), (tok_hbm, tok), (dhid_hbm, dhid), (beta_hbm, w.at[:, pl.ds(width, HEAD)])]
+    loads += [(qkv_hbm.at[i], w.at[:, pl.ds(i * 2 * HEAD, 2 * HEAD)]) for i in range(3)]
+    stores = [(gu_res, gu_out), (down_res, down_out), (mine, dx_hbm), (cat_res, cat_out), (outw_res, outw_out)]
 
     def loaded(i):
         return pltpu.make_async_copy(loads[i][0], loads[i][1], load.at[i])
@@ -497,6 +607,9 @@
 
     def pushed(src, dst, i, s, peer):
         return pltpu.make_async_remote_copy(src_ref=src, dst_ref=dst, send_sem=send_x.at[i, s], recv_sem=recv_x.at[i, s], device_id=(d, peer), device_id_type=MESH_ID)
+
+    def outward():
+        return pushed(across_hbm, landed_hbm, 6, 0, across)
 
     def block_at(owner, s):
         return row_block(owner, s, rows, part)
@@ -518,13 +631,13 @@
         for i in range(len(loads)):
             loaded(i).start()
         greet([(d, beside), (d, across), (d, corner)] + [(o, t) for o in others])
-        for i in range(4):
+        for i in range(3):
             loaded(i).wait()
         for s in range(HALF):
             rows_to(0, s, across).start()
             rows_to(1, s, beside).start()
         mlp_ring.round(0)
-        loaded(4).wait()
+        loaded(3).wait()
         dstate[...] = jnp.zeros_like(dstate)
         dbuf[BACK_ROWS:, :] = jnp.zeros((8, width), f32)
         cacc[...] = jnp.zeros_like(cacc)
@@ -548,6 +661,7 @@
         head_grad(across, 1)
         passed(1).wait_recv()
         head_grad(corner, 1)
+        outward().start()
         mlp_ring.round(4)
 
     for at, r in ((1, 5), (3, 6), (5, 7), (6, 8)):
@@ -598,19 +712,21 @@
 
     @pl.when(g == n - 1)
     def _():
-        for i in range(5, len(loads)):
+        for i in range(4, len(loads)):
             loaded(i).wait()
         mlp_ring.round(9)
 
         def cat_chunk(i):
-            at = pl.ds(i * 256, 256)
-            cat_src[at, :] = lax.dot_general(attn[:, i * 256:(i + 1) * 256], dcat[...], TN, preferred_element_type=f32).astype(bf16)
+            grad = lax.dot_general(attn[:, i * 256:(i + 1) * 256], dcat[:, :width], TN, preferred_element_type=f32).astype(bf16)
+            for j in range(3):
+                cat_src[pl.ds(j * attn.shape[1] + i * 256, 256), :] = grad[:, j * 2 * HEAD:(j + 1) * 2 * HEAD]
 
         count = attn.shape[1] // 256
         for i in range(count):
             cat_chunk(i)
             if i == count // 2 - 1:
                 mlp_ring.round(10)
+        beta_grad[...] = lax.dot_general(dcat[:, width:], attn[...], TN, preferred_element_type=f32)[:8]
         outw_src[...] = lax.dot_general(headed[...], dattn_all[...], TN, preferred_element_type=f32).astype(bf16)
         cat_ring.round(0)
         mlp_ring.round(11)
@@ -634,7 +750,7 @@
         cat_ring.round(3)
         cat_ring.round(4)
         mlp_ring.round(14)
-        for i in range(3):
+        for i in range(2):
             stored(i).start()
         cat_ring.round(5)
         owned(0).wait_recv()
@@ -645,13 +761,17 @@
         owned(1).wait_recv()
         summed(1).wait_recv()
         finish(1)
-        stored(3).start()
+        stored(2).start()
         cat_ring.round(8)
-        line = lax.broadcasted_iota(jnp.int32, small_ref.shape, 0)
-        small = jnp.where(line == 0, jnp.sum(gain_acc[...], axis=0, keepdims=True), small_ref[...])
-        head_part = jnp.sum(gacc[...], axis=0, keepdims=True)
-        small = jnp.where(line == 2, jnp.concatenate([head_part] + [jnp.zeros_like(head_part)] * (small.shape[1] // HEAD - 1), axis=1), small)
-        group_send[...] = small
+        line = lax.broadcasted_iota(jnp.int32, small_out.shape, 0)
+        lane = lax.broadcasted_iota(jnp.int32, small_out.shape, 1)
+        shared = (line < 2) | ((line == 3) & (lane >= width))
+        group_send[...] = jnp.zeros_like(group_send)
+        group_send[0:1, :] = jnp.sum(gain_acc[...], axis=0, keepdims=True)
+        group_send[1:2, :] = jnp.sum(second_grad[...], axis=0, keepdims=True)
+        group_send[2:3, :] = beta_grad[0:1, :]
+        group_send[7:8, :] = beta_grad[1:2, :]
+        group_send[3:4, width:width + HEAD] = jnp.sum(gacc[...], axis=0, keepdims=True)
         for j in range(4):
             group_send[3 + j:4 + j, :width] = jnp.sum(cacc[j], axis=0, keepdims=True)
         for i, peer in enumerate((beside, across, corner)):
@@ -661,7 +781,7 @@
         for i, peer in enumerate((beside, across, corner)):
             grouped(i, peer).wait_recv()
         both = (small + group_land[0]) + (group_land[1] + group_land[2])
-        small = jnp.where(line < 3, both, small)
+        small = jnp.where(shared, both, small)
         all_send[...] = small
         for i, o in enumerate(others):
             spread(i, o).start()
@@ -674,7 +794,7 @@
         cat_ring.round(12)
         cat_ring.round(13)
         cat_ring.round(14)
-        for i in range(4, 6):
+        for i in range(3, 5):
             stored(i).start()
         for s in range(HALF):
             for copy in (rows_to(0, s, across), rows_to(1, s, beside), passed(s), handed(s), summed(s), owned(s)):
@@ -683,11 +803,12 @@
             grouped(i, peer).wait_send()
         for i, o in enumerate(others):
             spread(i, o).wait_send()
+        outward().wait()
         for i in range(len(stores)):
             stored(i).wait()
 
 
-def backward(n_dp, flags, proj, conv, gain, saved, headed, attn_all, d_attn, out_w, w, tokens, d_hidden, first_gain, small, gate_part, up_part, down_part):
+def backward(n_dp, flags, proj, conv, gain, saved, headed, attn_all, d_attn, out_w, qkv, beta, tokens, d_hidden, first_gain, second_grad, gu_part, down_part, out_across):
     mixed, states, res, wu, inv = saved
     total_rows, total = proj.shape
     width = conv.shape[1]
@@ -699,10 +820,10 @@
     hbm = pl.BlockSpec(memory_space=pl.ANY)
     dma = pltpu.SemaphoreType.DMA
     like = lambda x: pltpu.VMEM(x.shape, x.dtype)
-    mlp_parts = (gate_part, up_part, down_part)
-    cat_shapes = [(model, total), (headed.shape[1], model)]
+    mlp_parts = (gu_part, down_part)
+    cat_shapes = [(3 * model, 2 * HEAD), (headed.shape[1], model)]
     half = lambda: pltpu.VMEM((rows, model), bf16)
-    line = small.shape
+    line = second_grad.shape
     out = lambda shape, kind: jax.ShapeDtypeStruct(shape, kind)
     return pl.pallas_call(
         functools.partial(back_kernel, n_dp),
@@ -712,21 +833,21 @@
                   pl.BlockSpec((4, width), z2), pl.BlockSpec((1, HEAD), z2), pl.BlockSpec((BACK_ROWS, 2 * HEAD), m2),
                   pl.BlockSpec((BACK_STEPS, 2 * HEAD, HEAD), m3), pl.BlockSpec((BACK_STEPS, 2 * STEP, HEAD), m3),
                   pl.BlockSpec((BACK_STEPS, 2 * STEP, 2 * HEAD), m3), pl.BlockSpec((BACK_STEPS, 2 * STEP, 2 * STEP), m3)]
-        + [hbm] * 7 + [pl.BlockSpec((1, model), z2), pl.BlockSpec(line, z2)] + [hbm] * 3,
+        + [hbm] * 8 + [pl.BlockSpec((1, model), z2), pl.BlockSpec(line, z2)] + [hbm] * 3,
         out_specs=[hbm, pl.BlockSpec(line, z2)] + [hbm] * 5,
-        out_shape=[out((rows, model), f32), out(line, f32)] + [out(x.shape, bf16) for x in mlp_parts] + [out(s, bf16) for s in cat_shapes],
-        scratch_shapes=[like(headed), like(attn_all), like(attn_all), like(out_w), like(w), like(tokens), like(d_hidden)]
+        out_shape=[out((rows, model), f32), out(line, f32)] + [out(x.shape, bf16) for x in mlp_parts] + [out(s, bf16) for s in cat_shapes] + [out((rows, model), bf16)],
+        scratch_shapes=[like(headed), like(attn_all), like(attn_all), like(out_w), pltpu.VMEM((model, total), bf16), like(tokens), like(d_hidden)]
         + [like(x) for x in mlp_parts] + [pltpu.VMEM(s, bf16) for s in cat_shapes]
         + [like(x) for x in mlp_parts] + [pltpu.VMEM(s, bf16) for s in cat_shapes]
-        + ring_lands([x.shape for x in mlp_parts], [True, True, False]) + ring_lands(cat_shapes, [True, True])
+        + ring_lands([down_part.shape] * 3, [False] * 3) + ring_lands(cat_shapes, [True, True])
         + [pltpu.VMEM((total_rows, 2 * HEAD), bf16), pltpu.VMEM((total_rows, total), bf16), pltpu.VMEM((2, HEAD, HEAD), f32),
            pltpu.VMEM((BACK_ROWS + 8, width), f32), pltpu.VMEM((BACK_ROWS + 8, width), f32), pltpu.VMEM((4, 8, width), f32), pltpu.VMEM((8, HEAD), f32),
            pltpu.VMEM((rows, model), f32), half(), half(), half(), half(), half(), half(),
-           pltpu.VMEM(line, f32), pltpu.VMEM((3,) + line, f32), pltpu.VMEM(line, f32), pltpu.VMEM((RING - 1,) + line, f32), pltpu.VMEM((8, model), f32),
-           dma((10,)), dma((6,)), dma((3, 2)), dma((3, 2, ROUNDS)), dma((2, 2)), dma((2, 2, ROUNDS)), dma((6, HALF)), dma((6, HALF)),
+           pltpu.VMEM(line, f32), pltpu.VMEM((3,) + line, f32), pltpu.VMEM(line, f32), pltpu.VMEM((RING - 1,) + line, f32), pltpu.VMEM((8, model), f32), pltpu.VMEM((8, model), f32),
+           dma((13,)), dma((5,)), dma((3, 2)), dma((3, 2, ROUNDS)), dma((2, 2)), dma((2, 2, ROUNDS)), dma((7, HALF)), dma((7, HALF)),
            dma((3,)), dma((3,)), dma((RING - 1,)), dma((RING - 1,))],
         compiler_params=pltpu.CompilerParams(dimension_semantics=("arbitrary",), collective_id=2, has_side_effects=True, vmem_limit_bytes=62 * 2**20),
-    )(flags, proj, proj, conv, gain, mixed, states, res, wu, inv, headed, attn_all, d_attn, out_w, w, tokens, d_hidden, first_gain, small, gate_part, up_part, down_part)
+    )(flags, proj, proj, conv, gain, mixed, states, res, wu, inv, headed, attn_all, d_attn, out_w, qkv, beta, tokens, d_hidden, first_gain, second_grad, gu_part, down_part, out_across)
 
 
 def rms_norm(values, scales):
@@ -754,45 +875,36 @@
     second_scale = mlp_gain.astype(f32)
     head_scale = head_gain.astype(f32)[None]
     conv = conv_weight.reshape(conv_weight.shape[0], -1).astype(f32)
-    qkv_matrix = jnp.concatenate([qkv_weight.reshape(model_width, -1), jnp.pad(beta_weight, ((0, 0), (0, HEAD - heads)))], axis=1)
+    qkv = jnp.transpose(qkv_weight, (1, 0, 2))
+    beta = jnp.pad(beta_weight, ((0, 0), (0, HEAD - heads)))
+    gate_up = jnp.transpose(gate_up_weight, (1, 2, 0)).reshape(-1, model_width)
     attn_in = rms_norm(local_in, first_scale).astype(bf16)
     attn_all = gather(attn_in)
     out_all = gather(out_weight)
     cot_all = gather(cotangent)
-    proj = dot(attn_all, qkv_matrix)
+    proj = dot(attn_all, jnp.concatenate([qkv[0], qkv[1], qkv[2], beta], axis=1))
     headed, *saved = mixer_fwd(flags, proj, conv, head_scale)
     headed_rows = lax.all_to_all(headed, "tensor", split_axis=0, concat_axis=1, tiled=True)
-    hidden_res = local_in + dot(headed_rows, out_all)
-    mlp_in = rms_norm(hidden_res, second_scale).astype(bf16)
-    gate_w, up_w = gate_up_weight[:, 0], gate_up_weight[:, 1]
-    mlp_all, activated, d_gate, d_up, out_parts, d_mlp_in = mlp(mlp_in, cot_all, gate_w, up_w, down_weight)
-    d_from_mlp, mlp_gain_part = jax.vjp(rms_norm, hidden_res, second_scale)[1](d_mlp_in)
-    d_hidden = cotangent.astype(f32) + d_from_mlp
-    d_attn = d_hidden.astype(bf16)
-    down_part = dot(activated, cot_all, TN).astype(bf16)
-    gate_part = dot(mlp_all, d_gate, TN).astype(bf16)
-    up_part = dot(mlp_all, d_up, TN).astype(bf16)
-    mlp_out = lax.psum_scatter(out_parts, "tensor", scatter_dimension=0, tiled=True).astype(f32)
-    output = (hidden_res + mlp_out).astype(bf16)
-    small = jnp.zeros((8, model_width), f32).at[1].set(mlp_gain_part)
+    d_hidden, d_attn, second_grad, gu_part, down_part, out_own, out_across = mlp(headed_rows, out_all, tokens, second_scale[None], gate_up, down_weight, cot_all)
     n_dp = lax.axis_size("dp")
-    input_grad, small, *sums = backward(
-        n_dp, flags, proj, conv, head_scale, saved, headed, attn_all, d_attn, out_weight, qkv_matrix, tokens, d_hidden, first_scale[None], small, gate_part, up_part, down_part)
+    input_grad, small, *sums, landed = backward(
+        n_dp, flags, proj, conv, head_scale, saved, headed, attn_all, d_attn, out_weight, qkv, beta, tokens, d_hidden, first_scale[None], second_grad, gu_part, down_part, out_across)
     if n_dp > RING:
         groups = [list(range(i, n_dp, RING)) for i in range(RING)]
         small, *sums = lax.psum((small, *sums), "dp", axis_index_groups=groups)
-    gate_sum, up_sum, down_sum, cat_sum, out_sum = sums
+    gu_sum, down_sum, cat_sum, out_sum = sums
+    output = (out_own + landed.astype(f32)).astype(bf16)
     return (
         output,
         input_grad,
         small[0],
-        cat_sum[:, :width].astype(f32).reshape(qkv_weight.shape),
-        cat_sum[:, width:width + heads].astype(f32),
+        jnp.transpose(cat_sum.astype(f32).reshape(3, model_width, -1), (1, 0, 2)),
+        jnp.stack([small[2], small[7]], axis=1),
         small[3:7, :width].reshape(conv_weight.shape),
-        small[2, :HEAD],
+        small[3, width:width + HEAD],
         out_sum.astype(f32),
         small[1],
-        jnp.stack([gate_sum, up_sum], axis=1).astype(f32),
+        jnp.transpose(gu_sum.astype(f32).reshape(2, -1, model_width), (2, 0, 1)),
         down_sum.astype(f32),
     )
 

time: 453 us -> 378 us (0.83)
  local copies, waits for them, and re-layouts: 38.6 us -> 11.2 us
  matrix products: 30.4 us -> 8.88 us
  Pallas kernels: 258 us -> 248 us
  other arithmetic: 26.9 us -> 17.1 us
    dot_general x5 -> x1, matrix products: 30.4 us -> 8.88 us  [dot(): return lax.dot_general(a, b, dims, preferred_element_type=f32)]
    reduce_scatter x1 -> x0, waiting for transfers between devices: 17.5 us -> none  [on_device(): lax.psum_scatter(out_parts, 'tensor', scatter_dimension=0, tiled=True)]
    unnamed x54 -> x42, local copies, waits for them, and re-layouts: 23.3 us -> 5.85 us
    pallas_call x1, Pallas kernels: 68.9 us -> 53.8 us  [mlp(): pl.pallas_call(mlp_kernel, in_specs=[hbm] * 3 + [vmem] + [hbm] * 3, out_s...]
    convert_element_type x5 -> x1, other arithmetic: 10.7 us -> 1.34 us  [on_device(): output = (out_own + landed.astype(f32)).astype(bf16)]
    all_gather x3, waiting for transfers between devices: 33.6 us -> 42.1 us  [gather(): return lax.all_gather(x, 'tensor', axis=0, tiled=True)]
    transpose x0 -> x2, other arithmetic: none -> 6.74 us  [the longest x1 3.49 us: on_device(): jnp.transpose(cat_sum.astype(f32).reshape(3, model_width, -1), (1, 0, 2))]
    all_to_all x1, waiting for transfers between devices: 20.3 us -> 25.2 us  [on_device(): lax.all_to_all(headed, 'tensor', split_axis=0, concat_axis=1, tiled=True)]
  transfers between devices with their start and end apart: 5 -> 4, of which waited for: 4 -> 3; matrix products, arithmetic and copies ran while one was open for 12% -> 3% of each run, Pallas kernels for 5% -> 6%
where the time goes in v4:
time: 378 us; the launch traced here: 372 us
  Pallas kernels  248 us (66%)
  waiting for transfers between devices  68.7 us (18%)
  other arithmetic  17.1 us (5%)
  between operations  14.1 us (4%)
  local copies, waits for them, and re-layouts  11.2 us (3%)
  matrix products  8.88 us (2%)
  starting transfers between devices  3.94 us (1%)
    pallas_call x1, Pallas kernels, backward(): pl.pallas_call(functools.partial(back_kernel, n_dp), grid=(n,), in_specs=...  172 us
    pallas_call x1, Pallas kernels, mlp(): pl.pallas_call(mlp_kernel, in_specs=[hbm] * 3 + [vmem] + [hbm] * 3, out_s...  53.8 us
    all_gather x3, waiting for transfers between devices, gather(): return lax.all_gather(x, 'tensor', axis=0, tiled=True)  42.1 us
    all_to_all x1, waiting for transfers between devices, on_device(): lax.all_to_all(headed, 'tensor', split_axis=0, concat_axis=1, tiled=True)  25.2 us
    pallas_call x1, Pallas kernels, mixer_fwd(): pl.pallas_call(mixer_fwd_kernel, grid_spec=pltpu.PrefetchScalarGridSpec(n...  21.7 us
    dot_general x1, matrix products, dot(): return lax.dot_general(a, b, dims, preferred_element_type=f32)  8.88 us
  transfers between devices with their start and end apart: 4, of which 3 were waited for; matrix products, arithmetic and copies ran while one was open for 3% of the time, Pallas kernels for 6%

profile of v4, /device:TPU:0, one launch (start us, length us, event | category | flops | bytes accessed | tf_op | source)
XLA Modules:
  0.0 371.8 jit_solution(8384055346888885625)
XLA Ops:
  7.2 0.0 all-gather.4.cloned.1.call-start
  7.2 0.7 convert_element_type.33
  7.9 0.0 copy-start.14
  7.9 1.5 fusion
  9.4 0.0 copy-start.16
  9.4 0.0 copy-start.15
  9.4 2.5 fusion.2
  12.0 0.0 copy-start.18
  12.0 0.0 copy-start.19
  12.0 0.0 copy-start.6
  12.0 0.0 all-gather.4.cloned.1.call-update
  12.0 0.0 copy-done.14
  12.0 0.0 all-gather.6.cloned.1.call-start
  12.1 0.7 all-gather.6.cloned.1.call-update
  12.8 0.0 all-gather.8.cloned.1.call-start
  12.8 0.7 all-gather.8.cloned.1.call-update
  13.5 0.0 copy-done.16
  13.5 0.2 copy.29
  13.7 0.0 copy-done.15
  13.7 0.0 copy-start.3
  13.8 0.1 pad.4.beta_hbm
  13.8 0.0 copy-start.11
  13.8 0.0 copy-done.18
  13.9 0.0 copy-done.19
  13.9 0.0 copy-start.4
  13.9 0.0 copy-start.5
  13.9 0.0 copy-done.6
  13.9 0.1 slice_bitcast_fusion.2
  14.1 35.3 %all-gather.4.cloned.1.call-done.attn_hbm = bf16[2048,1024]{1,0:T(8,128)(2,1)} async-done(((bf16[512,1024]{1,0:T(8,128)(2,1)}), bf16[2048,1024]{1,0:T(8,128)(2,1)}) %all-gather.4.cloned.1.call-update) | async-done | bytes 4194320 | tf_op jit(solution)/shard_map/all_gather | solution.py:859
  49.3 8.9 %fusion.3.proj_ref.prev_ref = f32[2048,896]{1,0:T(8,128)} fusion(bf16[2048,1024]{1,0:T(8,128)(2,1)} %all-gather.4.cloned.1.call-done.attn_hbm, bf16[1024,128]{1,0:T(8,128)(2,1)S(1)} %pad.4.beta_hbm, bf16[1024,256]{1,0:T(8,128)(2,1)S(1)} %get-tuple-element.63, bf16[1024,256]{1,0:T(8,128)(2,1)S(1)} %get-tuple-element.64, ...), kind=kOutput, calls=%fused_computation.8 | convolution fusion | flops 3765436416 | bytes 13369344 | tf_op jit(solution)/shard_map/dot_general | solution.py:863
  58.2 0.0 copy-done.3
  58.2 0.0 copy-done.11
  58.2 0.0 copy-done.4
  58.2 0.0 copy-done.5
  58.2 21.7 %shard_map.203 = (bf16[2048,256]{1,0:T(8,128)(2,1)}, f32[2048,256]{1,0:T(8,128)S(1)}, bf16[16,256,128]{2,1,0:T(8,128)(2,1)S(1)}, bf16[16,256,128]{2,1,0:T(8,128)...) custom-call(f32[40]{0:T(128)S(1)} %or_select_fusion.flags, f32[2048,896]{1,0:T(8,128)} %fusion.3.proj_ref.prev_ref, ...), custom_call_target="tpu_custom_call" | custom-call | tf_op jit(solution)/shard_map/pallas_call | solution.py:193
  79.9 0.0 copy-start
  79.9 1.3 copy-done
  81.3 0.0 copy-start.1
  81.3 1.0 copy-done.1
  82.2 1.0 copy-done.2
  83.2 3.8 %all-to-all-start = ((bf16[4,512,256]{2,1,0:T(8,128)(2,1)}), bf16[4,512,256]{2,1,0:T(8,128)(2,1)S(1)}, u32[]{:S(2)}, u32[]{:S(2)}) async-start(bf16[4,512,256]{2,1,0:T(8,128)(2,1)} %bitcast.7), calls=%async_computation | async-start | bytes 2097152 | tf_op jit(solution)/shard_map/all_to_all | solution.py:887
  87.1 0.0 copy-done.17
  87.1 0.6 broadcast_in_dim.31
  87.7 25.2 %all-to-all-done = bf16[4,512,256]{2,1,0:T(8,128)(2,1)S(1)} async-done(((bf16[4,512,256]{2,1,0:T(8,128)(2,1)}), bf16[4,512,256]{2,1,0:T(8,128)(2,1)S(1)}, u32[]{:S(2)}, u32[]{:S(2)}) %all-to-all-start) | async-done | bytes 1048608 | tf_op jit(solution)/shard_map/all_to_all | solution.py:887
  112.9 1.1 copy.31
  114.0 6.8 %all-gather.8.cloned.1.call-done.cot_hbm = bf16[2048,1024]{1,0:T(8,128)(2,1)} async-done(((bf16[512,1024]{1,0:T(8,128)(2,1)}), bf16[2048,1024]{1,0:T(8,128)(2,1)}) %all-gather.8.cloned.1.call-update) | async-done | bytes 4194320 | tf_op jit(solution)/shard_map/all_gather | solution.py:859
  120.8 53.8 %shard_map.204 = (f32[512,1024]{1,0:T(8,128)}, bf16[512,1024]{1,0:T(8,128)(2,1)}, f32[8,1024]{1,0:T(8,128)}, bf16[1408,1024]{1,0:T(8,128)(2,1)}, bf16[704,1024]{...) custom-call(bf16[512,1024]{1,0:T(8,128)(2,1)} %bitcast.43, ...), custom_call_target="tpu_custom_call" | custom-call | tf_op jit(solution)/shard_map/pallas_call | solution.py:415
  174.6 172.4 %shard_map.205 = (f32[512,1024]{1,0:T(8,128)}, f32[8,1024]{1,0:T(8,128)}, bf16[1408,1024]{1,0:T(8,128)(2,1)}, bf16[704,1024]{1,0:T(8,128)(2,1)}, bf16[3072,256]{...) custom-call(f32[40]{0:T(128)} %copy-done.4, f32[2048,896]{1,0:T(8,128)} %fusion.3.proj_ref.prev_ref, ...), custom_call_target="tpu_custom_call" | custom-call | tf_op jit(solution)/shard_map/pallas_call | solution.py:828
  347.1 1.5 fusion.12
  348.6 1.3 slice.37
  349.9 1.2 slice_bitcast_fusion.5
  351.1 3.5 convert_bitcast_fusion.1
  354.6 0.0 copy-done.13
  354.6 1.1 convert_element_type.39
  355.7 0.0 copy-done.7
  355.7 3.3 convert_bitcast_fusion
  358.9 0.0 copy-done.10
  358.9 1.9 convert_element_type.40
  360.9 0.3 copy-done.8
  361.2 0.7 copy-done.12
  361.8 1.3 add_convert_fusion
  363.2 0.6 pad_maximum_fusion
  363.8 0.0 copy-done.9
  363.8 1.3 copy.33
  (13 shorter events, 0.1 us)
Async XLA Ops:
  7.2 42.2 %all-gather.4.cloned.1.call-start = ((), (), s32[]{:S(2)}) async-start(), calls=%async_computation.1 | async-start | bytes 5242880 | tf_op jit(solution)/shard_map/all_gather | solution.py:859
  7.9 4.1 %copy-start.14 = (f32[1024]{0:T(1024)}, f32[1024]{0:T(1024)S(1)}, u32[]{:S(2)}) copy-start(f32[1024]{0:T(1024)S(1)} %convert_element_type.33) | copy-start | bytes 12292
  9.4 4.1 %copy-start.16 = (bf16[1024,2]{0,1:T(2,128)(2,1)S(1)}, bf16[1024,2]{0,1:T(2,128)(2,1)}, u32[]{:S(2)}) copy-start(bf16[1024,2]{0,1:T(2,128)(2,1)} %param.16) | copy-start | bytes 12292
  9.4 4.3 %copy-start.15 = (bf16[4,3,256]{2,0,1:T(4,128)(2,1)S(1)}, bf16[4,3,256]{2,0,1:T(4,128)(2,1)}, u32[]{:S(2)}) copy-start(bf16[4,3,256]{2,0,1:T(4,128)(2,1)} %param.17) | copy-start | bytes 18436
  12.0 1.9 copy-start.18
  12.0 1.9 copy-start.19
  12.0 2.0 copy-start.6
  12.0 102.0 %all-gather.6.cloned.1.call-start = ((), (), s32[]{:S(2)}) async-start(), calls=%async_computation.2 | async-start | bytes 2621440 | tf_op jit(solution)/shard_map/all_gather | solution.py:859
  12.8 108.1 %all-gather.8.cloned.1.call-start = ((), (), s32[]{:S(2)}) async-start(), calls=%async_computation.3 | async-start | bytes 5242880 | tf_op jit(solution)/shard_map/all_gather | solution.py:859
  13.7 44.5 %copy-start.3 = (f32[4,768]{1,0:T(4,128)}, f32[4,768]{1,0:T(4,128)S(1)}, u32[]{:S(2)}) copy-start(f32[4,768]{1,0:T(4,128)S(1)} %convert.7.conv_ref) | copy-start | bytes 36868
  13.8 44.4 %copy-start.11 = (bf16[1024,128]{1,0:T(8,128)(2,1)}, bf16[1024,128]{1,0:T(8,128)(2,1)S(1)}, u32[]{:S(2)}) copy-start(bf16[1024,128]{1,0:T(8,128)(2,1)S(1)} %pad.4.beta_hbm) | copy-start | bytes 786436
  13.9 44.3 %copy-start.4 = (f32[40]{0:T(128)}, f32[40]{0:T(128)S(1)}, u32[]{:S(2)}) copy-start(f32[40]{0:T(128)S(1)} %or_select_fusion.flags) | copy-start | bytes 484
  13.9 44.3 %copy-start.5 = (f32[1,128]{1,0:T(1,128)}, f32[1,128]{1,0:T(1,128)S(1)}, u32[]{:S(2)}) copy-start(f32[1,128]{1,0:T(1,128)S(1)} %bitcast_convert_fusion.gain_ref) | copy-start | bytes 1540
  79.9 1.3 copy-start
  81.3 1.0 copy-start.1
  82.2 1.0 copy-start.2
  83.2 3.8 %copy-start.17 = (bf16[1024]{0:T(1024)(128)(2,1)S(1)}, bf16[1024]{0:T(1024)(128)(2,1)}, u32[]{:S(2)}) copy-start(bf16[1024]{0:T(1024)(128)(2,1)} %param.20) | copy-start | bytes 6148
  83.2 29.6 %all-to-all-start = ((bf16[4,512,256]{2,1,0:T(8,128)(2,1)}), bf16[4,512,256]{2,1,0:T(8,128)(2,1)S(1)}, u32[]{:S(2)}, u32[]{:S(2)}) async-start(bf16[4,512,256]{2,1,0:T(8,128)(2,1)} %bitcast.7), calls=%async_computation | async-start | bytes 2097152 | tf_op jit(solution)/shard_map/all_to_all | solution.py:887
  351.1 3.5 copy-start.13
  351.1 4.6 %copy-start.7 = (bf16[1408,1024]{1,0:T(8,128)(2,1)S(1)}, bf16[1408,1024]{1,0:T(8,128)(2,1)}, u32[]{:S(2)}) copy-start(bf16[1408,1024]{1,0:T(8,128)(2,1)} %get-tuple-element.49) | copy-start | bytes 8650756
  355.7 3.3 copy-start.10
  358.9 2.2 copy-start.8
  358.9 2.9 copy-start.12
  361.8 2.0 copy-start.9
Sparse Core Ops, SparseCore 0:
  12.1 37.1 all-gather.3
  50.9 22.5 all-gather.5
  75.1 45.7 all-gather.7

commit v5 on v4

--- a/solution.py
+++ b/solution.py
@@ -120,15 +120,37 @@
     return jnp.concatenate(out, axis=0), grads
 
 
-def mixer_fwd_kernel(flags, proj_ref, conv_ref, gain_ref, headed_ref, mixed_ref, state_out, res_out, wu_out, inv_out, state, buf):
-    g = pl.program_id(0)
-
-    @pl.when(g == 0)
-    def _():
-        state[...] = jnp.zeros_like(state)
-        buf[0:8, :] = jnp.zeros((8, buf.shape[1]), f32)
-
-    width = buf.shape[1]
+MESH_ID = pl.DeviceIdType.MESH
+HALF = 2
+
+
+def places():
+    d = lax.axis_index("dp")
+    t = lax.axis_index("tensor")
+    beside = t + 1 - 2 * lax.rem(t, 2)
+    across = lax.rem(t + 2, 4)
+    corner = lax.rem(beside + 2, 4)
+    return d, t, beside, across, corner
+
+
+def push(src, dst, send, recv, device):
+    copy = pltpu.make_async_remote_copy(src_ref=src, dst_ref=dst, send_sem=send, recv_sem=recv, device_id=device, device_id_type=MESH_ID)
+    copy.start()
+    return copy
+
+
+def greet(devices):
+    barrier = pltpu.get_barrier_semaphore()
+    for device in devices:
+        pl.semaphore_signal(barrier, inc=1, device_id=device, device_id_type=MESH_ID)
+    pl.semaphore_wait(barrier, len(devices))
+
+
+def row_block(owner, part, owner_rows, part_rows):
+    return pl.ds(pl.multiple_of(owner * owner_rows + part * part_rows, part_rows), part_rows)
+
+
+def mixer_fwd_block(g, width, flags, proj_ref, conv_ref, gain_ref, headed_ref, mixed_ref, state_out, res_out, wu_out, inv_out, state, buf):
     buf[8:, :] = proj_ref[:, :width]
     heads, _ = span_masks(flags, g * (ROWS // SPAN), ROWS // SPAN)
     cols = []
@@ -180,63 +202,225 @@
         o = jnp.concatenate(qs, axis=0) + mm(p, res)
         mixed_ref[rs, :] = unstack(o)
         headed = o * lax.rsqrt(jnp.mean(o * o, axis=-1, keepdims=True) + 1e-5) * gain_ref[...]
-        headed_ref[rs, :] = unstack(headed).astype(bf16)
+        headed_ref[g, rs, :] = unstack(headed).astype(bf16)
     state[0] = mem[0]
     state[1] = mem[1]
 
 
-def mixer_fwd(flags, proj, conv, gain):
-    rows, total = proj.shape
-    width = conv.shape[1]
-    n = rows // ROWS
-    steps = rows // STEP
+def param_views(params, width):
+    return params.at[0:1, :], params.at[1:2, :], params.at[2:3, :HEAD], params.at[3:7, :width]
+
+
+class Gather:
+    def __init__(self, full, rows, send, recv):
+        self.full, self.rows, self.send, self.recv = full, rows, send, recv
+        self.d, self.t, self.beside, self.across, _ = places()
+        self.core = lax.rem(self.t, 2)
+        self.base = self.t - self.core
+        self.far = lax.rem(self.base + 2, 4)
+
+    def block(self, owner, h):
+        part = self.rows // 2
+        return self.full.at[pl.ds(pl.multiple_of(owner * self.rows + h * part, part), part)]
+
+    def copy(self, owner, h, i, j, peer):
+        block = self.block(owner, h)
+        return pltpu.make_async_remote_copy(src_ref=block, dst_ref=block, send_sem=self.send.at[i, j], recv_sem=self.recv.at[i, j], device_id=(self.d, peer), device_id_type=MESH_ID)
+
+    def near(self, h):
+        return self.copy(self.t, h, 0, h, self.beside)
+
+    def over(self, i):
+        return self.copy(self.base + i, self.core, 1, i, self.across)
+
+    def passed(self, i):
+        return self.copy(self.far + i, self.core, 2, i, self.beside)
+
+    def start_near(self):
+        self.near(0).start()
+        self.near(1).start()
+
+    def start_over(self, first=0):
+        @pl.when(self.core == first)
+        def _():
+            self.over(first).start()
+
+        self.near(self.core).wait_recv()
+
+        @pl.when(self.core != first)
+        def _():
+            self.over(first).start()
+
+        self.over(1 - first).start()
+
+    def fetch_near(self):
+        self.near(1 - self.core).wait_recv()
+
+    def fetch_over(self, i):
+        self.over(i).wait_recv()
+        self.passed(i).start()
+
+    def sent(self):
+        for i in range(2):
+            self.near(i).wait_send()
+            self.over(i).wait_send()
+            self.passed(i).wait_send()
+
+
+def front_kernel(flags, params, tok_hbm, qkv_hbm, beta_hbm, outw_hbm, cot_hbm,
+                 proj_ref, mixed_ref, state_out, res_out, wu_out, inv_out, attn_out, headed_out, heads_hbm, out_hbm, cots_hbm,
+                 w, beta_w, tok, attn, headed, out_all, cot_all, state, buf, load, store, send_r, recv_r, send_w, recv_w, send_c, recv_c, send_h, recv_h):
+    g = pl.program_id(0)
+    n = pl.num_programs(0)
+    d, t, beside, across, corner = places()
+    rows = tok.shape[0]
+    width = buf.shape[1]
+    heads = 2 * HEAD
+    first_gain, _, gain_ref, conv_ref = param_views(params, width)
+    rowset = Gather(attn, rows, send_r, recv_r)
+    weights = Gather(out_all, outw_hbm.shape[0], send_w, recv_w)
+    cots = Gather(cot_all, rows, send_c, recv_c)
+    loads = [(tok_hbm, tok)] + [(qkv_hbm.at[i], w.at[:, pl.ds(i * heads, heads)]) for i in range(3)] + [(beta_hbm, beta_w)]
+    loads += [(outw_hbm, out_all.at[pl.ds(pl.multiple_of(t * outw_hbm.shape[0], 16), outw_hbm.shape[0])]), (cot_hbm, cot_all.at[pl.ds(pl.multiple_of(t * rows, rows), rows)])]
+
+    def loaded(i):
+        return pltpu.make_async_copy(loads[i][0], loads[i][1], load.at[i])
+
+    def attn_stored():
+        return pltpu.make_async_copy(attn, attn_out, store.at[0])
+
+    def head_place(owner):
+        return heads_hbm.at[:, pl.ds(pl.multiple_of(owner * heads, heads), heads)]
+
+    def kept(i):
+        return pltpu.make_async_copy(headed.at[i], headed_out.at[pl.ds(i * rows, rows)], store.at[1 + i])
+
+    def own_heads():
+        return pltpu.make_async_copy(headed.at[t], head_place(t), store.at[1 + n_groups])
+
+    def gathered(i):
+        return pltpu.make_async_copy((out_all, cot_all)[i], (out_hbm, cots_hbm)[i], store.at[2 + n_groups + i])
+
+    n_groups = headed.shape[0]
+
+    def heads_to(owner, sender):
+        return pltpu.make_async_remote_copy(src_ref=headed.at[owner], dst_ref=head_place(sender), send_sem=send_h.at[owner], recv_sem=recv_h.at[sender], device_id=(d, owner), device_id_type=MESH_ID)
+
+    @pl.when(g == 0)
+    def _():
+        for i in range(len(loads)):
+            loaded(i).start()
+        greet([(d, beside), (d, across), (d, corner)])
+        loaded(0).wait()
+        piece = 64
+        gain = first_gain[...]
+
+        def chunk(i, carry):
+            x = tok[pl.ds(pl.multiple_of(i * piece, piece), piece), :].astype(f32)
+            attn[pl.ds(pl.multiple_of(t * rows + i * piece, piece), piece), :] = (x * lax.rsqrt(jnp.mean(x * x, axis=-1, keepdims=True) + 1e-5) * gain).astype(bf16)
+            return carry
+
+        lax.fori_loop(0, rows // piece, chunk, 0)
+        rowset.start_near()
+        rowset.start_over()
+        state[...] = jnp.zeros_like(state)
+        buf[0:8, :] = jnp.zeros((8, width), f32)
+        for i in range(1, len(loads)):
+            loaded(i).wait()
+        weights.start_near()
+        cots.start_near()
+
+    @pl.when(g == beside)
+    def _():
+        rowset.fetch_near()
+
+    @pl.when(g // 2 != t // 2)
+    def _():
+        i = lax.rem(g, 2)
+        rowset.fetch_over(i)
+        rowset.passed(i).wait_recv()
+
+    @pl.when(g == 2 - t // 2)
+    def _():
+        weights.start_over()
+        cots.start_over()
+
+    @pl.when(g == n - 1)
+    def _():
+        attn_stored().start()
+
+    now = attn[pl.ds(pl.multiple_of(g * rows, rows), rows), :]
+    proj_ref[:, :width] = lax.dot_general(now, w[...], NN, preferred_element_type=f32)
+    proj_ref[:, width:] = jnp.zeros((rows, HEAD), f32)
+    proj_ref[:, width:width + 16] = lax.dot_general(now, beta_w[...], NT, preferred_element_type=f32)
+    mixer_fwd_block(g, width, flags, proj_ref, conv_ref, gain_ref, headed, mixed_ref, state_out, res_out, wu_out, inv_out, state, buf)
+
+    @pl.when(g != t)
+    def _():
+        heads_to(g, t).start()
+
+    @pl.when(g == t)
+    def _():
+        own_heads().start()
+
+    @pl.when(g == n - 1)
+    def _():
+        for i in range(n_groups):
+            kept(i).start()
+        for gather in (weights, cots):
+            gather.fetch_near()
+            for i in range(2):
+                gather.fetch_over(i)
+        for gather in (weights, cots):
+            for i in range(2):
+                gather.passed(i).wait_recv()
+        gathered(0).start()
+        gathered(1).start()
+        for k in range(1, n_groups):
+            other = lax.rem(t + k, n_groups)
+            heads_to(other, t).wait_send()
+            heads_to(other, other).wait_recv()
+        for gather in (rowset, weights, cots):
+            gather.sent()
+        gathered(0).wait()
+        gathered(1).wait()
+        own_heads().wait()
+        attn_stored().wait()
+        for i in range(n_groups):
+            kept(i).wait()
+
+
+def front(flags, params, tokens, qkv, beta, out_weight, cot):
+    rows, model = tokens.shape
+    groups = 4
+    total_rows = rows * groups
+    width = 3 * qkv.shape[2]
+    total = width + HEAD
+    steps = total_rows // STEP
+    hbm = pl.BlockSpec(memory_space=pl.ANY)
+    z2 = lambda g: (0, 0)
+    m2 = lambda g: (g, 0)
+    m3 = lambda g: (g, 0, 0)
+    dma = pltpu.SemaphoreType.DMA
+    out = lambda shape, kind: jax.ShapeDtypeStruct(shape, kind)
+    heads = 2 * HEAD
     return pl.pallas_call(
-        mixer_fwd_kernel,
-        grid_spec=pltpu.PrefetchScalarGridSpec(
-            num_scalar_prefetch=1, grid=(n,),
-            in_specs=[pl.BlockSpec((ROWS, total), lambda g, f: (g, 0)), pl.BlockSpec((4, width), lambda g, f: (0, 0)), pl.BlockSpec((1, HEAD), lambda g, f: (0, 0))],
-            out_specs=[pl.BlockSpec((ROWS, 2 * HEAD), lambda g, f: (g, 0)), pl.BlockSpec((ROWS, 2 * HEAD), lambda g, f: (g, 0)),
-                       pl.BlockSpec((STEPS, 2 * HEAD, HEAD), lambda g, f: (g, 0, 0)), pl.BlockSpec((STEPS, 2 * STEP, HEAD), lambda g, f: (g, 0, 0)),
-                       pl.BlockSpec((STEPS, 2 * STEP, 2 * HEAD), lambda g, f: (g, 0, 0)), pl.BlockSpec((STEPS, 2 * STEP, 2 * STEP), lambda g, f: (g, 0, 0))],
-            scratch_shapes=[pltpu.VMEM((2, HEAD, HEAD), f32), pltpu.VMEM((ROWS + 8, width), f32)]),
-        out_shape=[jax.ShapeDtypeStruct((rows, 2 * HEAD), bf16), jax.ShapeDtypeStruct((rows, 2 * HEAD), f32),
-                   jax.ShapeDtypeStruct((steps, 2 * HEAD, HEAD), bf16), jax.ShapeDtypeStruct((steps, 2 * STEP, HEAD), bf16),
-                   jax.ShapeDtypeStruct((steps, 2 * STEP, 2 * HEAD), bf16), jax.ShapeDtypeStruct((steps, 2 * STEP, 2 * STEP), bf16)],
-        compiler_params=pltpu.CompilerParams(dimension_semantics=("arbitrary",), vmem_limit_bytes=48 * 2**20),
-    )(flags, proj, conv, gain)
-
-
-MESH_ID = pl.DeviceIdType.MESH
-HALF = 2
-
-
-def places():
-    d = lax.axis_index("dp")
-    t = lax.axis_index("tensor")
-    beside = t + 1 - 2 * lax.rem(t, 2)
-    across = lax.rem(t + 2, 4)
-    corner = lax.rem(beside + 2, 4)
-    return d, t, beside, across, corner
-
-
-def push(src, dst, send, recv, device):
-    copy = pltpu.make_async_remote_copy(src_ref=src, dst_ref=dst, send_sem=send, recv_sem=recv, device_id=device, device_id_type=MESH_ID)
-    copy.start()
-    return copy
-
-
-def greet(devices):
-    barrier = pltpu.get_barrier_semaphore()
-    for device in devices:
-        pl.semaphore_signal(barrier, inc=1, device_id=device, device_id_type=MESH_ID)
-    pl.semaphore_wait(barrier, len(devices))
-
-
-def row_block(owner, part, owner_rows, part_rows):
-    return pl.ds(pl.multiple_of(owner * owner_rows + part * part_rows, part_rows), part_rows)
-
-
-def mlp_kernel(headed_hbm, out_hbm, tok_hbm, gain_ref, gu_hbm, down_hbm, cot_hbm,
+        front_kernel,
+        grid=(groups,),
+        in_specs=[pl.BlockSpec(memory_space=pltpu.SMEM), pl.BlockSpec(params.shape, z2)] + [hbm] * 5,
+        out_specs=[pl.BlockSpec((ROWS, total), m2), pl.BlockSpec((ROWS, heads), m2), pl.BlockSpec((STEPS, heads, HEAD), m3), pl.BlockSpec((STEPS, 2 * STEP, HEAD), m3),
+                   pl.BlockSpec((STEPS, 2 * STEP, heads), m3), pl.BlockSpec((STEPS, 2 * STEP, 2 * STEP), m3)] + [hbm] * 5,
+        out_shape=[out((total_rows, total), f32), out((total_rows, heads), f32), out((steps, heads, HEAD), bf16), out((steps, 2 * STEP, HEAD), bf16),
+                   out((steps, 2 * STEP, heads), bf16), out((steps, 2 * STEP, 2 * STEP), bf16), out((total_rows, model), bf16), out((total_rows, heads), bf16),
+                   out((rows, model), bf16), out((groups * out_weight.shape[0], model), bf16), out((total_rows, model), bf16)],
+        scratch_shapes=[pltpu.VMEM((model, width), bf16), pltpu.VMEM(beta.shape, bf16), pltpu.VMEM((rows, model), bf16), pltpu.VMEM((total_rows, model), bf16), pltpu.VMEM((groups, rows, heads), bf16),
+                        pltpu.VMEM((groups * out_weight.shape[0], model), bf16), pltpu.VMEM((total_rows, model), bf16), pltpu.VMEM((2, HEAD, HEAD), f32), pltpu.VMEM((ROWS + 8, width), f32), dma((7,)), dma((4 + groups,))]
+        + [dma((3, 2))] * 6 + [dma((groups,))] * 2,
+        compiler_params=pltpu.CompilerParams(dimension_semantics=("arbitrary",), collective_id=3, has_side_effects=True, vmem_limit_bytes=56 * 2**20),
+    )(flags, params, tokens, qkv, beta, out_weight, cot)
+
+
+def mlp_kernel(headed_hbm, out_hbm, tok_hbm, params, gu_hbm, down_hbm, cot_hbm,
                dhid_hbm, dattn_hbm, gain_out, gu_out, downg_out, own_hbm, across_hbm,
                headed, out_w, tok, gu_w, down_w, cot, hidden, all_rows, act, d_gate, d_up, mine, keep, to_beside, from_beside, to_across, from_across, to_own, from_own,
                out_own, out_keep, from_beside_out, from_own_out, gu_acc, down_acc, gu_sum, down_sum, dattn, load, store, send, recv):
@@ -287,7 +471,7 @@
     greet([(d, beside), (d, across)])
     for i in range(3):
         loaded(i).wait()
-    gain = gain_ref[...]
+    gain = params[1:2, :]
     for s in range(HALF):
         at = pl.ds(s * part, part)
         x = tok[at, :].astype(f32) + lax.dot_general(headed[at, :], out_w[...], NN, preferred_element_type=f32)
@@ -517,6 +701,7 @@
     def __init__(self, here, after, before, sources, results, lands, by_rows, send, recv):
         self.here, self.targets = here, (after, before)
         self.sources, self.results, self.lands, self.by_rows, self.send, self.recv = sources, results, lands, by_rows, send, recv
+        self.visited = 0
 
     def shard(self, way, k):
         return lax.rem(self.here + (k if way else 2 * RING - k), RING)
@@ -539,8 +724,12 @@
             src = dst = self.view(self.results[i], i, way, r)
         return pltpu.make_async_remote_copy(src_ref=src, dst_ref=dst, send_sem=self.send.at[i, way], recv_sem=self.recv.at[i, way, r], device_id=self.targets[way], device_id_type=MESH_ID)
 
-    def round(self, r):
-        for i in range(len(self.sources)):
+    def visit(self, count):
+        for _ in range(count):
+            if self.visited == len(self.sources) * (ROUNDS + 1):
+                return
+            r, i = divmod(self.visited, len(self.sources))
+            self.visited += 1
             for way in range(2):
                 if r > 0:
                     last = self.copy(i, way, r - 1)
@@ -575,14 +764,14 @@
     return [pltpu.VMEM((2, RING - 1) + p, bf16) for p in pieces]
 
 
-def back_kernel(n_dp, flags, proj_ref, prev_ref, conv_ref, gain_ref, mixed_ref, state_in, res_in, wu_in, inv_in,
-                headed_hbm, attn_hbm, dattn_hbm, out_w_hbm, qkv_hbm, beta_hbm, tok_hbm, dhid_hbm, first_gain, second_grad, gu_hbm, down_hbm, across_hbm,
-                dx_hbm, small_out, gu_out, down_out, cat_out, outw_out, landed_hbm,
-                headed, attn, dattn_all, out_w, w, tok, dhid, gu_src, down_src, cat_src, outw_src,
-                gu_res, down_res, cat_res, outw_res, gate_land, up_land, down_land, cat_land, outw_land,
+def back_kernel(n_dp, flags, proj_ref, prev_ref, params, mixed_ref, state_in, res_in, wu_in, inv_in,
+                headed_hbm, attn_hbm, dattn_hbm, out_w_hbm, qkv_hbm, beta_hbm, tok_hbm, dhid_hbm, second_grad, gu_hbm, down_hbm, own_hbm, across_hbm,
+                dx_hbm, small_out, output_hbm, gu_out, down_out, cat_out, outw_out, landed_hbm,
+                headed, attn, dattn_all, out_w, w, beta_w, tok, dhid, gu_src, down_src, cat_src, outw_src,
+                gu_res, down_res, cat_res, outw_res, gate_land, up_land, down_land, q_land, k_land, v_land, outw_land,
                 dheaded, dcat, dstate, buf, dbuf, cacc, gacc, mine, to_beside, from_beside, to_across, from_across, to_own, from_own,
                 group_send, group_land, all_send, all_land, gain_acc, beta_grad,
-                load, store, send_m, recv_m, send_c, recv_c, send_x, recv_x, send_g, recv_g, send_a, recv_a):
+                load, store, send_m, recv_m, send_c, recv_c, send_r, recv_r, send_x, recv_x, send_g, recv_g, send_a, recv_a, late_sem):
     g = pl.program_id(0)
     n = pl.num_programs(0)
     d, t, beside, across, corner = places()
@@ -591,13 +780,17 @@
     part = rows // HALF
     width = buf.shape[1]
     others = [d // RING * RING + lax.rem(d + k, RING) for k in range(1, RING)]
+    first_gain, _, gain_ref, conv_ref = param_views(params, width)
     units = down_src.shape[0]
     gate_up = lambda ref: [ref.at[pl.ds(0, units)], ref.at[pl.ds(units, units)]]
     mlp_ring = Ring(here, (after, t), (before, t), gate_up(gu_src) + [down_src], gate_up(gu_res) + [down_res], [gate_land, up_land, down_land], [False] * 3, send_m, recv_m)
-    cat_ring = Ring(here, (after, t), (before, t), [cat_src, outw_src], [cat_res, outw_res], [cat_land, outw_land], [True, True], send_c, recv_c)
-    loads = [(gu_hbm, gu_src), (down_hbm, down_src), (dattn_hbm, dattn_all.at[pl.ds(pl.multiple_of(t * rows, rows), rows)]), (out_w_hbm, out_w), (headed_hbm, headed), (attn_hbm, attn), (tok_hbm, tok), (dhid_hbm, dhid), (beta_hbm, w.at[:, pl.ds(width, HEAD)])]
+    model = tok.shape[1]
+    thirds = lambda ref: [ref.at[pl.ds(i * model, model)] for i in range(3)]
+    cat_ring = Ring(here, (after, t), (before, t), thirds(cat_src) + [outw_src], thirds(cat_res) + [outw_res], [q_land, k_land, v_land, outw_land], [True] * 4, send_c, recv_c)
+    rowset = Gather(dattn_all, rows, send_r, recv_r)
+    loads = [(gu_hbm, gu_src), (down_hbm, down_src), (dattn_hbm, dattn_all.at[pl.ds(pl.multiple_of(t * rows, rows), rows)]), (out_w_hbm, out_w), (headed_hbm, headed), (attn_hbm, attn), (tok_hbm, tok), (dhid_hbm, dhid), (beta_hbm, beta_w)]
     loads += [(qkv_hbm.at[i], w.at[:, pl.ds(i * 2 * HEAD, 2 * HEAD)]) for i in range(3)]
-    stores = [(gu_res, gu_out), (down_res, down_out), (mine, dx_hbm), (cat_res, cat_out), (outw_res, outw_out)]
+    stores = [(gu_res, gu_out), (down_res, down_out), (mine, dx_hbm), (cat_res, cat_out), (outw_res, outw_out), (to_own, output_hbm)]
 
     def loaded(i):
         return pltpu.make_async_copy(loads[i][0], loads[i][1], load.at[i])
@@ -613,67 +806,63 @@
 
     def block_at(owner, s):
         return row_block(owner, s, rows, part)
-
-    def rows_to(i, s, peer):
-        block = dattn_all.at[block_at(t, s)]
-        return pushed(block, block, i, s, peer)
-
-    def passed(s):
-        block = dattn_all.at[block_at(across, s)]
-        return pushed(block, block, 2, s, beside)
-
-    def head_grad(owner, s):
-        at = block_at(owner, s)
-        dheaded[at, :] = lax.dot_general(dattn_all[at, :], out_w[...], NT, preferred_element_type=f32).astype(bf16)
 
     @pl.when(g == 0)
     def _():
         for i in range(len(loads)):
             loaded(i).start()
         greet([(d, beside), (d, across), (d, corner)] + [(o, t) for o in others])
-        for i in range(3):
-            loaded(i).wait()
-        for s in range(HALF):
-            rows_to(0, s, across).start()
-            rows_to(1, s, beside).start()
-        mlp_ring.round(0)
-        loaded(3).wait()
+        loaded(2).wait()
+        rowset.start_near()
+        loaded(0).wait()
+        loaded(1).wait()
+        mlp_ring.visit(3)
+        rowset.start_over(1)
         dstate[...] = jnp.zeros_like(dstate)
         dbuf[BACK_ROWS:, :] = jnp.zeros((8, width), f32)
         cacc[...] = jnp.zeros_like(cacc)
         gacc[...] = jnp.zeros_like(gacc)
         gain_acc[...] = jnp.zeros_like(gain_acc)
-        for s in range(HALF):
-            head_grad(t, s)
-        for s in range(HALF):
-            rows_to(1, s, beside).wait_recv()
-            head_grad(beside, s)
-        mlp_ring.round(1)
-        rows_to(0, 0, across).wait_recv()
-        passed(0).start()
-        head_grad(across, 0)
-        mlp_ring.round(2)
-        passed(0).wait_recv()
-        head_grad(corner, 0)
-        mlp_ring.round(3)
-        rows_to(0, 1, across).wait_recv()
-        passed(1).start()
-        head_grad(across, 1)
-        passed(1).wait_recv()
-        head_grad(corner, 1)
-        outward().start()
-        mlp_ring.round(4)
-
-    for at, r in ((1, 5), (3, 6), (5, 7), (6, 8)):
-        @pl.when(g == at)
-        def _(r=r):
-            mlp_ring.round(r)
+        loaded(3).wait()
+        mlp_ring.visit(5)
+
+        @pl.when(t < 2)
+        def _():
+            rowset.fetch_over(1)
+
+        mlp_ring.visit(1)
+
+    owner = n // 2 - 1 - g // 2
+    for k in range(1, n):
+        @pl.when(g == k)
+        def _(k=k):
+            if k == 3:
+                outward().start()
+            mlp_ring.visit(2)
+
+    @pl.when((lax.rem(g, 2) == 1) & (g < n - 1) & ((owner - 1) // 2 != t // 2))
+    def _():
+        rowset.fetch_over(lax.rem(owner + 1, 2))
+
+    @pl.when(lax.rem(g, 2) == 0)
+    def _():
+        @pl.when(owner == beside)
+        def _():
+            rowset.fetch_near()
+
+        @pl.when(owner // 2 != t // 2)
+        def _():
+            rowset.passed(lax.rem(owner, 2)).wait_recv()
+
+        at = pl.ds(pl.multiple_of(owner * rows, rows), rows)
+        dheaded[at, :] = lax.dot_general(dattn_all[at, :], out_w[...], NT, preferred_element_type=f32).astype(bf16)
 
     blk = n - 1 - g
     mixer_bwd_block(blk, width, flags, proj_ref, prev_ref, conv_ref, gain_ref, mixed_ref, state_in, res_in, wu_in, inv_in, dheaded, dcat, dstate, buf, dbuf, cacc, gacc)
 
     def work(owner, s):
-        return lax.dot_general(dcat[block_at(owner, s), :], w[...], NT, preferred_element_type=f32)
+        at = block_at(owner, s)
+        return lax.dot_general(dcat[at, :width], w[...], NT, preferred_element_type=f32) + lax.dot_general(dcat[at, width:width + 16], beta_w[...], NN, preferred_element_type=f32)
 
     def handed(s):
         at = pl.ds(s * part, part)
@@ -714,22 +903,21 @@
     def _():
         for i in range(4, len(loads)):
             loaded(i).wait()
-        mlp_ring.round(9)
 
         def cat_chunk(i):
             grad = lax.dot_general(attn[:, i * 256:(i + 1) * 256], dcat[:, :width], TN, preferred_element_type=f32).astype(bf16)
             for j in range(3):
                 cat_src[pl.ds(j * attn.shape[1] + i * 256, 256), :] = grad[:, j * 2 * HEAD:(j + 1) * 2 * HEAD]
 
-        count = attn.shape[1] // 256
-        for i in range(count):
+        def turn():
+            mlp_ring.visit(1)
+            cat_ring.visit(4)
+
+        for i in range(attn.shape[1] // 256):
             cat_chunk(i)
-            if i == count // 2 - 1:
-                mlp_ring.round(10)
-        beta_grad[...] = lax.dot_general(dcat[:, width:], attn[...], TN, preferred_element_type=f32)[:8]
+            mlp_ring.visit(1)
         outw_src[...] = lax.dot_general(headed[...], dattn_all[...], TN, preferred_element_type=f32).astype(bf16)
-        cat_ring.round(0)
-        mlp_ring.round(11)
+        cat_ring.visit(4)
         for s in range(HALF):
             at = pl.ds(s * part, part)
             to_beside[at, :] = work(corner, s).astype(bf16)
@@ -738,31 +926,42 @@
             handed(s).wait_recv()
             to_across[at, :] = (total + from_beside[at, :].astype(f32)).astype(bf16)
             summed(s).start()
-        cat_ring.round(1)
-        mlp_ring.round(12)
+            turn()
+        beta_grad[...] = lax.dot_general(dcat[:, width:width + 16], attn[...], TN, preferred_element_type=f32)[:8]
         for s in range(HALF):
             at = pl.ds(s * part, part)
             to_own[at, :] = work(beside, s).astype(bf16)
             owned(s).start()
             mine[at, :] = work(t, s)
-        cat_ring.round(2)
-        mlp_ring.round(13)
-        cat_ring.round(3)
-        cat_ring.round(4)
-        mlp_ring.round(14)
-        for i in range(2):
-            stored(i).start()
-        cat_ring.round(5)
+            turn()
+        turn()
         owned(0).wait_recv()
         summed(0).wait_recv()
         finish(0)
-        cat_ring.round(6)
-        cat_ring.round(7)
+        turn()
+        turn()
         owned(1).wait_recv()
         summed(1).wait_recv()
         finish(1)
         stored(2).start()
-        cat_ring.round(8)
+        for i, copy in enumerate((handed, summed, owned)):
+            for s in range(HALF):
+                copy(s).wait_send()
+        outward().wait_recv()
+        late = [pltpu.make_async_copy(own_hbm, dhid, late_sem.at[0]), pltpu.make_async_copy(landed_hbm, to_across, late_sem.at[1])]
+        for copy in late:
+            copy.start()
+        turn()
+        for copy in late:
+            copy.wait()
+
+        def add(i, carry):
+            at = pl.ds(pl.multiple_of(i * piece, piece), piece)
+            to_own[at, :] = (dhid[at, :] + to_across[at, :].astype(f32)).astype(bf16)
+            return carry
+
+        lax.fori_loop(0, rows // piece, add, 0)
+        stored(5).start()
         line = lax.broadcasted_iota(jnp.int32, small_out.shape, 0)
         lane = lax.broadcasted_iota(jnp.int32, small_out.shape, 1)
         shared = (line < 2) | ((line == 3) & (lane >= width))
@@ -776,7 +975,7 @@
             group_send[3 + j:4 + j, :width] = jnp.sum(cacc[j], axis=0, keepdims=True)
         for i, peer in enumerate((beside, across, corner)):
             grouped(i, peer).start()
-        cat_ring.round(9)
+        turn()
         small = group_send[...]
         for i, peer in enumerate((beside, across, corner)):
             grouped(i, peer).wait_recv()
@@ -785,33 +984,32 @@
         all_send[...] = small
         for i, o in enumerate(others):
             spread(i, o).start()
-        cat_ring.round(10)
-        cat_ring.round(11)
+        turn()
+        turn()
         for i, o in enumerate(others):
             spread(i, o).wait_recv()
             small = small + all_land[i]
         small_out[...] = small
-        cat_ring.round(12)
-        cat_ring.round(13)
-        cat_ring.round(14)
+        for _ in range(ROUNDS):
+            turn()
+        for i in range(2):
+            stored(i).start()
         for i in range(3, 5):
             stored(i).start()
-        for s in range(HALF):
-            for copy in (rows_to(0, s, across), rows_to(1, s, beside), passed(s), handed(s), summed(s), owned(s)):
-                copy.wait_send()
+        rowset.sent()
         for i, peer in enumerate((beside, across, corner)):
             grouped(i, peer).wait_send()
         for i, o in enumerate(others):
             spread(i, o).wait_send()
-        outward().wait()
+        outward().wait_send()
         for i in range(len(stores)):
             stored(i).wait()
 
 
-def backward(n_dp, flags, proj, conv, gain, saved, headed, attn_all, d_attn, out_w, qkv, beta, tokens, d_hidden, first_gain, second_grad, gu_part, down_part, out_across):
+def backward(n_dp, flags, proj, params, saved, headed, attn_all, d_attn, out_w, qkv, beta, tokens, d_hidden, second_grad, gu_part, down_part, out_own, out_across):
     mixed, states, res, wu, inv = saved
     total_rows, total = proj.shape
-    width = conv.shape[1]
+    width = 3 * qkv.shape[2]
     rows, model = tokens.shape
     n = total_rows // BACK_ROWS
     m2 = lambda g: (n - 1 - g, 0)
@@ -830,37 +1028,24 @@
         grid=(n,),
         in_specs=[pl.BlockSpec(memory_space=pltpu.SMEM), pl.BlockSpec((BACK_ROWS, total), m2),
                   pl.BlockSpec((8, total), lambda g: (jnp.maximum((n - 1 - g) * (BACK_ROWS // 8) - 1, 0), 0)),
-                  pl.BlockSpec((4, width), z2), pl.BlockSpec((1, HEAD), z2), pl.BlockSpec((BACK_ROWS, 2 * HEAD), m2),
+                  pl.BlockSpec(params.shape, z2), pl.BlockSpec((BACK_ROWS, 2 * HEAD), m2),
                   pl.BlockSpec((BACK_STEPS, 2 * HEAD, HEAD), m3), pl.BlockSpec((BACK_STEPS, 2 * STEP, HEAD), m3),
                   pl.BlockSpec((BACK_STEPS, 2 * STEP, 2 * HEAD), m3), pl.BlockSpec((BACK_STEPS, 2 * STEP, 2 * STEP), m3)]
-        + [hbm] * 8 + [pl.BlockSpec((1, model), z2), pl.BlockSpec(line, z2)] + [hbm] * 3,
-        out_specs=[hbm, pl.BlockSpec(line, z2)] + [hbm] * 5,
-        out_shape=[out((rows, model), f32), out(line, f32)] + [out(x.shape, bf16) for x in mlp_parts] + [out(s, bf16) for s in cat_shapes] + [out((rows, model), bf16)],
-        scratch_shapes=[like(headed), like(attn_all), like(attn_all), like(out_w), pltpu.VMEM((model, total), bf16), like(tokens), like(d_hidden)]
+        + [hbm] * 8 + [pl.BlockSpec(line, z2)] + [hbm] * 4,
+        out_specs=[hbm, pl.BlockSpec(line, z2)] + [hbm] * 6,
+        out_shape=[out((rows, model), f32), out(line, f32), out((rows, model), bf16)] + [out(x.shape, bf16) for x in mlp_parts] + [out(s, bf16) for s in cat_shapes] + [out((rows, model), bf16)],
+        scratch_shapes=[like(headed), like(attn_all), like(attn_all), like(out_w), pltpu.VMEM((model, width), bf16), like(beta), like(tokens), like(d_hidden)]
         + [like(x) for x in mlp_parts] + [pltpu.VMEM(s, bf16) for s in cat_shapes]
         + [like(x) for x in mlp_parts] + [pltpu.VMEM(s, bf16) for s in cat_shapes]
-        + ring_lands([down_part.shape] * 3, [False] * 3) + ring_lands(cat_shapes, [True, True])
+        + ring_lands([down_part.shape] * 3, [False] * 3) + ring_lands([(model, 2 * HEAD)] * 3 + cat_shapes[1:], [True] * 4)
         + [pltpu.VMEM((total_rows, 2 * HEAD), bf16), pltpu.VMEM((total_rows, total), bf16), pltpu.VMEM((2, HEAD, HEAD), f32),
            pltpu.VMEM((BACK_ROWS + 8, width), f32), pltpu.VMEM((BACK_ROWS + 8, width), f32), pltpu.VMEM((4, 8, width), f32), pltpu.VMEM((8, HEAD), f32),
            pltpu.VMEM((rows, model), f32), half(), half(), half(), half(), half(), half(),
            pltpu.VMEM(line, f32), pltpu.VMEM((3,) + line, f32), pltpu.VMEM(line, f32), pltpu.VMEM((RING - 1,) + line, f32), pltpu.VMEM((8, model), f32), pltpu.VMEM((8, model), f32),
-           dma((13,)), dma((5,)), dma((3, 2)), dma((3, 2, ROUNDS)), dma((2, 2)), dma((2, 2, ROUNDS)), dma((7, HALF)), dma((7, HALF)),
-           dma((3,)), dma((3,)), dma((RING - 1,)), dma((RING - 1,))],
+           dma((13,)), dma((6,)), dma((3, 2)), dma((3, 2, ROUNDS)), dma((4, 2)), dma((4, 2, ROUNDS)), dma((3, 2)), dma((3, 2)), dma((7, HALF)), dma((7, HALF)),
+           dma((3,)), dma((3,)), dma((RING - 1,)), dma((RING - 1,)), dma((2,))],
         compiler_params=pltpu.CompilerParams(dimension_semantics=("arbitrary",), collective_id=2, has_side_effects=True, vmem_limit_bytes=62 * 2**20),
-    )(flags, proj, proj, conv, gain, mixed, states, res, wu, inv, headed, attn_all, d_attn, out_w, qkv, beta, tokens, d_hidden, first_gain, second_grad, gu_part, down_part, out_across)
-
-
-def rms_norm(values, scales):
-    inverse = lax.rsqrt(jnp.mean(values * values, axis=-1, keepdims=True) + 1e-05)
-    return values * inverse * scales
-
-
-def gather(x):
-    return lax.all_gather(x, "tensor", axis=0, tiled=True)
-
-
-def dot(a, b, dims=NN):
-    return lax.dot_general(a, b, dims, preferred_element_type=f32)
+    )(flags, proj, proj, params, mixed, states, res, wu, inv, headed, attn_all, d_attn, out_w, qkv, beta, tokens, d_hidden, second_grad, gu_part, down_part, out_own, out_across)
 
 
 def on_device(tokens, lengths, attn_gain, qkv_weight, beta_weight, conv_weight, head_gain, out_weight, mlp_gain, gate_up_weight, down_weight, cotangent):
@@ -870,30 +1055,24 @@
     group_rows = tokens.shape[0] * lax.axis_size("tensor")
     starts = jnp.arange(group_rows // SPAN + 8, dtype=jnp.int32) * SPAN
     flags = jnp.where((starts == 0) | (starts == lengths[0, 0]), 1.0, 0.0).astype(f32)
-    local_in = tokens.astype(f32)
-    first_scale = attn_gain.astype(f32)
-    second_scale = mlp_gain.astype(f32)
-    head_scale = head_gain.astype(f32)[None]
-    conv = conv_weight.reshape(conv_weight.shape[0], -1).astype(f32)
     qkv = jnp.transpose(qkv_weight, (1, 0, 2))
-    beta = jnp.pad(beta_weight, ((0, 0), (0, HEAD - heads)))
+    beta = jnp.pad(beta_weight.T, ((0, 16 - heads), (0, 0)))
+    lines = [attn_gain[None], mlp_gain[None], jnp.pad(head_gain, (0, model_width - HEAD))[None]]
+    taps = jnp.concatenate([conv_weight[:, i] for i in range(3)], axis=1)
+    lines += [jnp.pad(taps, ((0, 1), (0, model_width - width)))]
+    params = jnp.concatenate(lines, axis=0).astype(f32)
     gate_up = jnp.transpose(gate_up_weight, (1, 2, 0)).reshape(-1, model_width)
-    attn_in = rms_norm(local_in, first_scale).astype(bf16)
-    attn_all = gather(attn_in)
-    out_all = gather(out_weight)
-    cot_all = gather(cotangent)
-    proj = dot(attn_all, jnp.concatenate([qkv[0], qkv[1], qkv[2], beta], axis=1))
-    headed, *saved = mixer_fwd(flags, proj, conv, head_scale)
-    headed_rows = lax.all_to_all(headed, "tensor", split_axis=0, concat_axis=1, tiled=True)
-    d_hidden, d_attn, second_grad, gu_part, down_part, out_own, out_across = mlp(headed_rows, out_all, tokens, second_scale[None], gate_up, down_weight, cot_all)
+    proj, mixed, states, res, wu, inv, attn_all, headed, headed_rows, out_all, cot_all = front(
+        flags, params, tokens, qkv, beta, out_weight, cotangent)
+    saved = (mixed, states, res, wu, inv)
+    d_hidden, d_attn, second_grad, gu_part, down_part, out_own, out_across = mlp(headed_rows, out_all, tokens, params, gate_up, down_weight, cot_all)
     n_dp = lax.axis_size("dp")
-    input_grad, small, *sums, landed = backward(
-        n_dp, flags, proj, conv, head_scale, saved, headed, attn_all, d_attn, out_weight, qkv, beta, tokens, d_hidden, first_scale[None], second_grad, gu_part, down_part, out_across)
+    input_grad, small, output, *sums, _ = backward(
+        n_dp, flags, proj, params, saved, headed, attn_all, d_attn, out_weight, qkv, beta, tokens, d_hidden, second_grad, gu_part, down_part, out_own, out_across)
     if n_dp > RING:
         groups = [list(range(i, n_dp, RING)) for i in range(RING)]
         small, *sums = lax.psum((small, *sums), "dp", axis_index_groups=groups)
     gu_sum, down_sum, cat_sum, out_sum = sums
-    output = (out_own + landed.astype(f32)).astype(bf16)
     return (
         output,
         input_grad,

time: 378 us -> 309 us (0.82)
  waiting for transfers between devices: 68.7 us -> 0 us
  Pallas kernels: 248 us -> 279 us
  between operations: 14.1 us -> 0.88 us
  matrix products: 8.88 us -> 0 us
  other arithmetic: 17.1 us -> 11.7 us
  starting transfers between devices: 3.94 us -> 0 us
    pallas_call x1, Pallas kernels: 21.7 us -> 75.8 us  [front(): pl.pallas_call(front_kernel, grid=(groups,), in_specs=[pl.BlockSpec(memor...]
    all_gather x3 -> x0, waiting for transfers between devices: 42.1 us -> none  [gather(): return lax.all_gather(x, 'tensor', axis=0, tiled=True)]
    all_to_all x1 -> x0, waiting for transfers between devices: 25.2 us -> none  [on_device(): lax.all_to_all(headed, 'tensor', split_axis=0, concat_axis=1, tiled=True)]
    pallas_call x1, Pallas kernels: 172 us -> 148 us  [backward(): pl.pallas_call(functools.partial(back_kernel, n_dp), grid=(n,), in_specs=...]
    dot_general x1 -> x0, matrix products: 8.88 us -> none  [dot(): return lax.dot_general(a, b, dims, preferred_element_type=f32)]
    convert_element_type x4 -> x1, other arithmetic: 4.54 us -> 0.64 us  [on_device(): params = jnp.concatenate(lines, axis=0).astype(f32)]
    all_to_all x1 -> x0, starting transfers between devices: 3.83 us -> none  [on_device(): lax.all_to_all(headed, 'tensor', split_axis=0, concat_axis=1, tiled=True)]
  transfers between devices with their start and end apart: 4 -> 0, of which waited for: 3 -> 0; matrix products, arithmetic and copies ran while one was open for 3% -> 0% of each run, Pallas kernels for 6% -> 0%
where the time goes in v5:
time: 309 us; the launch traced here: 304 us
  Pallas kernels  279 us (90%)
  local copies, waits for them, and re-layouts  12.5 us (4%)
  other arithmetic  11.7 us (4%)
    pallas_call x1, Pallas kernels, backward(): pl.pallas_call(functools.partial(back_kernel, n_dp), grid=(n,), in_specs=...  148 us
    pallas_call x1, Pallas kernels, front(): pl.pallas_call(front_kernel, grid=(groups,), in_specs=[pl.BlockSpec(memor...  75.8 us
    pallas_call x1, Pallas kernels, mlp(): pl.pallas_call(mlp_kernel, in_specs=[hbm] * 3 + [vmem] + [hbm] * 3, out_s...  55.2 us

profile of v5, /device:TPU:0, one launch (start us, length us, event | category | flops | bytes accessed | tf_op | source)
XLA Modules:
  0.0 303.8 jit_solution(16626996832133728698)
XLA Ops:
  0.6 1.2 or_select_fusion.flags
  1.8 0.7 pad.12
  2.5 0.7 broadcast_in_dim.19
  3.2 0.7 broadcast_in_dim.20
  3.8 0.7 slice_bitcast_fusion.4
  4.6 0.6 maximum_convert_fusion.params
  5.2 1.3 pad.14.beta_hbm
  6.5 75.8 %shard_map.203 = (f32[2048,896]{1,0:T(8,128)}, f32[2048,256]{1,0:T(8,128)}, bf16[16,256,128]{2,1,0:T(8,128)(2,1)}, bf16[16,256,128]{2,1,0:T(8,128)(2,1)}, bf16[1...) custom-call(f32[40]{0:T(128)} %or_select_fusion.flags, ...), custom_call_target="tpu_custom_call" | custom-call | tf_op jit(solution)/shard_map/pallas_call | solution.py:407
  82.4 55.2 %shard_map.204 = (f32[512,1024]{1,0:T(8,128)}, bf16[512,1024]{1,0:T(8,128)(2,1)}, f32[8,1024]{1,0:T(8,128)}, bf16[1408,1024]{1,0:T(8,128)(2,1)}, bf16[704,1024]{...) custom-call(bf16[512,1024]{1,0:T(8,128)(2,1)} %get-tuple-element.44.headed_hbm, ...), custom_call_target="tpu_custom_call" | custom-call | tf_op jit(solution)/shard_map/pallas_call | solution.py:599
  137.6 147.6 %shard_map.205 = (f32[512,1024]{1,0:T(8,128)}, f32[8,1024]{1,0:T(8,128)}, bf16[512,1024]{1,0:T(8,128)(2,1)}, bf16[1408,1024]{1,0:T(8,128)(2,1)}, bf16[704,1024]{...) custom-call(f32[40]{0:T(128)} %or_select_fusion.flags, ...), custom_call_target="tpu_custom_call" | custom-call | tf_op jit(solution)/shard_map/pallas_call | solution.py:1026
  285.2 0.0 copy-start.3
  285.2 1.3 slice_bitcast_fusion.5
  286.5 1.3 slice.37
  287.9 1.5 fusion.9
  289.4 0.6 pad_maximum_fusion
  290.0 2.1 convert_element_type.18
  292.1 0.0 copy-done.3
  292.1 0.0 copy-start.2
  292.1 1.9 convert_element_type.19
  294.1 0.0 copy-done.2
  294.1 0.0 copy-start
  294.1 1.9 convert_bitcast_fusion.1
  296.0 1.0 copy-done
  297.0 0.0 copy-start.4
  297.0 3.3 %convert_bitcast_fusion = f32[1024,2,704]{0,2,1:T(8,128)} fusion(bf16[2,704,1024]{2,1,0:T(8,128)(2,1)S(1)} %bitcast.32), kind=kLoop, calls=%fused_computation | loop fusion | flops 1441792 | bytes 8650752 | tf_op jit(solution)/shard_map/transpose | solution.py:1086
  300.3 0.0 copy-done.4
  300.3 0.0 copy-start.1
  300.3 1.0 copy.26
  301.3 1.0 copy-done.1
  302.3 1.3 copy.27
  (2 shorter events, 0.0 us)
Async XLA Ops:
  285.2 6.9 %copy-start.3 = (bf16[704,1024]{1,0:T(8,128)(2,1)S(1)}, bf16[704,1024]{1,0:T(8,128)(2,1)}, u32[]{:S(2)}) copy-start(bf16[704,1024]{1,0:T(8,128)(2,1)} %get-tuple-element.60) | copy-start | bytes 4325380
  292.1 1.9 copy-start.2
  294.1 3.0 copy-start
  297.0 3.3 %copy-start.4 = (bf16[512,1024]{1,0:T(8,128)(2,1)S(1)}, bf16[512,1024]{1,0:T(8,128)(2,1)}, u32[]{:S(2)}) copy-start(bf16[512,1024]{1,0:T(8,128)(2,1)} %get-tuple-element.90) | copy-start | bytes 3145732
  300.3 2.0 copy-start.1

commit v6 on v5

--- a/solution.py
+++ b/solution.py
@@ -71,8 +71,12 @@
     return enter, leave, keep
 
 
-def resets(flags, step):
-    return flags[2 * step], flags[2 * step + 1]
+def starts(lengths, span):
+    return jnp.where((span == 0) | (span * SPAN == lengths[0, 0]), 1.0, 0.0).astype(f32)
+
+
+def resets(lengths, step):
+    return starts(lengths, 2 * step), starts(lengths, 2 * step + 1)
 
 
 def sigmoid(x):
@@ -83,8 +87,8 @@
     row = lax.broadcasted_iota(jnp.int32, (8, HEAD), 0)
     heads, tails = [], []
     for i in range(count):
-        heads.append([None] + [jnp.where(row >= j, 1.0, 1.0 - flags[span + i]) for j in range(1, 4)])
-        tails.append([None] + [jnp.where(row + j < 8, 1.0, 1.0 - flags[span + i + 1]) for j in range(1, 4)])
+        heads.append([None] + [jnp.where(row >= j, 1.0, 1.0 - starts(flags, span + i)) for j in range(1, 4)])
+        tails.append([None] + [jnp.where(row + j < 8, 1.0, 1.0 - starts(flags, span + i + 1)) for j in range(1, 4)])
     return heads, tails
 
 
@@ -267,9 +271,9 @@
             self.passed(i).wait_send()
 
 
-def front_kernel(flags, params, tok_hbm, qkv_hbm, beta_hbm, outw_hbm, cot_hbm,
-                 proj_ref, mixed_ref, state_out, res_out, wu_out, inv_out, attn_out, headed_out, heads_hbm, out_hbm, cots_hbm,
-                 w, beta_w, tok, attn, headed, out_all, cot_all, state, buf, load, store, send_r, recv_r, send_w, recv_w, send_c, recv_c, send_h, recv_h):
+def front_kernel(flags, attn_gain, mlp_gain, head_gain, taps, beta_ref, tok_hbm, qkv_hbm, outw_hbm, cot_hbm,
+                 params, beta_w, proj_ref, mixed_ref, state_out, res_out, wu_out, inv_out, attn_out, headed_out, heads_hbm, out_hbm, cots_hbm,
+                 w, tok, attn, headed, out_all, cot_all, state, buf, load, store, send_r, recv_r, send_w, recv_w, send_c, recv_c, send_h, recv_h, send_s, recv_s):
     g = pl.program_id(0)
     n = pl.num_programs(0)
     d, t, beside, across, corner = places()
@@ -280,7 +284,7 @@
     rowset = Gather(attn, rows, send_r, recv_r)
     weights = Gather(out_all, outw_hbm.shape[0], send_w, recv_w)
     cots = Gather(cot_all, rows, send_c, recv_c)
-    loads = [(tok_hbm, tok)] + [(qkv_hbm.at[i], w.at[:, pl.ds(i * heads, heads)]) for i in range(3)] + [(beta_hbm, beta_w)]
+    loads = [(tok_hbm, tok)] + [(qkv_hbm.at[i], w.at[:, pl.ds(i * heads, heads)]) for i in range(3)]
     loads += [(outw_hbm, out_all.at[pl.ds(pl.multiple_of(t * outw_hbm.shape[0], 16), outw_hbm.shape[0])]), (cot_hbm, cot_all.at[pl.ds(pl.multiple_of(t * rows, rows), rows)])]
 
     def loaded(i):
@@ -302,6 +306,21 @@
         return pltpu.make_async_copy((out_all, cot_all)[i], (out_hbm, cots_hbm)[i], store.at[2 + n_groups + i])
 
     n_groups = headed.shape[0]
+
+    partners = [d + size - 2 * size * lax.rem(d // size, 2) for size in (1, 2, 4)]
+    slot = lax.rem(d, RING)
+    cut = outw_hbm.shape[0] // (2 * RING)
+
+    def slice_of(owner, size=1):
+        return out_all.at[pl.ds(pl.multiple_of(owner * outw_hbm.shape[0] + (weights.core * RING + slot // size * size) * cut, cut), size * cut)]
+
+    def slice_over(i):
+        ref = slice_of(weights.base + i)
+        return pltpu.make_async_remote_copy(src_ref=ref, dst_ref=ref, send_sem=send_w.at[1, i], recv_sem=recv_w.at[1, i], device_id=(d, across), device_id_type=MESH_ID)
+
+    def slice_spread(i, k):
+        ref = slice_of(weights.far + i, 2 ** k)
+        return pltpu.make_async_remote_copy(src_ref=ref, dst_ref=ref, send_sem=send_s.at[i, k], recv_sem=recv_s.at[i, k], device_id=(partners[k], t), device_id_type=MESH_ID)
 
     def heads_to(owner, sender):
         return pltpu.make_async_remote_copy(src_ref=headed.at[owner], dst_ref=head_place(sender), send_sem=send_h.at[owner], recv_sem=recv_h.at[sender], device_id=(d, owner), device_id_type=MESH_ID)
@@ -310,7 +329,15 @@
     def _():
         for i in range(len(loads)):
             loaded(i).start()
-        greet([(d, beside), (d, across), (d, corner)])
+        greet([(d, beside), (d, across), (d, corner)] + [(o, t) for o in partners])
+        model = tok.shape[1]
+        params[...] = jnp.zeros_like(params)
+        params[0:1, :] = attn_gain[...].astype(f32).reshape(1, model)
+        params[1:2, :] = mlp_gain[...].astype(f32).reshape(1, model)
+        params[2:3, :HEAD] = head_gain[...].astype(f32).reshape(1, HEAD)
+        for i in range(3):
+            params[3:7, i * heads:(i + 1) * heads] = taps[i].astype(f32)
+        beta_w[...] = jnp.concatenate([beta_ref[...].astype(f32), jnp.zeros((14, model), f32)], axis=0).astype(bf16)
         loaded(0).wait()
         piece = 64
         gain = first_gain[...]
@@ -322,12 +349,16 @@
 
         lax.fori_loop(0, rows // piece, chunk, 0)
         rowset.start_near()
+        loaded(4).wait()
+        weights.start_near()
         rowset.start_over()
+        weights.near(weights.core).wait_recv()
+        for i in range(2):
+            slice_over(i).start()
         state[...] = jnp.zeros_like(state)
         buf[0:8, :] = jnp.zeros((8, width), f32)
-        for i in range(1, len(loads)):
+        for i in (1, 2, 3, 5):
             loaded(i).wait()
-        weights.start_near()
         cots.start_near()
 
     @pl.when(g == beside)
@@ -342,8 +373,17 @@
 
     @pl.when(g == 2 - t // 2)
     def _():
-        weights.start_over()
         cots.start_over()
+
+    for k in range(2):
+        @pl.when(g == k + 2)
+        def _(k=k):
+            for i in range(2):
+                if k == 0:
+                    slice_over(i).wait_recv()
+                else:
+                    slice_spread(i, k - 1).wait_recv()
+                slice_spread(i, k).start()
 
     @pl.when(g == n - 1)
     def _():
@@ -367,10 +407,16 @@
     def _():
         for i in range(n_groups):
             kept(i).start()
-        for gather in (weights, cots):
-            gather.fetch_near()
-            for i in range(2):
-                gather.fetch_over(i)
+        weights.fetch_near()
+        for i in range(2):
+            slice_spread(i, 1).wait_recv()
+            slice_spread(i, 2).start()
+        cots.fetch_near()
+        cots.fetch_over(0)
+        for i in range(2):
+            slice_spread(i, 2).wait_recv()
+            weights.passed(i).start()
+        cots.fetch_over(1)
         for gather in (weights, cots):
             for i in range(2):
                 gather.passed(i).wait_recv()
@@ -380,7 +426,13 @@
             other = lax.rem(t + k, n_groups)
             heads_to(other, t).wait_send()
             heads_to(other, other).wait_recv()
-        for gather in (rowset, weights, cots):
+        for i in range(2):
+            weights.near(i).wait_send()
+            weights.passed(i).wait_send()
+            slice_over(i).wait_send()
+            for k in range(3):
+                slice_spread(i, k).wait_send()
+        for gather in (rowset, cots):
             gather.sent()
         gathered(0).wait()
         gathered(1).wait()
@@ -390,7 +442,7 @@
             kept(i).wait()
 
 
-def front(flags, params, tokens, qkv, beta, out_weight, cot):
+def front(lengths, attn_gain, mlp_gain, head_gain, taps, beta, tokens, qkv, out_weight, cot):
     rows, model = tokens.shape
     groups = 4
     total_rows = rows * groups
@@ -407,17 +459,17 @@
     return pl.pallas_call(
         front_kernel,
         grid=(groups,),
-        in_specs=[pl.BlockSpec(memory_space=pltpu.SMEM), pl.BlockSpec(params.shape, z2)] + [hbm] * 5,
-        out_specs=[pl.BlockSpec((ROWS, total), m2), pl.BlockSpec((ROWS, heads), m2), pl.BlockSpec((STEPS, heads, HEAD), m3), pl.BlockSpec((STEPS, 2 * STEP, HEAD), m3),
+        in_specs=[pl.BlockSpec(memory_space=pltpu.SMEM)] + [pl.BlockSpec(memory_space=pltpu.VMEM)] * 5 + [hbm] * 4,
+        out_specs=[pl.BlockSpec((8, model), z2), pl.BlockSpec((16, model), z2), pl.BlockSpec((ROWS, total), m2), pl.BlockSpec((ROWS, heads), m2), pl.BlockSpec((STEPS, heads, HEAD), m3), pl.BlockSpec((STEPS, 2 * STEP, HEAD), m3),
                    pl.BlockSpec((STEPS, 2 * STEP, heads), m3), pl.BlockSpec((STEPS, 2 * STEP, 2 * STEP), m3)] + [hbm] * 5,
-        out_shape=[out((total_rows, total), f32), out((total_rows, heads), f32), out((steps, heads, HEAD), bf16), out((steps, 2 * STEP, HEAD), bf16),
+        out_shape=[out((8, model), f32), out((16, model), bf16), out((total_rows, total), f32), out((total_rows, heads), f32), out((steps, heads, HEAD), bf16), out((steps, 2 * STEP, HEAD), bf16),
                    out((steps, 2 * STEP, heads), bf16), out((steps, 2 * STEP, 2 * STEP), bf16), out((total_rows, model), bf16), out((total_rows, heads), bf16),
                    out((rows, model), bf16), out((groups * out_weight.shape[0], model), bf16), out((total_rows, model), bf16)],
-        scratch_shapes=[pltpu.VMEM((model, width), bf16), pltpu.VMEM(beta.shape, bf16), pltpu.VMEM((rows, model), bf16), pltpu.VMEM((total_rows, model), bf16), pltpu.VMEM((groups, rows, heads), bf16),
-                        pltpu.VMEM((groups * out_weight.shape[0], model), bf16), pltpu.VMEM((total_rows, model), bf16), pltpu.VMEM((2, HEAD, HEAD), f32), pltpu.VMEM((ROWS + 8, width), f32), dma((7,)), dma((4 + groups,))]
-        + [dma((3, 2))] * 6 + [dma((groups,))] * 2,
+        scratch_shapes=[pltpu.VMEM((model, width), bf16), pltpu.VMEM((rows, model), bf16), pltpu.VMEM((total_rows, model), bf16), pltpu.VMEM((groups, rows, heads), bf16),
+                        pltpu.VMEM((groups * out_weight.shape[0], model), bf16), pltpu.VMEM((total_rows, model), bf16), pltpu.VMEM((2, HEAD, HEAD), f32), pltpu.VMEM((ROWS + 8, width), f32), dma((6,)), dma((4 + groups,))]
+        + [dma((3, 2))] * 6 + [dma((groups,))] * 2 + [dma((2, 3))] * 2,
         compiler_params=pltpu.CompilerParams(dimension_semantics=("arbitrary",), collective_id=3, has_side_effects=True, vmem_limit_bytes=56 * 2**20),
-    )(flags, params, tokens, qkv, beta, out_weight, cot)
+    )(lengths, attn_gain, mlp_gain, head_gain, taps, beta, tokens, qkv, out_weight, cot)
 
 
 def mlp_kernel(headed_hbm, out_hbm, tok_hbm, params, gu_hbm, down_hbm, cot_hbm,
@@ -824,13 +876,13 @@
         gacc[...] = jnp.zeros_like(gacc)
         gain_acc[...] = jnp.zeros_like(gain_acc)
         loaded(3).wait()
-        mlp_ring.visit(5)
+        mlp_ring.visit(7)
 
         @pl.when(t < 2)
         def _():
             rowset.fetch_over(1)
 
-        mlp_ring.visit(1)
+        mlp_ring.visit(2)
 
     owner = n // 2 - 1 - g // 2
     for k in range(1, n):
@@ -1048,43 +1100,68 @@
     )(flags, proj, proj, params, mixed, states, res, wu, inv, headed, attn_all, d_attn, out_w, qkv, beta, tokens, d_hidden, second_grad, gu_part, down_part, out_own, out_across)
 
 
+def cast_kernel(small, gu, down, cat, outw, dx, out, attn_grad, mlp_grad, head_grad, taps_grad, beta_grad, gu_out, down_out, cat_out, outw_out, dx_out, out_out):
+    gu_out[...] = gu[...].astype(f32)
+    down_out[...] = down[...].astype(f32)
+    cat_out[...] = cat[...].astype(f32)
+    outw_out[...] = outw[...].astype(f32)
+    dx_out[...] = dx[...]
+    out_out[...] = out[...]
+    width = 3 * taps_grad.shape[2]
+    attn_grad[...] = small[0, :]
+    mlp_grad[...] = small[1, :]
+    head_grad[...] = small[3, width:width + HEAD]
+    for i in range(3):
+        taps_grad[i] = small[3:7, i * width // 3:(i + 1) * width // 3]
+    beta_grad[0:1, :] = small[2:3, :]
+    beta_grad[1:2, :] = small[7:8, :]
+
+
+def cast(small, gu, down, cat, outw, dx, out):
+    steps = 4
+    model = small.shape[1]
+    arrays = (gu, down, cat, outw, dx, out)
+    kinds = [f32] * 5 + [out.dtype]
+    spec = lambda x: pl.BlockSpec((x.shape[0] // steps, x.shape[1]), lambda g: (g, 0))
+    shapes = [(model,), (model,), (HEAD,), (3, 4, cat.shape[1]), (2, model)]
+    whole = lambda s: pl.BlockSpec(s, lambda g: (0,) * len(s))
+    return pl.pallas_call(
+        cast_kernel,
+        grid=(steps,),
+        in_specs=[whole(small.shape)] + [spec(x) for x in arrays],
+        out_specs=[whole(s) for s in shapes] + [spec(x) for x in arrays],
+        out_shape=[jax.ShapeDtypeStruct(s, f32) for s in shapes] + [jax.ShapeDtypeStruct(x.shape, k) for x, k in zip(arrays, kinds)],
+        compiler_params=pltpu.CompilerParams(dimension_semantics=("arbitrary",), vmem_limit_bytes=62 * 2**20),
+    )(small, *arrays)
+
+
 def on_device(tokens, lengths, attn_gain, qkv_weight, beta_weight, conv_weight, head_gain, out_weight, mlp_gain, gate_up_weight, down_weight, cotangent):
     model_width = tokens.shape[1]
-    width = qkv_weight.shape[1] * qkv_weight.shape[2]
-    heads = beta_weight.shape[1]
-    group_rows = tokens.shape[0] * lax.axis_size("tensor")
-    starts = jnp.arange(group_rows // SPAN + 8, dtype=jnp.int32) * SPAN
-    flags = jnp.where((starts == 0) | (starts == lengths[0, 0]), 1.0, 0.0).astype(f32)
     qkv = jnp.transpose(qkv_weight, (1, 0, 2))
-    beta = jnp.pad(beta_weight.T, ((0, 16 - heads), (0, 0)))
-    lines = [attn_gain[None], mlp_gain[None], jnp.pad(head_gain, (0, model_width - HEAD))[None]]
-    taps = jnp.concatenate([conv_weight[:, i] for i in range(3)], axis=1)
-    lines += [jnp.pad(taps, ((0, 1), (0, model_width - width)))]
-    params = jnp.concatenate(lines, axis=0).astype(f32)
     gate_up = jnp.transpose(gate_up_weight, (1, 2, 0)).reshape(-1, model_width)
-    proj, mixed, states, res, wu, inv, attn_all, headed, headed_rows, out_all, cot_all = front(
-        flags, params, tokens, qkv, beta, out_weight, cotangent)
+    params, beta, proj, mixed, states, res, wu, inv, attn_all, headed, headed_rows, out_all, cot_all = front(
+        lengths, attn_gain, mlp_gain, head_gain, jnp.transpose(conv_weight, (1, 0, 2)), beta_weight.T, tokens, qkv, out_weight, cotangent)
     saved = (mixed, states, res, wu, inv)
     d_hidden, d_attn, second_grad, gu_part, down_part, out_own, out_across = mlp(headed_rows, out_all, tokens, params, gate_up, down_weight, cot_all)
     n_dp = lax.axis_size("dp")
     input_grad, small, output, *sums, _ = backward(
-        n_dp, flags, proj, params, saved, headed, attn_all, d_attn, out_weight, qkv, beta, tokens, d_hidden, second_grad, gu_part, down_part, out_own, out_across)
+        n_dp, lengths, proj, params, saved, headed, attn_all, d_attn, out_weight, qkv, beta, tokens, d_hidden, second_grad, gu_part, down_part, out_own, out_across)
     if n_dp > RING:
         groups = [list(range(i, n_dp, RING)) for i in range(RING)]
         small, *sums = lax.psum((small, *sums), "dp", axis_index_groups=groups)
-    gu_sum, down_sum, cat_sum, out_sum = sums
+    attn_gain_grad, mlp_gain_grad, head_gain_grad, taps_grad, beta_grad, gu_sum, down_sum, cat_sum, out_sum, input_grad, output = cast(small, *sums, input_grad, output)
     return (
         output,
         input_grad,
-        small[0],
-        jnp.transpose(cat_sum.astype(f32).reshape(3, model_width, -1), (1, 0, 2)),
-        jnp.stack([small[2], small[7]], axis=1),
-        small[3:7, :width].reshape(conv_weight.shape),
-        small[3, width:width + HEAD],
-        out_sum.astype(f32),
-        small[1],
-        jnp.transpose(gu_sum.astype(f32).reshape(2, -1, model_width), (2, 0, 1)),
-        down_sum.astype(f32),
+        attn_gain_grad,
+        jnp.transpose(cat_sum.reshape(3, model_width, -1), (1, 0, 2)),
+        beta_grad.T,
+        jnp.transpose(taps_grad, (1, 0, 2)),
+        head_gain_grad,
+        out_sum,
+        mlp_gain_grad,
+        jnp.transpose(gu_sum.reshape(2, -1, model_width), (2, 0, 1)),
+        down_sum,
     )
 
 

time: 309 us -> 282 us (0.913)
  local copies, waits for them, and re-layouts: 12.5 us -> 0 us
  other arithmetic: 11.7 us -> 0 us
    pallas_call x0 -> x1, Pallas kernels: none -> 10.3 us  [cast(): pl.pallas_call(cast_kernel, grid=(steps,), in_specs=[whole(small.shape)]...]
    pallas_call x1, Pallas kernels: 75.8 us -> 69.1 us  [front(): pl.pallas_call(front_kernel, grid=(groups,), in_specs=[pl.BlockSpec(memor...]
    pallas_call x1, Pallas kernels: 148 us -> 141 us  [backward(): pl.pallas_call(functools.partial(back_kernel, n_dp), grid=(n,), in_specs=...]
    transpose x2 -> x0, other arithmetic: 5.18 us -> none  [the longest x1 3.25 us: on_device(): jnp.transpose(gu_sum.astype(f32).reshape(2, -1, model_width), (2, 0, 1))]
    convert_element_type x3 -> x0, other arithmetic: 4.7 us -> none  [the longest x1 2.13 us: on_device(): out_sum.astype(f32)]
    unnamed x12 -> x0, local copies, waits for them, and re-layouts: 4.31 us -> none
where the time goes in v6:
time: 282 us; the launch traced here: 277 us
  Pallas kernels  276 us (98%)
    pallas_call x1, Pallas kernels, backward(): pl.pallas_call(functools.partial(back_kernel, n_dp), grid=(n,), in_specs=...  141 us
    pallas_call x1, Pallas kernels, front(): pl.pallas_call(front_kernel, grid=(groups,), in_specs=[pl.BlockSpec(memor...  69.1 us
    pallas_call x1, Pallas kernels, mlp(): pl.pallas_call(mlp_kernel, in_specs=[hbm] * 3 + [vmem] + [hbm] * 3, out_s...  55.6 us
    pallas_call x1, Pallas kernels, cast(): pl.pallas_call(cast_kernel, grid=(steps,), in_specs=[whole(small.shape)]...  10.3 us

profile of v6, /device:TPU:0, one launch (start us, length us, event | category | flops | bytes accessed | tf_op | source)
XLA Modules:
  0.0 277.4 jit_solution(14132149801675743811)
XLA Ops:
  0.6 69.1 %shard_map.203 = (f32[8,1024]{1,0:T(8,128)}, bf16[16,1024]{1,0:T(8,128)(2,1)}, f32[2048,896]{1,0:T(8,128)}, f32[2048,256]{1,0:T(8,128)}, bf16[16,256,128]{2,1,0:...) custom-call(s32[1,2]{1,0:T(1,128)} %flags.3, ...), custom_call_target="tpu_custom_call" | custom-call | tf_op jit(solution)/shard_map/pallas_call | solution.py:459
  69.8 55.6 %shard_map.204 = (f32[512,1024]{1,0:T(8,128)}, bf16[512,1024]{1,0:T(8,128)(2,1)}, f32[8,1024]{1,0:T(8,128)}, bf16[1408,1024]{1,0:T(8,128)(2,1)}, bf16[704,1024]{...) custom-call(bf16[512,1024]{1,0:T(8,128)(2,1)} %get-tuple-element.58.headed_hbm, ...), custom_call_target="tpu_custom_call" | custom-call | tf_op jit(solution)/shard_map/pallas_call | solution.py:651
  125.4 141.5 %shard_map.205 = (f32[512,1024]{1,0:T(8,128)}, f32[8,1024]{1,0:T(8,128)}, bf16[512,1024]{1,0:T(8,128)(2,1)}, bf16[1408,1024]{1,0:T(8,128)(2,1)}, bf16[704,1024]{...) custom-call(s32[1,2]{1,0:T(1,128)} %flags.3, ...), custom_call_target="tpu_custom_call" | custom-call | tf_op jit(solution)/shard_map/pallas_call | solution.py:1078
  266.9 10.3 %shard_map.206 = (f32[1024]{0:T(1024)}, f32[1024]{0:T(1024)}, f32[128]{0:T(128)}, f32[3,4,256]{2,1,0:T(4,128)}, f32[2,1024]{1,0:T(2,128)}, /*index=5*/f32[1408,1...) custom-call(f32[8,1024]{1,0:T(8,128)} %get-tuple-element.69.small, ...), custom_call_target="tpu_custom_call" | custom-call | tf_op jit(solution)/shard_map/pallas_call | solution.py:1128

commit v7 on v6

--- a/solution.py
+++ b/solution.py
@@ -126,6 +126,7 @@
 
 MESH_ID = pl.DeviceIdType.MESH
 HALF = 2
+EARLY_A, EARLY_B, EARLY_C = 5, 6, 5
 
 
 def places():
@@ -472,16 +473,26 @@
     )(lengths, attn_gain, mlp_gain, head_gain, taps, beta, tokens, qkv, out_weight, cot)
 
 
+def norm_back(grad, x, gain, through):
+    r = lax.rsqrt(jnp.mean(x * x, axis=-1, keepdims=True) + 1e-5)
+    scaled = gain * grad
+    full = through + r * scaled - x * (r * r * r * jnp.mean(x * scaled, axis=-1, keepdims=True))
+    return full, jnp.sum((grad * x * r).reshape(x.shape[0] // 8, 8, x.shape[1]), axis=0)
+
+
 def mlp_kernel(headed_hbm, out_hbm, tok_hbm, params, gu_hbm, down_hbm, cot_hbm,
-               dhid_hbm, dattn_hbm, gain_out, gu_out, downg_out, own_hbm, across_hbm,
+               dhid_hbm, dattn_hbm, gain_out, gu_out, downg_out, own_hbm, across_hbm, late_hbm, hidden_hbm,
                headed, out_w, tok, gu_w, down_w, cot, hidden, all_rows, act, d_gate, d_up, mine, keep, to_beside, from_beside, to_across, from_across, to_own, from_own,
                out_own, out_keep, from_beside_out, from_own_out, gu_acc, down_acc, gu_sum, down_sum, dattn, load, store, send, recv):
     d, t, beside, across, corner = places()
     rows = tok.shape[0]
     part = rows // HALF
     units = down_w.shape[0]
+    def half(ref, s):
+        return ref.at[pl.ds(s * part, part)]
+
     loads = [(headed_hbm, headed), (out_hbm, out_w), (tok_hbm, tok), (gu_hbm, gu_w), (down_hbm, down_w), (cot_hbm, cot)]
-    stores = [(mine, dhid_hbm), (dattn, dattn_hbm), (gu_sum, gu_out), (down_sum, downg_out), (out_own, own_hbm), (out_keep, across_hbm)]
+    stores = [(mine, dhid_hbm), (dattn, dattn_hbm), (gu_sum, gu_out), (down_sum, downg_out), (out_own, own_hbm), (out_keep, across_hbm), (half(to_across, 1), late_hbm), (half(hidden, 1), hidden_hbm)]
 
     def loaded(i):
         return pltpu.make_async_copy(loads[i][0], loads[i][1], load.at[i])
@@ -491,9 +502,6 @@
 
     def pushed(src, dst, i, s, peer):
         return pltpu.make_async_remote_copy(src_ref=src, dst_ref=dst, send_sem=send.at[i, s], recv_sem=recv.at[i, s], device_id=(d, peer), device_id_type=MESH_ID)
-
-    def half(ref, s):
-        return ref.at[pl.ds(s * part, part)]
 
     def rows_to(i, s, peer):
         block = all_rows.at[row_block(t, s, rows, part)]
@@ -592,9 +600,12 @@
         handed_out(s).start()
         handed(s).wait_recv()
         to_across[at, :] = (keep[...] + from_beside[at, :].astype(f32)).astype(bf16)
-        summed(s).start()
         if s == 0:
+            summed(s).start()
             weight_grads(t // 2, False)
+        else:
+            stored(6).start()
+            stored(7).start()
     weight_grads(1 - t // 2, True)
     stored(2).start()
     stored(3).start()
@@ -609,29 +620,28 @@
     stored(5).start()
     gain_out[...] = jnp.zeros_like(gain_out)
     piece = 64
-    for s in range(HALF):
-        owned(s).wait_recv()
-        summed(s).wait_recv()
-
-        def chunk(i, carry, s=s):
-            at = pl.ds(pl.multiple_of(s * part + i * piece, piece), piece)
-            grad = mine[at, :] + from_own[at, :].astype(f32) + from_across[at, :].astype(f32)
-            x = hidden[at, :]
-            r = lax.rsqrt(jnp.mean(x * x, axis=-1, keepdims=True) + 1e-5)
-            scaled = gain * grad
-            cot_rows = cot[pl.ds(pl.multiple_of(t * rows + s * part + i * piece, piece), piece), :].astype(f32)
-            full = cot_rows + r * scaled - x * (r * r * r * jnp.mean(x * scaled, axis=-1, keepdims=True))
-            mine[at, :] = full
-            dattn[at, :] = full.astype(bf16)
-            gain_out[...] += jnp.sum((grad * x * r).reshape(piece // 8, 8, grad.shape[1]), axis=0)
-            return carry
-
-        lax.fori_loop(0, part // piece, chunk, 0)
+    owned(0).wait_recv()
+    summed(0).wait_recv()
+
+    def chunk(i, carry):
+        at = pl.ds(pl.multiple_of(i * piece, piece), piece)
+        grad = mine[at, :] + from_own[at, :].astype(f32) + from_across[at, :].astype(f32)
+        cot_rows = cot[pl.ds(pl.multiple_of(t * rows + i * piece, piece), piece), :].astype(f32)
+        full, part_gain = norm_back(grad, hidden[at, :], gain, cot_rows)
+        mine[at, :] = full
+        dattn[at, :] = full.astype(bf16)
+        gain_out[...] += part_gain
+        return carry
+
+    lax.fori_loop(0, part // piece, chunk, 0)
+    owned(1).wait_recv()
+    mine[pl.ds(part, part), :] = mine[pl.ds(part, part), :] + from_own[pl.ds(part, part), :].astype(f32)
     stored(0).start()
     stored(1).start()
     for s in range(HALF):
-        for copy in (rows_to(0, s, across), rows_to(1, s, beside), passed(s), handed(s), summed(s), owned(s), handed_out(s)):
+        for copy in (rows_to(0, s, across), rows_to(1, s, beside), passed(s), handed(s), owned(s), handed_out(s)):
             copy.wait_send()
+    summed(0).wait_send()
     for i in range(len(stores)):
         stored(i).wait()
 
@@ -651,11 +661,11 @@
     return pl.pallas_call(
         mlp_kernel,
         in_specs=[hbm] * 3 + [vmem] + [hbm] * 3,
-        out_specs=[hbm] * 2 + [vmem] + [hbm] * 4,
-        out_shape=[out((rows, width), f32), out((rows, width), bf16), out((8, width), f32), out(gate_up.shape, bf16), out(down.shape, bf16), out((rows, width), f32), out((rows, width), bf16)],
+        out_specs=[hbm] * 2 + [vmem] + [hbm] * 6,
+        out_shape=[out((rows, width), f32), out((rows, width), bf16), out((8, width), f32), out(gate_up.shape, bf16), out(down.shape, bf16), out((rows, width), f32), out((rows, width), bf16), out((rows // HALF, width), bf16), out((rows // HALF, width), f32)],
         scratch_shapes=[like(headed), like(out_all), like(tokens), like(gate_up), like(down), like(cot), wide(), pltpu.VMEM((total, width), bf16), unit(), unit(), unit(),
                         wide(), pltpu.VMEM((rows // HALF, width), f32), half(), half(), half(), half(), half(), half(), wide(), half(), half(), half(),
-                        pltpu.VMEM(gate_up.shape, f32), pltpu.VMEM(down.shape, f32), like(gate_up), like(down), half(), dma((6,)), dma((6,)), dma((8, HALF)), dma((8, HALF))],
+                        pltpu.VMEM(gate_up.shape, f32), pltpu.VMEM(down.shape, f32), like(gate_up), like(down), half(), dma((6,)), dma((8,)), dma((8, HALF)), dma((8, HALF))],
         compiler_params=pltpu.CompilerParams(collective_id=1, has_side_effects=True, vmem_limit_bytes=62 * 2**20),
     )(headed, out_all, tokens, gain, gate_up, down, cot)
 
@@ -817,12 +827,12 @@
 
 
 def back_kernel(n_dp, flags, proj_ref, prev_ref, params, mixed_ref, state_in, res_in, wu_in, inv_in,
-                headed_hbm, attn_hbm, dattn_hbm, out_w_hbm, qkv_hbm, beta_hbm, tok_hbm, dhid_hbm, second_grad, gu_hbm, down_hbm, own_hbm, across_hbm,
+                headed_hbm, attn_hbm, dattn_hbm, out_w_hbm, qkv_hbm, beta_hbm, tok_hbm, dhid_hbm, second_grad, gu_hbm, down_hbm, own_hbm, across_hbm, late_hbm, hidden_hbm, cot_hbm,
                 dx_hbm, small_out, output_hbm, gu_out, down_out, cat_out, outw_out, landed_hbm,
                 headed, attn, dattn_all, out_w, w, beta_w, tok, dhid, gu_src, down_src, cat_src, outw_src,
                 gu_res, down_res, cat_res, outw_res, gate_land, up_land, down_land, q_land, k_land, v_land, outw_land,
                 dheaded, dcat, dstate, buf, dbuf, cacc, gacc, mine, to_beside, from_beside, to_across, from_across, to_own, from_own,
-                group_send, group_land, all_send, all_land, gain_acc, beta_grad,
+                group_send, group_land, all_send, all_land, gain_acc, beta_grad, second_acc, late_land,
                 load, store, send_m, recv_m, send_c, recv_c, send_r, recv_r, send_x, recv_x, send_g, recv_g, send_a, recv_a, late_sem):
     g = pl.program_id(0)
     n = pl.num_programs(0)
@@ -832,7 +842,7 @@
     part = rows // HALF
     width = buf.shape[1]
     others = [d // RING * RING + lax.rem(d + k, RING) for k in range(1, RING)]
-    first_gain, _, gain_ref, conv_ref = param_views(params, width)
+    first_gain, second_gain, gain_ref, conv_ref = param_views(params, width)
     units = down_src.shape[0]
     gate_up = lambda ref: [ref.at[pl.ds(0, units)], ref.at[pl.ds(units, units)]]
     mlp_ring = Ring(here, (after, t), (before, t), gate_up(gu_src) + [down_src], gate_up(gu_res) + [down_res], [gate_land, up_land, down_land], [False] * 3, send_m, recv_m)
@@ -842,6 +852,9 @@
     rowset = Gather(dattn_all, rows, send_r, recv_r)
     loads = [(gu_hbm, gu_src), (down_hbm, down_src), (dattn_hbm, dattn_all.at[pl.ds(pl.multiple_of(t * rows, rows), rows)]), (out_w_hbm, out_w), (headed_hbm, headed), (attn_hbm, attn), (tok_hbm, tok), (dhid_hbm, dhid), (beta_hbm, beta_w)]
     loads += [(qkv_hbm.at[i], w.at[:, pl.ds(i * 2 * HEAD, 2 * HEAD)]) for i in range(3)]
+    early = len(loads)
+    dhid_load = 7
+    loads += [(hidden_hbm, mine.at[pl.ds(0, part)]), (cot_hbm.at[pl.ds(pl.multiple_of(t * rows + part, part), part)], to_own.at[pl.ds(0, part)])]
     stores = [(gu_res, gu_out), (down_res, down_out), (mine, dx_hbm), (cat_res, cat_out), (outw_res, outw_out), (to_own, output_hbm)]
 
     def loaded(i):
@@ -855,6 +868,9 @@
 
     def outward():
         return pushed(across_hbm, landed_hbm, 6, 0, across)
+
+    def late():
+        return pushed(late_hbm, late_land, 6, 1, across)
 
     def block_at(owner, s):
         return row_block(owner, s, rows, part)
@@ -864,25 +880,42 @@
         for i in range(len(loads)):
             loaded(i).start()
         greet([(d, beside), (d, across), (d, corner)] + [(o, t) for o in others])
+        late().start()
         loaded(2).wait()
-        rowset.start_near()
+        rowset.near(0).start()
         loaded(0).wait()
         loaded(1).wait()
         mlp_ring.visit(3)
-        rowset.start_over(1)
         dstate[...] = jnp.zeros_like(dstate)
         dbuf[BACK_ROWS:, :] = jnp.zeros((8, width), f32)
         cacc[...] = jnp.zeros_like(cacc)
         gacc[...] = jnp.zeros_like(gacc)
         gain_acc[...] = jnp.zeros_like(gain_acc)
-        loaded(3).wait()
-        mlp_ring.visit(7)
+        second_acc[...] = jnp.zeros_like(second_acc)
+        for i in (3, dhid_load, early, early + 1):
+            loaded(i).wait()
+        mlp_ring.visit(EARLY_A)
+        late().wait_recv()
+
+        def last(i, carry):
+            here_at = pl.ds(pl.multiple_of(i * 64, 64), 64)
+            at = pl.ds(pl.multiple_of(part + i * 64, 64), 64)
+            full, part_gain = norm_back(dhid[at, :] + late_land[here_at, :].astype(f32), mine[here_at, :], second_gain[...], to_own[here_at, :].astype(f32))
+            dhid[at, :] = full
+            dattn_all[pl.ds(pl.multiple_of(t * rows + part + i * 64, 64), 64), :] = full.astype(bf16)
+            second_acc[...] += part_gain
+            return carry
+
+        lax.fori_loop(0, part // 64, last, 0)
+        rowset.near(1).start()
+        rowset.start_over(1)
+        mlp_ring.visit(EARLY_B)
 
         @pl.when(t < 2)
         def _():
             rowset.fetch_over(1)
 
-        mlp_ring.visit(2)
+        mlp_ring.visit(EARLY_C)
 
     owner = n // 2 - 1 - g // 2
     for k in range(1, n):
@@ -953,8 +986,9 @@
 
     @pl.when(g == n - 1)
     def _():
-        for i in range(4, len(loads)):
-            loaded(i).wait()
+        for i in range(4, early):
+            if i != dhid_load:
+                loaded(i).wait()
 
         def cat_chunk(i):
             grad = lax.dot_general(attn[:, i * 256:(i + 1) * 256], dcat[:, :width], TN, preferred_element_type=f32).astype(bf16)
@@ -1000,11 +1034,11 @@
             for s in range(HALF):
                 copy(s).wait_send()
         outward().wait_recv()
-        late = [pltpu.make_async_copy(own_hbm, dhid, late_sem.at[0]), pltpu.make_async_copy(landed_hbm, to_across, late_sem.at[1])]
-        for copy in late:
+        ends = [pltpu.make_async_copy(own_hbm, dhid, late_sem.at[0]), pltpu.make_async_copy(landed_hbm, to_across, late_sem.at[1])]
+        for copy in ends:
             copy.start()
         turn()
-        for copy in late:
+        for copy in ends:
             copy.wait()
 
         def add(i, carry):
@@ -1019,7 +1053,7 @@
         shared = (line < 2) | ((line == 3) & (lane >= width))
         group_send[...] = jnp.zeros_like(group_send)
         group_send[0:1, :] = jnp.sum(gain_acc[...], axis=0, keepdims=True)
-        group_send[1:2, :] = jnp.sum(second_grad[...], axis=0, keepdims=True)
+        group_send[1:2, :] = jnp.sum(second_grad[...] + second_acc[...], axis=0, keepdims=True)
         group_send[2:3, :] = beta_grad[0:1, :]
         group_send[7:8, :] = beta_grad[1:2, :]
         group_send[3:4, width:width + HEAD] = jnp.sum(gacc[...], axis=0, keepdims=True)
@@ -1054,11 +1088,12 @@
         for i, o in enumerate(others):
             spread(i, o).wait_send()
         outward().wait_send()
+        late().wait_send()
         for i in range(len(stores)):
             stored(i).wait()
 
 
-def backward(n_dp, flags, proj, params, saved, headed, attn_all, d_attn, out_w, qkv, beta, tokens, d_hidden, second_grad, gu_part, down_part, out_own, out_across):
+def backward(n_dp, flags, proj, params, saved, headed, attn_all, d_attn, out_w, qkv, beta, tokens, d_hidden, second_grad, gu_part, down_part, out_own, out_across, late, hidden_late, cot_all):
     mixed, states, res, wu, inv = saved
     total_rows, total = proj.shape
     width = 3 * qkv.shape[2]
@@ -1083,7 +1118,7 @@
                   pl.BlockSpec(params.shape, z2), pl.BlockSpec((BACK_ROWS, 2 * HEAD), m2),
                   pl.BlockSpec((BACK_STEPS, 2 * HEAD, HEAD), m3), pl.BlockSpec((BACK_STEPS, 2 * STEP, HEAD), m3),
                   pl.BlockSpec((BACK_STEPS, 2 * STEP, 2 * HEAD), m3), pl.BlockSpec((BACK_STEPS, 2 * STEP, 2 * STEP), m3)]
-        + [hbm] * 8 + [pl.BlockSpec(line, z2)] + [hbm] * 4,
+        + [hbm] * 8 + [pl.BlockSpec(line, z2)] + [hbm] * 7,
         out_specs=[hbm, pl.BlockSpec(line, z2)] + [hbm] * 6,
         out_shape=[out((rows, model), f32), out(line, f32), out((rows, model), bf16)] + [out(x.shape, bf16) for x in mlp_parts] + [out(s, bf16) for s in cat_shapes] + [out((rows, model), bf16)],
         scratch_shapes=[like(headed), like(attn_all), like(attn_all), like(out_w), pltpu.VMEM((model, width), bf16), like(beta), like(tokens), like(d_hidden)]
@@ -1093,11 +1128,11 @@
         + [pltpu.VMEM((total_rows, 2 * HEAD), bf16), pltpu.VMEM((total_rows, total), bf16), pltpu.VMEM((2, HEAD, HEAD), f32),
            pltpu.VMEM((BACK_ROWS + 8, width), f32), pltpu.VMEM((BACK_ROWS + 8, width), f32), pltpu.VMEM((4, 8, width), f32), pltpu.VMEM((8, HEAD), f32),
            pltpu.VMEM((rows, model), f32), half(), half(), half(), half(), half(), half(),
-           pltpu.VMEM(line, f32), pltpu.VMEM((3,) + line, f32), pltpu.VMEM(line, f32), pltpu.VMEM((RING - 1,) + line, f32), pltpu.VMEM((8, model), f32), pltpu.VMEM((8, model), f32),
-           dma((13,)), dma((6,)), dma((3, 2)), dma((3, 2, ROUNDS)), dma((4, 2)), dma((4, 2, ROUNDS)), dma((3, 2)), dma((3, 2)), dma((7, HALF)), dma((7, HALF)),
+           pltpu.VMEM(line, f32), pltpu.VMEM((3,) + line, f32), pltpu.VMEM(line, f32), pltpu.VMEM((RING - 1,) + line, f32), pltpu.VMEM((8, model), f32), pltpu.VMEM((8, model), f32), pltpu.VMEM((8, model), f32), like(late),
+           dma((15,)), dma((6,)), dma((3, 2)), dma((3, 2, ROUNDS)), dma((4, 2)), dma((4, 2, ROUNDS)), dma((3, 2)), dma((3, 2)), dma((7, HALF)), dma((7, HALF)),
            dma((3,)), dma((3,)), dma((RING - 1,)), dma((RING - 1,)), dma((2,))],
         compiler_params=pltpu.CompilerParams(dimension_semantics=("arbitrary",), collective_id=2, has_side_effects=True, vmem_limit_bytes=62 * 2**20),
-    )(flags, proj, proj, params, mixed, states, res, wu, inv, headed, attn_all, d_attn, out_w, qkv, beta, tokens, d_hidden, second_grad, gu_part, down_part, out_own, out_across)
+    )(flags, proj, proj, params, mixed, states, res, wu, inv, headed, attn_all, d_attn, out_w, qkv, beta, tokens, d_hidden, second_grad, gu_part, down_part, out_own, out_across, late, hidden_late, cot_all)
 
 
 def cast_kernel(small, gu, down, cat, outw, dx, out, attn_grad, mlp_grad, head_grad, taps_grad, beta_grad, gu_out, down_out, cat_out, outw_out, dx_out, out_out):
@@ -1142,10 +1177,10 @@
     params, beta, proj, mixed, states, res, wu, inv, attn_all, headed, headed_rows, out_all, cot_all = front(
         lengths, attn_gain, mlp_gain, head_gain, jnp.transpose(conv_weight, (1, 0, 2)), beta_weight.T, tokens, qkv, out_weight, cotangent)
     saved = (mixed, states, res, wu, inv)
-    d_hidden, d_attn, second_grad, gu_part, down_part, out_own, out_across = mlp(headed_rows, out_all, tokens, params, gate_up, down_weight, cot_all)
+    d_hidden, d_attn, second_grad, gu_part, down_part, out_own, out_across, late, hidden_late = mlp(headed_rows, out_all, tokens, params, gate_up, down_weight, cot_all)
     n_dp = lax.axis_size("dp")
     input_grad, small, output, *sums, _ = backward(
-        n_dp, lengths, proj, params, saved, headed, attn_all, d_attn, out_weight, qkv, beta, tokens, d_hidden, second_grad, gu_part, down_part, out_own, out_across)
+        n_dp, lengths, proj, params, saved, headed, attn_all, d_attn, out_weight, qkv, beta, tokens, d_hidden, second_grad, gu_part, down_part, out_own, out_across, late, hidden_late, cot_all)
     if n_dp > RING:
         groups = [list(range(i, n_dp, RING)) for i in range(RING)]
         small, *sums = lax.psum((small, *sums), "dp", axis_index_groups=groups)

time: 282 us -> 279 us (0.989)
  Pallas kernels: 276 us -> 273 us
    pallas_call x1, Pallas kernels: 55.6 us -> 47.9 us  [mlp(): pl.pallas_call(mlp_kernel, in_specs=[hbm] * 3 + [vmem] + [hbm] * 3, out_s...]
    pallas_call x1, Pallas kernels: 141 us -> 146 us  [backward(): pl.pallas_call(functools.partial(back_kernel, n_dp), grid=(n,), in_specs=...]
where the time goes in v7:
time: 279 us; the launch traced here: 274 us
  Pallas kernels  273 us (98%)
    pallas_call x1, Pallas kernels, backward(): pl.pallas_call(functools.partial(back_kernel, n_dp), grid=(n,), in_specs=...  146 us
    pallas_call x1, Pallas kernels, front(): pl.pallas_call(front_kernel, grid=(groups,), in_specs=[pl.BlockSpec(memor...  69 us
    pallas_call x1, Pallas kernels, mlp(): pl.pallas_call(mlp_kernel, in_specs=[hbm] * 3 + [vmem] + [hbm] * 3, out_s...  47.9 us
    pallas_call x1, Pallas kernels, cast(): pl.pallas_call(cast_kernel, grid=(steps,), in_specs=[whole(small.shape)]...  10.3 us

profile of v7, /device:TPU:0, one launch (start us, length us, event | category | flops | bytes accessed | tf_op | source)
XLA Modules:
  0.0 274.3 jit_solution(18334010623673358866)
XLA Ops:
  0.6 69.0 %shard_map.203 = (f32[8,1024]{1,0:T(8,128)}, bf16[16,1024]{1,0:T(8,128)(2,1)}, f32[2048,896]{1,0:T(8,128)}, f32[2048,256]{1,0:T(8,128)}, bf16[16,256,128]{2,1,0:...) custom-call(s32[1,2]{1,0:T(1,128)} %flags.3, ...), custom_call_target="tpu_custom_call" | custom-call | tf_op jit(solution)/shard_map/pallas_call | solution.py:460
  69.7 47.9 %shard_map.204 = (f32[512,1024]{1,0:T(8,128)}, bf16[512,1024]{1,0:T(8,128)(2,1)}, f32[8,1024]{1,0:T(8,128)}, bf16[1408,1024]{1,0:T(8,128)(2,1)}, bf16[704,1024]{...) custom-call(bf16[512,1024]{1,0:T(8,128)(2,1)} %get-tuple-element.60., ...), custom_call_target="tpu_custom_call" | custom-call | tf_op jit(solution)/shard_map/pallas_call | solution.py:661
  117.6 146.1 %shard_map.205 = (f32[512,1024]{1,0:T(8,128)}, f32[8,1024]{1,0:T(8,128)}, bf16[512,1024]{1,0:T(8,128)(2,1)}, bf16[1408,1024]{1,0:T(8,128)(2,1)}, bf16[704,1024]{...) custom-call(s32[1,2]{1,0:T(1,128)} %flags.3, ...), custom_call_target="tpu_custom_call" | custom-call | tf_op jit(solution)/shard_map/pallas_call | solution.py:1113
  263.7 10.3 %shard_map.206 = (f32[1024]{0:T(1024)}, f32[1024]{0:T(1024)}, f32[128]{0:T(128)}, f32[3,4,256]{2,1,0:T(4,128)}, f32[2,1024]{1,0:T(2,128)}, /*index=5*/f32[1408,1...) custom-call(f32[8,1024]{1,0:T(8,128)} %get-tuple-element.73.small, ...), custom_call_target="tpu_custom_call" | custom-call | tf_op jit(solution)/shard_map/pallas_call | solution.py:1163

commit v8 on v7

--- a/solution.py
+++ b/solution.py
@@ -1153,11 +1153,15 @@
 
 
 def cast(small, gu, down, cat, outw, dx, out):
-    steps = 4
+    steps = 8
     model = small.shape[1]
     arrays = (gu, down, cat, outw, dx, out)
     kinds = [f32] * 5 + [out.dtype]
-    spec = lambda x: pl.BlockSpec((x.shape[0] // steps, x.shape[1]), lambda g: (g, 0))
+    def spec(x):
+        if x is down:
+            return pl.BlockSpec((x.shape[0], x.shape[1] // steps), lambda g: (0, g))
+        return pl.BlockSpec((x.shape[0] // steps, x.shape[1]), lambda g: (g, 0))
+
     shapes = [(model,), (model,), (HEAD,), (3, 4, cat.shape[1]), (2, model)]
     whole = lambda s: pl.BlockSpec(s, lambda g: (0,) * len(s))
     return pl.pallas_call(

time: 279 us -> 279 us (level)
  no operation moved by 1% of the time
where the time goes in v8:
time: 279 us; the launch traced here: 275 us
  Pallas kernels  274 us (98%)
    pallas_call x1, Pallas kernels, backward(): pl.pallas_call(functools.partial(back_kernel, n_dp), grid=(n,), in_specs=...  146 us
    pallas_call x1, Pallas kernels, front(): pl.pallas_call(front_kernel, grid=(groups,), in_specs=[pl.BlockSpec(memor...  69 us
    pallas_call x1, Pallas kernels, mlp(): pl.pallas_call(mlp_kernel, in_specs=[hbm] * 3 + [vmem] + [hbm] * 3, out_s...  47.9 us
    pallas_call x1, Pallas kernels, cast(): pl.pallas_call(cast_kernel, grid=(steps,), in_specs=[whole(small.shape)]...  10.8 us

profile of v8, /device:TPU:0, one launch (start us, length us, event | category | flops | bytes accessed | tf_op | source)
XLA Modules:
  0.0 274.7 jit_solution(11229377122921475149)
XLA Ops:
  0.6 69.0 %shard_map.203 = (f32[8,1024]{1,0:T(8,128)}, bf16[16,1024]{1,0:T(8,128)(2,1)}, f32[2048,896]{1,0:T(8,128)}, f32[2048,256]{1,0:T(8,128)}, bf16[16,256,128]{2,1,0:...) custom-call(s32[1,2]{1,0:T(1,128)} %flags.3, ...), custom_call_target="tpu_custom_call" | custom-call | tf_op jit(solution)/shard_map/pallas_call | solution.py:460
  69.7 47.9 %shard_map.204 = (f32[512,1024]{1,0:T(8,128)}, bf16[512,1024]{1,0:T(8,128)(2,1)}, f32[8,1024]{1,0:T(8,128)}, bf16[1408,1024]{1,0:T(8,128)(2,1)}, bf16[704,1024]{...) custom-call(bf16[512,1024]{1,0:T(8,128)(2,1)} %get-tuple-element.60., ...), custom_call_target="tpu_custom_call" | custom-call | tf_op jit(solution)/shard_map/pallas_call | solution.py:661
  117.6 146.1 %shard_map.205 = (f32[512,1024]{1,0:T(8,128)}, f32[8,1024]{1,0:T(8,128)}, bf16[512,1024]{1,0:T(8,128)(2,1)}, bf16[1408,1024]{1,0:T(8,128)(2,1)}, bf16[704,1024]{...) custom-call(s32[1,2]{1,0:T(1,128)} %flags.3, ...), custom_call_target="tpu_custom_call" | custom-call | tf_op jit(solution)/shard_map/pallas_call | solution.py:1113
  263.7 10.8 %shard_map.206 = (f32[1024]{0:T(1024)}, f32[1024]{0:T(1024)}, f32[128]{0:T(128)}, f32[3,4,256]{2,1,0:T(4,128)}, f32[2,1024]{1,0:T(2,128)}, /*index=5*/f32[1408,1...) custom-call(f32[8,1024]{1,0:T(8,128)} %get-tuple-element.73.small, ...), custom_call_target="tpu_custom_call" | custom-call | tf_op jit(solution)/shard_map/pallas_call | solution.py:1167
